TPU v7x, 32 devices: a whole 2x2x4 slice. The times are simulated.
32 devices in a mesh: seq: 16 (over z, y, x), head: 2 (over core).
Axes of the slice: x: 2, y: 2, z: 4, core: 2. Of those that a mesh axis runs over, the one named last changes fastest.
Arguments:
- hidden: float32 [2, 4096, 768], P(None, 'seq'), may hold values from -6 to 6
- lengths: int32 [2, 8], replicated, may hold values from 1 to 3967, as said below
- prenorm: float32 [768], replicated, may hold values from 0.5 to 1.5
- gating: float32 [768, 1536], P(None, 'head'), may hold values from -0.21875 to 0.21875
- values: float32 [768, 1536], P(None, 'head'), may hold values from -0.21875 to 0.21875
- states: float32 [768, 4, 64], replicated, may hold values from -0.21875 to 0.21875
- stepper: float32 [768, 2, 24], P(None, None, 'head'), may hold values from -0.21875 to 0.21875
- offsets: float32 [2, 24], P(None, 'head'), may hold values from -2 to 1
- decays: float32 [2, 24], P(None, 'head'), may hold values from -9 to 0
- filters: float32 [7, 1536], P(None, 'head'), may hold values from -2 to 2
- shifts: float32 [1536], P('head'), may hold values from -0.5 to 0.5
- kernels: float32 [7, 4, 64], replicated, may hold values from -2 to 2
- biases: float32 [4, 64], replicated, may hold values from -0.5 to 0.5
- direct: float32 [24], P('head'), may hold values from 0.5 to 1.5
- postnorm: float32 [1536], P('head'), may hold values from 0.5 to 1.5
- output: float32 [1536, 768], P('head'), may hold values from -0.15625 to 0.15625
- cotangent: float32 [2, 4096, 768], P(None, 'seq'), may hold values from -6 to 6
Outputs:
- result: float32 [2, 4096, 768], P(None, 'seq')
- grad_hidden: float32 [2, 4096, 768], P(None, 'seq')
- grad_prenorm: float32 [768], replicated
- grad_gating: float32 [768, 1536], P(None, 'head')
- grad_values: float32 [768, 1536], P(None, 'head')
- grad_states: float32 [768, 4, 64], replicated
- grad_stepper: float32 [768, 2, 24], P(None, None, 'head')
- grad_offsets: float32 [2, 24], P(None, 'head')
- grad_decays: float32 [2, 24], P(None, 'head')
- grad_filters: float32 [7, 1536], P(None, 'head')
- grad_shifts: float32 [1536], P('head')
- grad_kernels: float32 [7, 4, 64], replicated
- grad_biases: float32 [4, 64], replicated
- grad_direct: float32 [24], P('head')
- grad_postnorm: float32 [1536], P('head')
- grad_output: float32 [1536, 768], P('head')
Inputs may be any that keep to these rules, and one draw needn't show every extreme that they name: In each micro-batch the 8 lengths sum to 4096; exactly one of them, at a place drawn from the seed, is 3967; the others are at most 36 and sum to 129.
All inputs are finite; a program needn't handle non-finite values.
Results may differ from a plain program's by a relative error of at most 0.0003.
Values sent between devices are 32-bit elements; how exact they have to be, the bound alone decides.
No kernel may reach another device: no remote copies, remote signals or barrier semaphores. Data moves between devices by JAX's collectives and lax.ppermute only.
A program may use at most 640 MiB of HBM per device.

v0:
```python
from functools import partial

import jax
import jax.numpy as jnp
from jax import lax
from jax.experimental import pallas as pl
from jax.experimental.pallas import tpu as pltpu
from jax.sharding import PartitionSpec as P

EPSILON = 1e-05
HIGH = lax.Precision.HIGH
F32 = jnp.float32
BF16 = jnp.bfloat16
LANES = 128
WIDE = 256
CHUNK = 128
EDGE = 8
PARAMS = pltpu.CompilerParams(vmem_limit_bytes=56 * 1024 * 1024)


def dot(left, right, over_left=1, over_right=0, precision=HIGH):
    return lax.dot_general(
        left,
        right,
        (((over_left,), (over_right,)), ((), ())),
        precision=precision,
        preferred_element_type=F32,
    )


def split(x):
    top = x.astype(BF16)
    return top, (x - top.astype(F32)).astype(BF16)


def dot_bf16(left, right, over_left=1, over_right=0):
    return lax.dot_general(
        left,
        right,
        (((over_left,), (over_right,)), ((), ())),
        preferred_element_type=F32,
    )


def spread(first, head_size, both):
    rows = lax.broadcasted_iota(jnp.int32, (2 * both, WIDE), 0)
    columns = lax.broadcasted_iota(jnp.int32, (2 * both, WIDE), 1)
    return (lax.rem(rows, both) == first + columns // head_size).astype(BF16)


def gather_heads(first, head_size, both, parts=2):
    rows = lax.broadcasted_iota(jnp.int32, (parts * WIDE, both), 0)
    columns = lax.broadcasted_iota(jnp.int32, (parts * WIDE, both), 1)
    return (columns == first + lax.rem(rows, WIDE) // head_size).astype(BF16)


def split3(x):
    top = x.astype(BF16)
    rest = x - top.astype(F32)
    middle = rest.astype(BF16)
    return top, middle, (rest - middle.astype(F32)).astype(BF16)


def halves(x):
    return jnp.concatenate(split(x), axis=1)


def triangle(size, keep):
    rows = lax.broadcasted_iota(jnp.int32, (size, size), 0)
    columns = lax.broadcasted_iota(jnp.int32, (size, size), 1)
    return keep(rows, columns)


def exact_sum(zero_one, x):
    a, b, c = split3(x)
    return dot_bf16(zero_one, a) + dot_bf16(zero_one, b) + dot_bf16(zero_one, c)


def flip(x):
    size = x.shape[1]
    one = triangle(size, lambda r, c: r == c).astype(BF16)
    a, b, c = split3(x)
    return dot_bf16(one, a, 1, 1) + dot_bf16(one, b, 1, 1) + dot_bf16(one, c, 1, 1)


def sigmoid(x):
    return 1.0 / (1.0 + jnp.exp(-x))


def softplus(x):
    return jnp.maximum(x, 0.0) + jnp.log1p(jnp.exp(-jnp.abs(x)))


def bounds_of(lengths, i):
    ends = []
    total = jnp.int32(0)
    for k in range(lengths.shape[1]):
        total = total + lengths[i, k]
        ends.append(total)
    return ends


def document(places, ends):
    found = sum(jnp.where(places >= end, 1, 0) for end in ends)
    return jnp.where(places < 0, -1, jnp.where(places >= ends[-1], -2, found))


def same_document(first, ends, length):
    rows = document(first + lax.broadcasted_iota(jnp.int32, (length, LANES), 0), ends)
    columns = document(first + lax.broadcasted_iota(jnp.int32, (1, length), 1), ends)
    return jnp.concatenate([rows] * (length // LANES), axis=1) == columns


def fill_masks(masks, documents, first, ends, start, rows, reach_cells):
    total = documents.shape[0]
    documents[...] = document(
        first - 2 * EDGE + lax.broadcasted_iota(jnp.int32, (total, LANES), 0), ends
    )
    center = documents[EDGE + start : EDGE + start + rows]
    for o in range(2 * reach_cells + 1):
        at = EDGE + start + o - reach_cells
        masks[o] = (documents[at : at + rows] == center).astype(F32)


def left3(x):
    top = x.astype(BF16).astype(F32)
    return jnp.concatenate([top, top, x - top], axis=1).astype(BF16)


def right3(x):
    top, low = split(x)
    return jnp.concatenate([top, low, top], axis=0)


def stacked(x):
    return jnp.concatenate(split(x), axis=0)


def front_kernel(
    dims,
    place,
    lengths,
    before,
    hidden,
    after,
    prenorm,
    values,
    states,
    stepper,
    filters,
    kernels,
    shifts,
    biases,
    offsets,
    decays,
    normed,
    mixed,
    conv,
    act,
    maps_t,
    z_out,
    run,
    late,
    run_rows,
    late_rows,
    reach,
    tail,
    keep,
    taps,
    pay,
    documents,
    masks,
):
    length, inner, heads, state, reach_cells, rows = dims
    head_size = inner // heads
    both = 2 * heads
    maps_width = 4 * state
    width = inner + maps_width
    offsets_count = 2 * reach_cells + 1
    i = pl.program_id(0)
    ends = bounds_of(lengths, i)
    first = place[0] * length
    fill_masks(masks, documents, first, ends, EDGE, length, reach_cells)

    gain = prenorm[...]

    def norm(x):
        mean = jnp.sum(x * x, axis=1, keepdims=True) / x.shape[1]
        return x * lax.rsqrt(mean + EPSILON) * gain

    normed[0, :EDGE] = norm(before[0])
    for r in range(0, length, 64):
        normed[0, EDGE + r : EDGE + r + 64] = norm(hidden[0, r : r + 64])
    normed[0, EDGE + length :] = norm(after[0])

    whole = normed[0]
    for t in range(inner // WIDE):
        at = slice(t * WIDE, (t + 1) * WIDE)
        mixed[0, :, at] = dot(whole, values[:, at])
    mixed[0, :, inner:] = dot(whole, states[...])
    raw = dot(normed[0, EDGE : EDGE + length], stepper[...])

    taps[:offsets_count, :inner] = filters[...]
    taps[offsets_count:, :inner] = shifts[...]
    for k in range(4):
        at = slice(inner + k * state, inner + (k + 1) * state)
        taps[:offsets_count, at] = kernels[:, k, :]
        taps[offsets_count:, at] = biases[k : k + 1, :]

    for t in range(width // WIDE):
        at = slice(t * WIDE, (t + 1) * WIDE)
        for r in range(0, length, CHUNK):
            total = jnp.broadcast_to(taps[offsets_count:, at], (CHUNK, WIDE))
            for o in range(offsets_count):
                begin = EDGE - reach_cells + o + r
                mask = masks[o, r : r + CHUNK]
                total = total + (mixed[0, begin : begin + CHUNK, at] * taps[o : o + 1, at]) * (
                    jnp.concatenate([mask] * (WIDE // LANES), axis=1)
                )
            conv[0, r : r + CHUNK, at] = total
            act[0, r : r + CHUNK, at] = total * sigmoid(total)
    flipped = jnp.transpose(act[0, :, inner:])
    maps_t[0] = flipped

    ahead = lax.broadcasted_iota(jnp.int32, (length, both), 1) < heads
    ahead_row = ahead[:1]
    z = raw + jnp.concatenate([offsets[0:1, :], offsets[1:2, :]], axis=1)
    rates = jnp.exp(jnp.concatenate([decays[0:1, :], decays[1:2, :]], axis=1))
    step = softplus(z)
    decay = -step * rates
    lower = triangle(length, lambda r, c: r >= c).astype(BF16)
    upper = triangle(length, lambda r, c: r <= c).astype(BF16)
    running = jnp.where(ahead, exact_sum(lower, decay), exact_sum(upper, decay))
    edge = jnp.where(ahead_row, running[length - 1 :], running[:1])
    here = document(first + lax.broadcasted_iota(jnp.int32, (length, both), 0), ends)
    seg_before = document(first - 1, ends)
    seg_after = document(first + length, ends)
    seg_first = document(first, ends)
    seg_last = document(first + length - 1, ends)
    enter = (here == jnp.where(ahead, seg_before, seg_after)).astype(F32)
    leave = (here == jnp.where(ahead, seg_last, seg_first)).astype(F32)
    keep_mask = jnp.where(
        ahead_row,
        jnp.where(seg_last == seg_before, 1.0, 0.0),
        jnp.where(seg_first == seg_after, 1.0, 0.0),
    )
    reach_now = enter * jnp.exp(running)
    tail_now = leave * jnp.exp(edge - running) * step
    keep_now = keep_mask * jnp.exp(edge)
    late_now = running - jnp.log(jnp.maximum(step, 1e-37))
    z_out[0] = z
    run[0] = running
    late[0] = late_now
    reach[0] = reach_now
    tail[0] = tail_now
    run_rows[0] = flip(running)
    late_rows[0] = flip(late_now)
    keep[0] = keep_now

    tail_halves = halves(tail_now)
    keep_halves = halves(jnp.broadcast_to(keep_now, (EDGE, both)))
    pieces = state // rows
    per_tile = WIDE // head_size
    for d in range(2):
        maps_now = stacked(flipped[2 * d * state : (2 * d + 1) * state])
        keeps = []
        for t in range(inner // WIDE):
            grow = spread(d * heads + t * per_tile, head_size, both)
            weighted = act[0, :, t * WIDE : (t + 1) * WIDE] * dot_bf16(tail_halves, grow)
            put_states(pay, d, t, product_of_stack(maps_now, weighted, state), pieces, rows)
            keep_wide = dot_bf16(keep_halves, grow)[:1]
            keeps += [keep_wide[:, k * LANES : (k + 1) * LANES] for k in range(WIDE // LANES)]
        tiles = inner // LANES
        keeps.append(jnp.zeros((EDGE - tiles, LANES), F32))
        keep_block = jnp.concatenate(keeps, axis=0)
        for j in range(pieces):
            pay[d * pieces + j, tiles * rows :, :] = keep_block


def product_of_stack(stack, x, size):
    top, low = split(x)
    twice = dot_bf16(stack, top)
    return twice[:size] + twice[size:] + dot_bf16(stack[:size], low)


def put_states(pay, d, t, own, pieces, rows):
    for k in range(WIDE // LANES):
        at = (t * (WIDE // LANES) + k) * rows
        for j in range(pieces):
            pay[d * pieces + j, at : at + rows, :] = own[
                j * rows : (j + 1) * rows, k * LANES : (k + 1) * LANES
            ]


def prefix_kernel(tiles, rows, flipped, terms, keeps, into):
    peers = terms.shape[0]
    back = flipped[0] != 0

    def turn(i, carry):
        at = jnp.where(back, peers - 1 - i, i)
        factor = keeps[at, tiles * rows :, :]
        new = []
        for t in range(tiles):
            into[at, t * rows : (t + 1) * rows, :] = carry[t]
            new.append(
                carry[t] * factor[t : t + 1] + terms[at, t * rows : (t + 1) * rows, :]
            )
        return tuple(new)

    lax.fori_loop(0, peers, turn, tuple(jnp.zeros((rows, LANES), F32) for _ in range(tiles)))


def scores_of(act, ends, first, inner, state, length):
    def part(k):
        return act[0, :, inner + k * state : inner + (k + 1) * state]

    same = same_document(first, ends, length)
    below = triangle(length, lambda r, c: r > c)
    above = triangle(length, lambda r, c: r < c)
    return part, same, below, above


def inside_kernel(dims, place, lengths, act, run, late_rows, inside):
    length, inner, heads, state, _, _ = dims
    head_size = inner // heads
    per_tile = LANES // head_size
    ends = bounds_of(lengths, pl.program_id(0))
    part, same, below, above = scores_of(act, ends, place[0] * length, inner, state, length)
    scores = jnp.where(below & same, dot(part(1), part(0), 1, 1), 0.0) + jnp.where(
        above & same, dot(part(3), part(2), 1, 1), 0.0
    )
    run_at = run[0]
    lane = lax.broadcasted_iota(jnp.int32, (length, LANES), 1) // head_size
    for t in range(inner // LANES):
        top, low = split(act[0, :, t * LANES : (t + 1) * LANES])
        pair = jnp.concatenate([top, low], axis=1)
        total = jnp.zeros((length, LANES), F32)
        for k in range(per_tile):
            h = t * per_tile + k
            weights = jnp.exp(
                jnp.where(
                    below,
                    run_at[:, h : h + 1] - late_rows[0, h : h + 1, :],
                    run_at[:, heads + h : heads + h + 1]
                    - late_rows[0, heads + h : heads + h + 1, :],
                )
            )
            m_top, m_low = split(scores * weights)
            wide = dot_bf16(m_top, pair)
            now = wide[:, :LANES] + wide[:, LANES:] + dot_bf16(m_low, top)
            total = jnp.where(lane == k, now, total)
        inside[0, :, t * LANES : (t + 1) * LANES] = total


def unpack(pay, into, tiles, rows, state):
    pieces = state // rows
    for d in range(2):
        for j in range(pieces):
            for t in range(tiles):
                into[d, j * rows : (j + 1) * rows, t * LANES : (t + 1) * LANES] = pay[
                    d * pieces + j, t * rows : (t + 1) * rows, :
                ]


def join_kernel(
    dims, inside, pay, act, reach, gate, back, direct, postnorm, mixed_y, sums, states
):
    length, inner, heads, state, _, rows = dims
    head_size = inner // heads
    both = 2 * heads
    per_tile = WIDE // head_size
    unpack(pay, states.at[0], inner // LANES, rows, state)
    reach_halves = halves(reach[0])
    readers = [left3(act[0, :, inner + k * state : inner + (k + 1) * state]) for k in (1, 3)]
    squares = jnp.zeros((length, WIDE), F32)
    crossed = jnp.zeros((length, WIDE), F32)
    for t in range(inner // WIDE):
        at = slice(t * WIDE, (t + 1) * WIDE)
        total = inside[0, :, at] + direct[:, at] * act[0, :, at]
        for d in range(2):
            grow = spread(d * heads + t * per_tile, head_size, both)
            total = total + dot_bf16(readers[d], right3(states[0, d, :, at])) * dot_bf16(
                reach_halves, grow
            )
        mixed_y[0, :, at] = total
        gate_now = gate[0, EDGE : EDGE + length, at]
        gated = total * (gate_now * sigmoid(gate_now))
        squares = squares + gated * gated
        crossed = crossed + gated * postnorm[:, at] * back[0, :, at]
    lane = lax.broadcasted_iota(jnp.int32, (length, LANES), 1)
    sums[0] = jnp.where(
        lane == 0,
        jnp.sum(squares, axis=1, keepdims=True),
        jnp.sum(crossed, axis=1, keepdims=True),
    )


def norm_of(sums, peer_sums, inner_all, length):
    both_sums = sums[0] + peer_sums[0]
    q = lax.rsqrt(both_sums[:, 0:1] / inner_all + EPSILON)
    pull = both_sums[:, 1:2] * (q * q * q) / inner_all
    return (
        jnp.broadcast_to(q, (length, LANES)),
        jnp.broadcast_to(pull, (length, LANES)),
    )


def turn_kernel(
    dims,
    inner_all,
    sums,
    peer_sums,
    mixed_y,
    gate,
    back,
    maps_t,
    reach,
    postnorm,
    grad_y,
    normal,
    pay,
):
    length, inner, heads, state, _, rows = dims
    head_size = inner // heads
    both = 2 * heads
    per_tile = WIDE // head_size
    pieces = state // rows
    q, pull = norm_of(sums, peer_sums, inner_all, length)
    reach_halves = halves(reach[0])
    readers = [stacked(maps_t[0, k * state : (k + 1) * state]) for k in (1, 3)]
    for t in range(inner // WIDE):
        upstreams = []
        for k in range(WIDE // LANES):
            at = slice(t * WIDE + k * LANES, t * WIDE + (k + 1) * LANES)
            gate_now = gate[0, EDGE : EDGE + length, at]
            opened = gate_now * sigmoid(gate_now)
            gated = mixed_y[0, :, at] * opened
            post = postnorm[:, at]
            upstream = (q * back[0, :, at] * post - pull * gated) * opened
            grad_y[0, :, at] = upstream
            normal[0, :, at] = gated * post * q
            upstreams.append(upstream)
        upstream = jnp.concatenate(upstreams, axis=1)
        for d in range(2):
            grow = spread(d * heads + t * per_tile, head_size, both)
            seed = product_of_stack(readers[d], upstream * dot_bf16(reach_halves, grow), state)
            put_states(pay, d, t, seed, pieces, rows)


def side_kernel(
    dims,
    inner_all,
    sums,
    peer_sums,
    mixed_y,
    gate,
    back,
    act,
    grad_y,
    postnorm,
    grad_gate,
    smalls,
):
    length, inner, heads, _, _, _ = dims
    q, pull = norm_of(sums, peer_sums, inner_all, length)
    grad_gate[0, :EDGE] = jnp.zeros((EDGE, inner), F32)
    grad_gate[0, EDGE + length :] = jnp.zeros((EDGE, inner), F32)
    smalls[0] = jnp.zeros((EDGE, inner), F32)
    for t in range(inner // LANES):
        at = slice(t * LANES, (t + 1) * LANES)
        y = mixed_y[0, :, at]
        gate_now = gate[0, EDGE : EDGE + length, at]
        chance = sigmoid(gate_now)
        gated = y * (gate_now * chance)
        scaled = q * back[0, :, at]
        grad_gated = scaled * postnorm[:, at] - pull * gated
        grad_gate[0, EDGE : EDGE + length, at] = (
            grad_gated * y * (chance * (1.0 + gate_now * (1.0 - chance)))
        )
        smalls[0, 0:1, at] = jnp.sum(scaled * gated, axis=0, keepdims=True)
        smalls[0, 1:2, at] = jnp.sum(grad_y[0, :, at] * act[0, :, at], axis=0, keepdims=True)


def inside_back_kernel(
    dims,
    place,
    lengths,
    act,
    grad_y,
    late,
    run_rows,
    reach,
    states,
    direct,
    grad_signal,
    grad_maps,
    own,
    column_sums,
    read_parts,
):
    length, inner, heads, state, _, _ = dims
    head_size = inner // heads
    per_tile = LANES // head_size
    both = 2 * heads
    ends = bounds_of(lengths, pl.program_id(0))
    part, same, below, above = scores_of(act, ends, place[0] * length, inner, state, length)
    scores = jnp.where(above & same, dot(part(0), part(1), 1, 1), 0.0) + jnp.where(
        below & same, dot(part(2), part(3), 1, 1), 0.0
    )
    late_at = late[0]
    lane = lax.broadcasted_iota(jnp.int32, (length, LANES), 1)
    write_sums = jnp.zeros((length, LANES), F32)
    grad_scores = jnp.zeros((length, length), F32)
    zero = jnp.zeros((length, LANES), BF16)
    for t in range(inner // LANES):
        at = slice(t * LANES, (t + 1) * LANES)
        s_top, s_low = split(act[0, :, at])
        g_top, g_low = split(grad_y[0, :, at])
        pair = jnp.concatenate([g_top, g_low], axis=1)
        two = jnp.concatenate([g_top, g_top], axis=1)
        total = jnp.zeros((length, LANES), F32)
        for k in range(per_tile):
            h = t * per_tile + k
            weights = jnp.exp(
                jnp.where(
                    above,
                    run_rows[0, h : h + 1, :] - late_at[:, h : h + 1],
                    run_rows[0, heads + h : heads + h + 1, :]
                    - late_at[:, heads + h : heads + h + 1],
                )
            )
            mine = lane // head_size == k
            i_top = jnp.where(mine, s_top, zero)
            i_low = jnp.where(mine, s_low, zero)
            overlap = dot_bf16(jnp.concatenate([i_top, i_low], axis=1), two, 1, 1) + dot_bf16(
                i_top, g_low, 1, 1
            )
            product = weights * overlap
            grad_scores = grad_scores + product
            whole = product * scores
            ahead = jnp.where(above, whole, 0.0)
            ahead_writes = jnp.sum(ahead, axis=1, keepdims=True)
            all_writes = jnp.sum(whole, axis=1, keepdims=True)
            write_sums = jnp.where(lane == h, ahead_writes, write_sums)
            write_sums = jnp.where(lane == heads + h, all_writes - ahead_writes, write_sums)
            ahead_reads = jnp.sum(ahead, axis=0, keepdims=True)
            read_parts[h : h + 1, :] = ahead_reads
            read_parts[heads + h : heads + h + 1, :] = (
                jnp.sum(whole, axis=0, keepdims=True) - ahead_reads
            )
            m_top, m_low = split(scores * weights)
            wide = dot_bf16(m_top, pair)
            now = wide[:, :LANES] + wide[:, LANES:] + dot_bf16(m_low, g_top)
            total = jnp.where(mine, now, total)
        grad_signal[0, :, at] = total + direct[:, at] * grad_y[0, :, at]

    writes = write_sums[:, :both]
    column_sums[0] = writes
    total_own = flip_back(read_parts[...]) - writes
    reach_halves = halves(reach[0])
    per_wide = WIDE // head_size
    for d in range(2):
        side = (above, below)[d]
        grads = jnp.where(side & same, grad_scores, 0.0)
        reader = part(2 * d + 1)
        reader3 = left3(reader)
        grad_reader = dot(grads, part(2 * d), 0, 0)
        for t in range(inner // WIDE):
            at = slice(t * WIDE, (t + 1) * WIDE)
            first = d * heads + t * per_wide
            before = states[0, d, :, at]
            reached = grad_y[0, :, at] * dot_bf16(
                reach_halves, spread(first, head_size, both)
            )
            seen = dot_bf16(reader3, right3(before))
            total_own = total_own + dot_bf16(
                halves(reached * seen), gather_heads(first, head_size, both)
            )
            grad_reader = grad_reader + product_with(reached, stacked(before), state)
        grad_maps[0, :, 2 * d * state : (2 * d + 1) * state] = dot(grads, reader)
        grad_maps[0, :, (2 * d + 1) * state : (2 * d + 2) * state] = grad_reader
    own[0] = total_own


def product_with(x, stack, size):
    top, low = split(x)
    twice = dot_bf16(top, stack, 1, 1)
    return twice[:, :size] + twice[:, size:] + dot_bf16(low, stack[:size], 1, 1)


def flip_back(x):
    size = x.shape[0]
    one = triangle(size, lambda r, c: r == c).astype(BF16)
    a, b, c = split3(x)
    return dot_bf16(a, one, 0, 0) + dot_bf16(b, one, 0, 0) + dot_bf16(c, one, 0, 0)


def fold_rows(x):
    total = x[:EDGE]
    for r in range(EDGE, x.shape[0], EDGE):
        total = total + x[r : r + EDGE]
    return total


def end_kernel(
    dims,
    place,
    lengths,
    pay,
    act,
    z_in,
    tail,
    conv,
    states,
    keep,
    grad_inside,
    grad_maps,
    own,
    column_sums,
    mixed,
    taps,
    decays,
    grad_values,
    grad_states,
    grad_raw,
    smalls,
    later,
    grad_act,
    documents,
    masks,
):
    length, inner, heads, state, reach_cells, rows = dims
    head_size = inner // heads
    both = 2 * heads
    per_tile = WIDE // head_size
    width = inner + 4 * state
    offsets_count = 2 * reach_cells + 1
    long = length + 2 * EDGE
    first_row = EDGE - reach_cells
    unpack(pay, later, inner // LANES, rows, state)
    ends = bounds_of(lengths, pl.program_id(0))
    fill_masks(masks, documents, place[0] * length, ends, EDGE, length, reach_cells)

    tail_halves = halves(tail[0])
    leave = jnp.zeros((length, both), F32)
    through = jnp.zeros((1, both), F32)
    for d in range(2):
        writer3 = left3(act[0, :, inner + 2 * d * state : inner + (2 * d + 1) * state])
        grad_writer = grad_maps[0, :, 2 * d * state : (2 * d + 1) * state]
        for t in range(inner // WIDE):
            at = slice(t * WIDE, (t + 1) * WIDE)
            first = d * heads + t * per_tile
            fold = gather_heads(first, head_size, both)
            after = later[d, :, at]
            tails = dot_bf16(tail_halves, spread(first, head_size, both))
            weighted = act[0, :, at] * tails
            pulled = dot_bf16(writer3, right3(after))
            base = grad_inside[0, :, at] if d == 0 else grad_act[:, at]
            grad_act[:, at] = base + tails * pulled
            leave = leave + dot_bf16(halves(weighted * pulled), fold)
            grad_writer = grad_writer + product_with(weighted, stacked(after), state)
            crossed = jnp.sum(states[0, d, :, at] * after, axis=0, keepdims=True)
            through = (
                through + dot_bf16(halves(jnp.broadcast_to(crossed, (EDGE, WIDE))), fold)[:1]
            )
        at = inner + 2 * d * state
        grad_act[:, at : at + state] = grad_writer
        grad_act[:, at + state : at + 2 * state] = grad_maps[
            0, :, (2 * d + 1) * state : (2 * d + 2) * state
        ]

    grad_values[0] = jnp.zeros((long, inner), F32)
    grad_states[0] = jnp.zeros((long, width - inner), F32)
    def column(t, _, into, shift):
        at = pl.ds(pl.multiple_of(t * WIDE, WIDE), WIDE)
        put = pl.ds(pl.multiple_of((t - shift) * WIDE, WIDE), WIDE)
        bias_sum = jnp.zeros((EDGE, WIDE), F32)
        tap_sums = [jnp.zeros((EDGE, WIDE), F32) for _ in range(offsets_count)]
        for r in range(0, length, CHUNK):
            value = conv[0, r : r + CHUNK, at]
            chance = sigmoid(value)
            grad = grad_act[r : r + CHUNK, at] * (chance * (1.0 + value * (1.0 - chance)))
            bias_sum = bias_sum + fold_rows(grad)
            for o in range(offsets_count):
                begin = first_row + o + r
                mask = masks[o, r : r + CHUNK]
                now = grad * jnp.concatenate([mask] * (WIDE // LANES), axis=1)
                into[0, begin : begin + CHUNK, put] += now * taps[o : o + 1, at]
                tap_sums[o] = tap_sums[o] + fold_rows(now * mixed[0, begin : begin + CHUNK, at])
        smalls[0, offsets_count : offsets_count + 1, at] = jnp.sum(bias_sum, axis=0, keepdims=True)
        for o in range(offsets_count):
            smalls[0, o : o + 1, at] = jnp.sum(tap_sums[o], axis=0, keepdims=True)
        return 0

    split_at = inner // WIDE
    lax.fori_loop(0, split_at, partial(column, into=grad_values, shift=0), 0)
    lax.fori_loop(
        split_at, width // WIDE, partial(column, into=grad_states, shift=split_at), 0
    )

    ahead = lax.broadcasted_iota(jnp.int32, (length, both), 1) < heads
    from_here = triangle(length, lambda r, c: c >= r).astype(BF16)
    to_here = triangle(length, lambda r, c: c <= r).astype(BF16)
    before_here = triangle(length, lambda r, c: c < r).astype(BF16)
    after_here = triangle(length, lambda r, c: c > r).astype(BF16)
    entered = own[0]
    grad_decay = (
        jnp.where(
            ahead,
            exact_sum(from_here, entered) + exact_sum(before_here, leave),
            exact_sum(to_here, entered) + exact_sum(after_here, leave),
        )
        + through * keep[0]
    )
    z = z_in[0]
    step = softplus(z)
    chance = sigmoid(z)
    rates = jnp.exp(jnp.concatenate([decays[0:1, :], decays[1:2, :]], axis=1))
    ratio = jnp.where(step > 1e-30, chance / jnp.maximum(step, 1e-30), 1.0)
    grad_z = (leave + column_sums[0]) * ratio - rates * grad_decay * chance
    grad_raw[0, :EDGE] = jnp.zeros((EDGE, both), F32)
    grad_raw[0, EDGE + length :] = jnp.zeros((EDGE, both), F32)
    grad_raw[0, EDGE : EDGE + length] = grad_z
    smalls[0, EDGE:, :] = jnp.zeros((EDGE, width), F32)
    smalls[0, EDGE : EDGE + 1, :both] = jnp.sum(grad_z, axis=0, keepdims=True)
    smalls[0, EDGE + 1 : EDGE + 2, :both] = -rates * jnp.sum(
        step * grad_decay, axis=0, keepdims=True
    )


def pack_kernel(
    dims, rest, own_states, smalls, side_smalls, grad_stepper, grad_prenorm, packed
):
    _, inner, _, state, reach_cells, _ = dims
    both = grad_stepper.shape[0]
    small = smalls[0]
    side = side_smalls[0]
    for i in range(1, smalls.shape[0]):
        small = small + smalls[i]
        side = side + side_smalls[i]
    at = rest.shape[0]
    packed[:at] = rest[...]
    cut = own_states.shape[0]
    packed[at : at + cut] = own_states[...]
    at += cut
    packed[at:] = jnp.zeros((packed.shape[0] - at, inner), F32)
    packed[at : at + both] = grad_stepper[...]
    at += both
    packed[at : at + EDGE] = small[:EDGE, :inner]
    packed[at + EDGE : at + 2 * EDGE, : 4 * state] = small[:EDGE, inner:]
    packed[at + 2 * EDGE : at + 2 * EDGE + 2, :] = side[:2]
    packed[at + 2 * EDGE + 2 : at + 2 * EDGE + 4, :] = small[EDGE : EDGE + 2, :inner]
    packed[at + 2 * EDGE + 4 : at + 2 * EDGE + 5, :] = grad_prenorm[...]


def unpack_kernel(
    dims,
    mine,
    peer,
    filters,
    shifts,
    kernels,
    biases,
    postnorm,
    direct,
    offsets,
    decays,
    prenorm,
):
    _, inner, heads, state, reach_cells, _ = dims
    head_size = inner // heads
    count = 2 * reach_cells + 1
    at = 2 * state + 2 * heads
    filters[...] = mine[at : at + count]
    shifts[...] = mine[at + count]
    at += EDGE
    shared = mine[at : at + EDGE, : 4 * state] + peer[at : at + EDGE, : 4 * state]
    for k in range(4):
        kernels[:, k, :] = shared[:count, k * state : (k + 1) * state]
        biases[k : k + 1, :] = shared[count:, k * state : (k + 1) * state]
    at += EDGE
    postnorm[...] = mine[at]
    fold = jnp.zeros((EDGE, heads), F32)
    for t in range(inner // WIDE):
        row = jnp.broadcast_to(mine[at + 1 : at + 2, t * WIDE : (t + 1) * WIDE], (EDGE, WIDE))
        fold = fold + dot_bf16(
            jnp.concatenate(split3(row), axis=1),
            gather_heads(t * (WIDE // head_size), head_size, heads, 3),
        )
    direct[...] = fold[0]
    for d in range(2):
        offsets[d : d + 1, :] = mine[at + 2 : at + 3, d * heads : (d + 1) * heads]
        decays[d : d + 1, :] = mine[at + 3 : at + 4, d * heads : (d + 1) * heads]
    prenorm[...] = mine[at + 4] + peer[at + 4]


def exchange(x, axis, bit):
    peers = lax.axis_size(axis)
    return lax.ppermute(x, axis, [(i, i ^ (1 << bit)) for i in range(peers)])


def bit_of(place, bit):
    return (place >> bit) & 1


def join_halves(mine, own, other):
    return jnp.where(
        mine == 0, jnp.concatenate([own, other]), jnp.concatenate([other, own])
    )


def tie(*arrays):
    return lax.optimization_barrier(arrays)


class PairTotal:
    def __init__(self, axis):
        self.axis = axis
        self.place = lax.axis_index(axis)
        bits = lax.axis_size(axis).bit_length() - 1
        down = [(0, 1), (1, 0), (2,)] + [(bit,) for bit in range(3, bits)]
        self.steps = [("halve", order) for order in down]
        self.steps += [("join", order) for order in reversed(down)]
        self.at = 0
        self.now = [None, None]
        self.came = [None, None]

    def mine(self, bit):
        return bit_of(self.place, bit)

    def outgoing(self, k=None):
        kind, order = self.steps[self.at]
        which = range(len(order)) if k is None else (k,)
        out = []
        for i in which:
            x, mine = self.now[i], self.mine(order[i])
            if kind == "join":
                out.append(x)
            elif order == (2,):
                out.append(jnp.where(mine == 0, self.now[1], self.now[0]))
            else:
                half = x.shape[0] // 2
                out.append(lax.dynamic_slice_in_dim(x, (1 - mine) * half, half))
        return out

    def go(self, sent, k=None):
        _, order = self.steps[self.at]
        which = range(len(order)) if k is None else (k,)
        for i, x in zip(which, sent):
            self.came[i] = exchange(x, self.axis, order[i])

    def take(self, *others):
        kind, order = self.steps[self.at]
        came = [c for c in self.came[: len(order)]]
        if others:
            came = list(tie(*came, *others)[: len(order)])
        now = []
        for i, bit in enumerate(order):
            x, mine, c = self.now[i], self.mine(bit), came[i]
            if order == (2,):
                if kind == "halve":
                    now = [jnp.where(mine == 0, self.now[0], self.now[1]) + c]
                else:
                    now = [jnp.where(mine == 0, x, c), jnp.where(mine == 0, c, x)]
            elif kind == "halve":
                half = x.shape[0] // 2
                now.append(lax.dynamic_slice_in_dim(x, mine * half, half) + c)
            else:
                now.append(join_halves(mine, x, c))
        self.now = now
        self.at += 1

    def ahead_of(self, array, k=None):
        sent = self.outgoing(k)
        self.go(sent, k)
        return tie(array, *sent)[0]

    @property
    def done(self):
        return self.at == len(self.steps)

    def turn(self, *others):
        if self.done:
            return self.now[0]
        self.take(*others)
        if not self.done:
            sent = self.outgoing()
            self.go(sent)
            return sent[0]
        return self.now[0]


def local(
    hidden,
    lengths,
    prenorm,
    gating,
    values,
    states,
    stepper,
    offsets,
    decays,
    filters,
    shifts,
    kernels,
    biases,
    direct,
    postnorm,
    output,
    cotangent,
):
    micro, length, model = hidden.shape
    inner = gating.shape[1]
    heads = direct.shape[0]
    both = 2 * heads
    head_size = inner // heads
    state = states.shape[2]
    reach_cells = (filters.shape[0] - 1) // 2
    count = 2 * reach_cells + 1
    peers = lax.axis_size("seq")
    place = lax.axis_index("seq")
    head_place = lax.axis_index("head")
    inner_all = inner * lax.axis_size("head")
    rows = micro * 2 * state // peers
    tiles = inner // LANES
    dims = (length, inner, heads, state, reach_cells, rows)
    maps_width = 4 * state
    width = inner + maps_width
    long = length + 2 * EDGE
    half_peers = peers // micro
    where = place.reshape(1).astype(jnp.int32)

    up = [(i, i + 1) for i in range(peers - 1)]
    down = [(i + 1, i) for i in range(peers - 1)]
    swap = [(0, 1), (1, 0)]
    before = lax.ppermute(hidden[:, length - EDGE :], "seq", up)
    after = lax.ppermute(hidden[:, :EDGE], "seq", down)
    states_flat = states.reshape(model, maps_width)
    stepper_flat = stepper.reshape(model, both)
    direct_row = jnp.repeat(direct, head_size)[None]
    post_row = postnorm[None]

    def spec(*block):
        return pl.BlockSpec((1,) + block, lambda i: (i,) + (0,) * len(block))

    def fixed(*block):
        return pl.BlockSpec(block, lambda i: (0,) * len(block))

    def shape(*dims):
        return jax.ShapeDtypeStruct(dims, F32)

    smem = pl.BlockSpec(memory_space=pltpu.SMEM)
    vmem = pl.BlockSpec(memory_space=pltpu.VMEM)
    packed = tiles * rows + EDGE
    pay_spec = pl.BlockSpec((half_peers, packed, LANES), lambda i: (i, 0, 0))
    plain_spec = pl.BlockSpec((half_peers, tiles * rows, LANES), lambda i: (i, 0, 0))
    small = spec(length, both)
    wide = spec(length, inner)
    acts = spec(length, width)
    row = fixed(1, inner)
    flat = spec(both, length)

    (
        normed,
        mixed,
        conv,
        act,
        maps_t,
        z,
        run,
        late,
        run_rows,
        late_rows,
        reach,
        tail,
        keep,
        taps,
        pay,
    ) = pl.pallas_call(
        partial(front_kernel, dims),
        grid=(micro,),
        in_specs=[
            smem,
            smem,
            spec(EDGE, model),
            spec(length, model),
            spec(EDGE, model),
            fixed(1, model),
            fixed(model, inner),
            fixed(model, maps_width),
            fixed(model, both),
            fixed(count, inner),
            fixed(count, 4, state),
            fixed(1, inner),
            fixed(4, state),
            fixed(2, heads),
            fixed(2, heads),
        ],
        out_specs=[
            spec(long, model),
            spec(long, width),
            acts,
            acts,
            spec(maps_width, length),
            small,
            small,
            small,
            flat,
            flat,
            small,
            small,
            spec(1, both),
            fixed(EDGE, width),
            pay_spec,
        ],
        out_shape=[
            shape(micro, long, model),
            shape(micro, long, width),
            shape(micro, length, width),
            shape(micro, length, width),
            shape(micro, maps_width, length),
            shape(micro, length, both),
            shape(micro, length, both),
            shape(micro, length, both),
            shape(micro, both, length),
            shape(micro, both, length),
            shape(micro, length, both),
            shape(micro, length, both),
            shape(micro, 1, both),
            shape(EDGE, width),
            shape(peers, packed, LANES),
        ],
        scratch_shapes=[
            pltpu.VMEM((long + 2 * EDGE, LANES), jnp.int32),
            pltpu.VMEM((count, length, LANES), F32),
        ],
        compiler_params=PARAMS,
        name="front",
    )(
        where,
        lengths,
        before,
        hidden,
        after,
        prenorm[None],
        values,
        states_flat,
        stepper_flat,
        filters,
        kernels,
        shifts[None],
        biases,
        offsets,
        decays,
    )

    direction = lax.rem(place // (peers // (2 * micro)), 2)

    def prefix(terms, keeps, flipped):
        return pl.pallas_call(
            partial(prefix_kernel, tiles, rows),
            grid=(1,),
            in_specs=[smem, fixed(*terms.shape), fixed(*keeps.shape)],
            out_specs=fixed(peers, tiles * rows, LANES),
            out_shape=shape(peers, tiles * rows, LANES),
            compiler_params=PARAMS,
            name="prefix",
        )(flipped.reshape(1).astype(jnp.int32), terms, keeps)

    def swap_all(x):
        return lax.all_to_all(x, "seq", 0, 0, tiled=True)

    terms = swap_all(pay)
    arrived = swap_all(prefix(terms, terms, direction))

    normed_flat = normed.reshape(micro * long, model)
    cotangent_flat = cotangent.reshape(micro * length, model)
    back = dot(cotangent_flat, output, 1, 1).reshape(micro, length, inner)
    inside = pl.pallas_call(
        partial(inside_kernel, dims),
        grid=(micro,),
        in_specs=[smem, smem, acts, small, flat],
        out_specs=wide,
        out_shape=shape(micro, length, inner),
        compiler_params=PARAMS,
        name="inside",
    )(where, lengths, act, run, late_rows)
    gate = dot(normed_flat, gating).reshape(micro, long, inner)

    gates = spec(long, inner)
    sum_spec = spec(length, LANES)
    state_spec = spec(2, state, inner)
    mixed_y, sums, before_states = pl.pallas_call(
        partial(join_kernel, dims),
        grid=(micro,),
        in_specs=[wide, plain_spec, acts, small, gates, wide, row, row],
        out_specs=[wide, sum_spec, state_spec],
        out_shape=[
            shape(micro, length, inner),
            shape(micro, length, LANES),
            shape(micro, 2, state, inner),
        ],
        compiler_params=PARAMS,
        name="join",
    )(inside, arrived, act, reach, gate, back, direct_row, post_row)
    peer_sums = lax.ppermute(sums, "head", swap)

    grad_y, normal, pay_back = pl.pallas_call(
        partial(turn_kernel, dims, inner_all),
        grid=(micro,),
        in_specs=[
            sum_spec,
            sum_spec,
            wide,
            gates,
            wide,
            spec(maps_width, length),
            small,
            row,
        ],
        out_specs=[wide, wide, plain_spec],
        out_shape=[
            shape(micro, length, inner),
            shape(micro, length, inner),
            shape(peers, tiles * rows, LANES),
        ],
        compiler_params=PARAMS,
        name="turn",
    )(sums, peer_sums, mixed_y, gate, back, maps_t, reach, post_row)

    back_terms = swap_all(pay_back)

    normal_flat = normal.reshape(micro * length, inner)
    grad_output = dot(normal_flat, cotangent_flat, 0, 0)

    grad_gate, side_smalls = pl.pallas_call(
        partial(side_kernel, dims, inner_all),
        grid=(micro,),
        in_specs=[sum_spec, sum_spec, wide, gates, wide, acts, wide, row],
        out_specs=[gates, spec(EDGE, inner)],
        out_shape=[shape(micro, long, inner), shape(micro, EDGE, inner)],
        compiler_params=PARAMS,
        name="side",
    )(sums, peer_sums, mixed_y, gate, back, act, grad_y, post_row)
    grad_gate_flat = grad_gate.reshape(micro * long, inner)
    grad_gating = dot(normed_flat, grad_gate_flat, 0, 0)
    early = PairTotal("seq")
    early.now = [grad_output, grad_gating]
    back_terms = early.ahead_of(back_terms)
    prefixed = prefix(back_terms, terms, 1 - direction)
    back_arrived = swap_all(prefixed)
    grad_y = tie(grad_y, prefixed)[0]

    grad_inside, grad_maps, own, column_sums = pl.pallas_call(
        partial(inside_back_kernel, dims),
        grid=(micro,),
        in_specs=[smem, smem, acts, wide, small, flat, small, state_spec, row],
        out_specs=[wide, spec(length, maps_width), small, small],
        out_shape=[
            shape(micro, length, inner),
            shape(micro, length, maps_width),
            shape(micro, length, both),
            shape(micro, length, both),
        ],
        scratch_shapes=[pltpu.VMEM((both, length), F32)],
        compiler_params=PARAMS,
        name="inside_back",
    )(where, lengths, act, grad_y, late, run_rows, reach, before_states, direct_row)

    grad_normed_gate = dot(grad_gate_flat, gating, 1, 1)
    back_arrived = tie(back_arrived, own, grad_normed_gate)[0]

    grad_mixed, grad_mixed_maps, grad_raw, smalls = pl.pallas_call(
        partial(end_kernel, dims),
        grid=(micro,),
        in_specs=[
            smem,
            smem,
            plain_spec,
            acts,
            small,
            small,
            acts,
            state_spec,
            spec(1, both),
            wide,
            spec(length, maps_width),
            small,
            small,
            spec(long, width),
            fixed(EDGE, width),
            fixed(2, heads),
        ],
        out_specs=[gates, spec(long, maps_width), spec(long, both), spec(2 * EDGE, width)],
        out_shape=[
            shape(micro, long, inner),
            shape(micro, long, maps_width),
            shape(micro, long, both),
            shape(micro, 2 * EDGE, width),
        ],
        scratch_shapes=[
            pltpu.VMEM((2, state, inner), F32),
            pltpu.VMEM((length, width), F32),
            pltpu.VMEM((long + 2 * EDGE, LANES), jnp.int32),
            pltpu.VMEM((count, length, LANES), F32),
        ],
        compiler_params=PARAMS,
        name="end",
    )(
        where,
        lengths,
        back_arrived,
        act,
        z,
        tail,
        conv,
        before_states,
        keep,
        grad_inside,
        grad_maps,
        own,
        column_sums,
        mixed,
        taps,
        decays,
    )
    all_maps = grad_mixed_maps.reshape(micro * long, maps_width)
    all_maps = all_maps + lax.ppermute(all_maps, "head", swap)

    early.take(grad_raw)
    grad_mixed = early.ahead_of(grad_mixed)
    grad_mixed = grad_mixed.reshape(micro * long, inner)
    grad_mixed_maps = grad_mixed_maps.reshape(micro * long, maps_width)
    grad_raw = grad_raw.reshape(micro * long, both)
    cut = maps_width // 2
    most = (model + cut + cut) // 2
    late_total = PairTotal("seq")
    late_total.now = [dot(normed_flat[:, :most], grad_mixed, 0, 0), None]
    grad_normed = (
        dot(grad_mixed, values, 1, 1)
        + dot(grad_mixed_maps, states_flat, 1, 1)
        + grad_normed_gate
        + dot(grad_raw, stepper_flat, 1, 1)
    )
    grad_prenorm = jnp.sum(grad_normed * normed_flat, axis=0, keepdims=True) / prenorm[None]
    early.take(grad_prenorm, late_total.now[0])
    normed_flat = early.ahead_of(normed_flat)
    own_maps = lax.dynamic_slice_in_dim(all_maps, head_place * cut, cut, 1)
    second_late = pl.pallas_call(
        partial(pack_kernel, dims),
        in_specs=[vmem] * 6,
        out_specs=vmem,
        out_shape=shape(most, inner),
        compiler_params=PARAMS,
        name="pack",
    )(
        dot(normed_flat[:, most:], grad_mixed, 0, 0),
        dot(own_maps, normed_flat, 0, 0),
        smalls,
        side_smalls,
        dot(grad_raw, normed_flat, 0, 0),
        grad_prenorm,
    )
    late_total.now[1] = second_late
    grad_normed = late_total.ahead_of(grad_normed)

    grad_normed = grad_normed.reshape(micro, long, model)
    grad_normed = grad_normed + lax.ppermute(grad_normed, "head", swap)
    from_after = lax.ppermute(grad_normed[:, :EDGE], "seq", down)
    from_before = lax.ppermute(grad_normed[:, EDGE + length :], "seq", up)
    grad_here = grad_normed[:, EDGE : EDGE + length] + jnp.concatenate(
        [from_before, jnp.zeros((micro, length - 2 * EDGE, model), F32), from_after], axis=1
    )
    scale = lax.rsqrt(jnp.mean(hidden * hidden, axis=2, keepdims=True) + EPSILON)
    pulled = grad_here * prenorm
    grad_hidden = (
        cotangent
        + scale * pulled
        - hidden * (scale**3 * jnp.sum(pulled * hidden, axis=2, keepdims=True) / model)
    )

    normal_flat = tie(normal_flat, second_late)[0]
    projected = dot(normal_flat, output)
    result = hidden + (projected + lax.ppermute(projected, "head", swap)).reshape(hidden.shape)

    held = second_late
    for mine in "eelelellellel":
        total = late_total if mine == "l" else early
        held = total.turn(held)
    while late_total.at < len(late_total.steps) - 1:
        held = late_total.turn(held)
        held = early.turn(held)
    while not early.done:
        held = early.turn(held)
    late_total.take(held, grad_hidden, result)
    late_done = late_total.now
    grad_output, grad_gating = early.now
    last = late_done[1][model - most :]
    peer_last = lax.ppermute(last, "head", swap)
    own_states, other_states = last[:cut], peer_last[:cut]
    grad_states = jnp.where(
        head_place == 0,
        jnp.concatenate([own_states, other_states]),
        jnp.concatenate([other_states, own_states]),
    ).T.reshape(states.shape)
    grad_stepper = last[cut : cut + both].T.reshape(stepper.shape)
    (
        grad_filters,
        grad_shifts,
        grad_kernels,
        grad_biases,
        grad_postnorm,
        grad_direct,
        grad_offsets,
        grad_decays,
        grad_prenorm,
    ) = pl.pallas_call(
        partial(unpack_kernel, dims),
        in_specs=[vmem, vmem],
        out_specs=[vmem] * 9,
        out_shape=[
            shape(count, inner),
            shape(inner),
            shape(*kernels.shape),
            shape(*biases.shape),
            shape(inner),
            shape(heads),
            shape(*offsets.shape),
            shape(*decays.shape),
            shape(model),
        ],
        compiler_params=PARAMS,
        name="unpack",
    )(last, peer_last)
    late_done = jnp.concatenate([late_done[0], late_done[1][: model - most]], axis=0)
    return (
        result,
        grad_hidden,
        grad_prenorm,
        grad_gating,
        late_done,
        grad_states,
        grad_stepper,
        grad_offsets,
        grad_decays,
        grad_filters,
        grad_shifts,
        grad_kernels,
        grad_biases,
        grad_direct,
        grad_postnorm,
        grad_output,
    )


def solution(mesh):
    in_specs = (
        P(None, "seq", None),
        P(),
        P(),
        P(None, "head"),
        P(None, "head"),
        P(),
        P(None, None, "head"),
        P(None, "head"),
        P(None, "head"),
        P(None, "head"),
        P("head"),
        P(),
        P(),
        P("head"),
        P("head"),
        P("head", None),
        P(None, "seq", None),
    )
    out_specs = (
        P(None, "seq", None),
        P(None, "seq", None),
        P(),
        P(None, "head"),
        P(None, "head"),
        P(),
        P(None, None, "head"),
        P(None, "head"),
        P(None, "head"),
        P(None, "head"),
        P("head"),
        P(),
        P(),
        P("head"),
        P("head"),
        P("head", None),
    )
    return jax.shard_map(local, mesh=mesh, in_specs=in_specs, out_specs=out_specs, check_vma=False)
```

profile of v0, /device:TPU:9, one launch (start us, length us, event | category | flops | bytes accessed | tf_op | source)
XLA Modules:
  0.0 342.8 jit_solution(9972872407225245268)
XLA Ops:
  1.7 3.1 collective-permute-start
  4.8 4.0 %collective-permute-start.1 = (f32[2,8,768]{2,1,0:T(8,128)S(1)}, f32[2,8,768]{2,1,0:T(8,128)S(1)}, u32[]{:S(2)}, u32[]{:S(2)}) collective-permute-start(f32[2,8,768]{2,1,0:T(8,128)S(1)} %get-tuple-element.198), channel_id=1, source_target_pairs={{2,0},{4,2},{6,4},{8,6},{10,8},{12,10},{14,12},{16,14},{18,16},{20... | collective-permute-start | bytes 147464 | tf_op jit(solution)/shard_map/ppermute | solution.py:937
  8.8 2.3 copy.38.states
  13.8 14.3 %front.1 = (f32[2,272,768]{2,1,0:T(8,128)}, f32[2,272,1024]{2,1,0:T(8,128)}, f32[2,256,1024]{2,1,0:T(8,128)}, f32[2,256,1024]{2,1,0:T(8,128)}, f32[2,256,256]{2,...) custom-call(s32[1]{0:T(128)} %bitcast.place, ...), custom_call_target="tpu_custom_call" | custom-call | tf_op jit(solution)/shard_map/front/pallas_call | solution.py:979
  28.1 4.9 %all-to-all-start = ((f32[16,104,128]{2,1,0:T(8,128)}), f32[16,104,128]{2,1,0:T(8,128)S(1)}, u32[]{:S(2)}, u32[]{:S(2)}) async-start(f32[16,104,128]{2,1,0:T(8,128)} %get-tuple-element.90), calls=%async_computation | async-start | bytes 1703936 | tf_op jit(solution)/shard_map/all_to_all | solution.py:1071
  33.0 20.2 %all-to-all-done.terms.keeps = f32[16,104,128]{2,1,0:T(8,128)S(1)} async-done(((f32[16,104,128]{2,1,0:T(8,128)}), f32[16,104,128]{2,1,0:T(8,128)S(1)}, u32[]{:S(2)}, u32[]{:S(2)}) %all-to-all-start) | async-done | bytes 852000 | tf_op jit(solution)/shard_map/all_to_all | solution.py:1071
  54.2 2.4 prefix.2
  56.6 5.0 %all-to-all-start.1 = ((f32[16,96,128]{2,1,0:T(8,128)}), f32[16,96,128]{2,1,0:T(8,128)S(1)}, u32[]{:S(2)}, u32[]{:S(2)}) async-start(f32[16,96,128]{2,1,0:T(8,128)} %prefix.2), calls=%async_computation.1 | async-start | bytes 1572864 | tf_op jit(solution)/shard_map/all_to_all | solution.py:1071
  62.9 5.4 %fusion.back = f32[2,256,768]{2,1,0:T(8,128)} fusion(f32[2,256,768]{2,1,0:T(8,128)} %param.33, f32[768,768]{1,0:T(8,128)} %param.32), kind=kOutput, calls=%fused_computation.3 | convolution fusion | flops 1811939328 | bytes 5505024 | tf_op jit(solution)/shard_map/dot_general | solution.py:22
  68.3 5.9 %inside.1 = f32[2,256,768]{2,1,0:T(8,128)} custom-call(s32[1]{0:T(128)} %bitcast.place, s32[2,8]{1,0:T(2,128)} %lengths.7, f32[2,256,1024]{2,1,0:T(8,128)} %get-tuple-element.87.act, f32[2,256,24]{2,1,0:T(8,128)} %get-tuple-element.88.run, f32[2,24,256]{2,1,0:T(8,128)} %get-tuple-element.89.late_rows), custom_call_target="tpu_custom_call" | custom-call | tf_op jit(solution)/shard_map/inside/pallas_call | solution.py:1079
  74.3 3.4 %fusion.2.gate = f32[2,272,768]{2,1,0:T(8,128)} fusion(f32[2,272,768]{2,1,0:T(8,128)S(1)} %copy-done.2, f32[768,768]{1,0:T(8,128)S(1)} %copy-done), kind=kOutput, calls=%fused_computation.5 | convolution fusion | flops 1925185536 | bytes 5701632 | tf_op jit(solution)/shard_map/dot_general | solution.py:22
  77.7 2.7 all-to-all-done.1.pay
  81.3 5.1 %join.1 = (f32[2,256,768]{2,1,0:T(8,128)}, f32[2,256,128]{2,1,0:T(8,128)}, f32[2,2,64,768]{3,2,1,0:T(8,128)}) custom-call(f32[2,256,768]{2,1,0:T(8,128)} %inside.1, f32[16,96,128]{2,1,0:T(8,128)} %copy-done.28, f32[2,256,1024]{2,1,0:T(8,128)} %get-tuple-element.87.act, f32[2,256,24]{2,1,0:T(8,128)} %get-tuple-element.91.reach, f32[2,272,768]{2,1,0:T(8,128)} %fusion.2.gate, ...), custom_call_target="tpu_custom_call" | custom-call | tf_op jit(solution)/shard_map/join/pallas_call | solution.py:1093
  86.4 2.3 collective-permute-start.2
  90.8 5.0 %turn.1 = (f32[2,256,768]{2,1,0:T(8,128)}, f32[2,256,768]{2,1,0:T(8,128)}, f32[16,96,128]{2,1,0:T(8,128)}) custom-call(f32[2,256,128]{2,1,0:T(8,128)} %get-tuple-element.93.sums, f32[2,256,128]{2,1,0:T(8,128)} %copy-done.32, f32[2,256,768]{2,1,0:T(8,128)} %get-tuple-element.94.mixed_y, f32[2,272,768]{2,1,0:T(8,128)} %fusion.2.gate, ...), custom_call_target="tpu_custom_call" | custom-call | tf_op jit(solution)/shard_map/turn/pallas_call | solution.py:1108
  95.7 4.7 %all-to-all-start.2 = ((f32[16,96,128]{2,1,0:T(8,128)}), f32[16,96,128]{2,1,0:T(8,128)S(1)}, u32[]{:S(2)}, u32[]{:S(2)}) async-start(f32[16,96,128]{2,1,0:T(8,128)} %get-tuple-element.99), calls=%async_computation.2 | async-start | bytes 1572864 | tf_op jit(solution)/shard_map/all_to_all | solution.py:1071
  100.5 5.3 %side.1 = (f32[2,272,768]{2,1,0:T(8,128)}, f32[2,8,768]{2,1,0:T(8,128)}) custom-call(f32[2,256,128]{2,1,0:T(8,128)} %get-tuple-element.93.sums, f32[2,256,128]{2,1,0:T(8,128)} %copy-done.32, f32[2,256,768]{2,1,0:T(8,128)} %get-tuple-element.94.mixed_y, f32[2,272,768]{2,1,0:T(8,128)} %fusion.2.gate, f32[2,256,768]{2,1,0:T(8,128)} %fusion.back, ...), custom_call_target="tpu_custom_call" | custom-call | tf_op jit(solution)/shard_map/side/pallas_call | solution.py:1136
  105.8 5.0 %convolution_bitcast_fusion = f32[768,768]{1,0:T(8,128)S(1)} fusion(f32[2,272,768]{2,1,0:T(8,128)S(1)} %copy-done.3, f32[2,272,768]{2,1,0:T(8,128)} %get-tuple-element.98), kind=kOutput, calls=%fused_computation.7 | convolution fusion | flops 1925185536 | bytes 5701632 | tf_op jit(solution)/shard_map/dot_general | solution.py:22
  113.4 2.4 convolution_bitcast_fusion.1
  120.3 2.4 prefix.3
  122.7 5.6 %all-to-all-start.3 = ((f32[16,96,128]{2,1,0:T(8,128)}), f32[16,96,128]{2,1,0:T(8,128)S(1)}, u32[]{:S(2)}, u32[]{:S(2)}) async-start(f32[16,96,128]{2,1,0:T(8,128)} %prefix.3), calls=%async_computation.3 | async-start | bytes 1572864 | tf_op jit(solution)/shard_map/all_to_all | solution.py:1071
  130.7 4.8 %fusion.17 = f32[544,768]{1,0:T(8,128)} fusion(f32[544,768]{1,0:T(8,128)} %bitcast.60, f32[768,768]{1,0:T(8,128)S(1)} %copy-done), kind=kOutput, calls=%fused_computation.69 | convolution fusion | flops 1925185536 | bytes 5701632 | tf_op jit(solution)/shard_map/dot_general | solution.py:22
  135.5 13.6 %inside_back.1 = (f32[2,256,768]{2,1,0:T(8,128)}, f32[2,256,256]{2,1,0:T(8,128)}, f32[2,256,24]{2,1,0:T(8,128)}, f32[2,256,24]{2,1,0:T(8,128)}) custom-call(s32[1]{0:T(128)} %bitcast.place, s32[2,8]{1,0:T(2,128)} %lengths.7, f32[2,256,1024]{2,1,0:T(8,128)} %get-tuple-element.87.act, f32[2,256,768]{2,1,0:T(8,128)} %get-tuple-element.101.grad_y, ...), custom_call_target="tpu_custom_call" | custom-call | tf_op jit(solution)/shard_map/inside_back/pallas_call | solution.py:1154
  150.0 16.4 %end.1 = (f32[2,272,768]{2,1,0:T(8,128)}, f32[2,272,256]{2,1,0:T(8,128)}, f32[2,272,24]{2,1,0:T(8,128)}, f32[2,16,1024]{2,1,0:T(8,128)}) custom-call(s32[1]{0:T(128)} %bitcast.place, s32[2,8]{1,0:T(2,128)} %lengths.7, f32[16,96,128]{2,1,0:T(8,128)} %copy-done.24, f32[2,256,1024]{2,1,0:T(8,128)} %get-tuple-element.87.act, ...), custom_call_target="tpu_custom_call" | custom-call | tf_op jit(solution)/shard_map/end/pallas_call | solution.py:1173
  166.4 1.6 dynamic-slice_add_fusion.1
  168.4 1.6 dynamic-slice_add_fusion
  170.7 2.3 fusion.18
  173.9 2.7 collective-permute-start.7
  176.6 2.4 multiply_reduce_fusion
  179.0 2.3 fusion.5
  184.3 1.6 fusion.9.own_states
  187.1 2.1 fusion.7.rest
  189.2 2.6 pack.1
  191.8 2.1 constant_dynamic-slice_fusion.4
  195.0 1.6 collective-permute-done.14
  196.9 2.1 collective-permute-start.15
  199.0 12.7 %collective-permute-done.15 = f32[96,768]{1,0:T(8,128)S(1)} collective-permute-done((f32[96,768]{1,0:T(8,128)S(1)}, f32[96,768]{1,0:T(8,128)S(1)}, u32[]{:S(2)}, u32[]{:S(2)}) %collective-permute-start.15) | collective-permute-done | bytes 294944 | tf_op jit(solution)/shard_map/ppermute | solution.py:799
  212.5 3.1 collective-permute-start.18
  219.7 2.6 collective-permute-start.16
  222.4 3.9 %collective-permute-done.18 = f32[96,768]{1,0:T(8,128)} collective-permute-done((f32[96,768]{1,0:T(8,128)}, f32[96,768]{1,0:T(8,128)}, u32[]{:S(2)}, u32[]{:S(2)}) %collective-permute-start.18) | collective-permute-done | bytes 294944 | tf_op jit(solution)/shard_map/ppermute | solution.py:799
  227.5 2.1 collective-permute-start.20
  232.4 5.0 %fusion.21 = f32[512,768]{1,0:T(8,128)} fusion(f32[512,768]{1,0:T(8,128)} %bitcast.61, f32[768,768]{1,0:T(8,128)S(1)} %copy-done.15), kind=kOutput, calls=%fused_computation.73 | convolution fusion | flops 1811939328 | bytes 5505024 | tf_op jit(solution)/shard_map/dot_general | solution.py:22
  237.3 1.7 collective-permute-start.8
  239.0 2.4 collective-permute-done.20
  243.0 6.9 %collective-permute-done.19 = f32[128,768]{1,0:T(8,128)S(1)} collective-permute-done((f32[128,768]{1,0:T(8,128)S(1)}, f32[128,768]{1,0:T(8,128)S(1)}, u32[]{:S(2)}, u32[]{:S(2)}) %collective-permute-start.19) | collective-permute-done | bytes 393248 | tf_op jit(solution)/shard_map/ppermute | solution.py:799
  251.1 3.7 %collective-permute-start.21 = (f32[64,768]{1,0:T(8,128)S(1)}, f32[64,768]{1,0:T(8,128)S(1)}, u32[]{:S(2)}, u32[]{:S(2)}) collective-permute-start(f32[64,768]{1,0:T(8,128)S(1)} %constant_dynamic-slice_fusion), channel_id=1, source_target_pairs={{0,16},{2,18},{4,20},{6,22},{8,24},{10,26},{12,28},{14,30},{16,0},... | collective-permute-start | bytes 589832 | tf_op jit(solution)/shard_map/ppermute | solution.py:799
  254.8 8.8 %collective-permute-done.21 = f32[64,768]{1,0:T(8,128)S(1)} collective-permute-done((f32[64,768]{1,0:T(8,128)S(1)}, f32[64,768]{1,0:T(8,128)S(1)}, u32[]{:S(2)}, u32[]{:S(2)}) %collective-permute-start.21) | collective-permute-done | bytes 196640 | tf_op jit(solution)/shard_map/ppermute | solution.py:799
  263.7 3.2 collective-permute-start.22
  268.2 2.4 collective-permute-start.29
  274.2 2.1 add.158
  276.3 2.1 add.164
  278.4 4.2 %collective-permute-done.25 = f32[128,768]{1,0:T(8,128)S(1)} collective-permute-done((f32[128,768]{1,0:T(8,128)S(1)}, f32[128,768]{1,0:T(8,128)S(1)}, u32[]{:S(2)}, u32[]{:S(2)}) %collective-permute-start.25) | collective-permute-done | bytes 393248 | tf_op jit(solution)/shard_map/ppermute | solution.py:799
  285.0 2.1 collective-permute-start.10
  287.1 10.1 %collective-permute-done.29 = f32[384,768]{1,0:T(8,128)S(1)} collective-permute-done((f32[384,768]{1,0:T(8,128)S(1)}, f32[384,768]{1,0:T(8,128)S(1)}, u32[]{:S(2)}, u32[]{:S(2)}) %collective-permute-start.29) | collective-permute-done | bytes 1179680 | tf_op jit(solution)/shard_map/ppermute | solution.py:799
  297.1 1.9 collective-permute-start.11
  299.1 1.6 maximum_select_fusion
  300.7 4.9 %collective-permute-done.26 = f32[128,768]{1,0:T(8,128)S(1)} collective-permute-done((f32[128,768]{1,0:T(8,128)S(1)}, f32[128,768]{1,0:T(8,128)S(1)}, u32[]{:S(2)}, u32[]{:S(2)}) %collective-permute-start.26) | collective-permute-done | bytes 393248 | tf_op jit(solution)/shard_map/ppermute | solution.py:799
  310.0 2.2 multiply_subtract_fusion
  312.2 11.0 %collective-permute-done.31 = f32[256,768]{1,0:T(8,128)S(1)} collective-permute-done((f32[256,768]{1,0:T(8,128)S(1)}, f32[256,768]{1,0:T(8,128)S(1)}, u32[]{:S(2)}, u32[]{:S(2)}) %collective-permute-start.31) | collective-permute-done | bytes 786464 | tf_op jit(solution)/shard_map/ppermute | solution.py:799
  323.2 1.7 collective-permute-done.30
  326.9 3.4 %collective-permute-start.32 = (f32[256,768]{1,0:T(8,128)}, f32[256,768]{1,0:T(8,128)}, u32[]{:S(2)}, u32[]{:S(2)}) collective-permute-start(f32[256,768]{1,0:T(8,128)} %get-tuple-element.195.mine), channel_id=1, source_target_pairs={{0,1},{1,0},{2,3},{3,2},{4,5},{5,4},{6,7},{7,6},{8,9},{9,8},{10,11... | collective-permute-start | bytes 2359304 | tf_op jit(solution)/shard_map/ppermute | solution.py:1299
  330.3 3.4 maximum_select_fusion.1
  336.4 1.6 pad_maximum_fusion
  340.2 2.2 unpack.1
  (181 shorter events, 56.9 us)
Async XLA Ops:
  0.6 73.6 %copy-start = (f32[768,768]{1,0:T(8,128)S(1)}, f32[768,768]{1,0:T(8,128)}, u32[]{:S(2)}) copy-start(f32[768,768]{1,0:T(8,128)} %param.20) | copy-start | bytes 7077892
  0.7 10.4 %copy-start.36 = (f32[768,2,12]{0,1,2:T(2,128)S(1)}, f32[768,2,12]{0,1,2:T(2,128)}, u32[]{:S(2)}) copy-start(f32[768,2,12]{0,1,2:T(2,128)} %param.23) | copy-start | bytes 221188
  0.7 11.3 %copy-start.37 = (f32[768]{0:T(1024)S(1)}, f32[768]{0:T(1024)}, u32[]{:S(2)}) copy-start(f32[768]{0:T(1024)} %param.19) | copy-start | bytes 9220
  0.7 11.9 %copy-start.40 = (f32[768]{0:T(1024)S(1)}, f32[768]{0:T(1024)}, u32[]{:S(2)}) copy-start(f32[768]{0:T(1024)} %param.27) | copy-start | bytes 9220
  1.7 11.5 %collective-permute-start = (f32[2,8,768]{2,1,0:T(8,128)S(1)}, f32[2,8,768]{2,1,0:T(8,128)S(1)}, u32[]{:S(2)}, u32[]{:S(2)}) collective-permute-start(f32[2,8,768]{2,1,0:T(8,128)S(1)} %get-tuple-element.199), channel_id=1, source_target_pairs={{0,2},{2,4},{4,6},{6,8},{8,10},{10,12},{12,14},{14,16},{16,18},{18... | collective-permute-start | bytes 147464 | tf_op jit(solution)/shard_map/ppermute | solution.py:936
  4.8 8.4 %collective-permute-start.1 = (f32[2,8,768]{2,1,0:T(8,128)S(1)}, f32[2,8,768]{2,1,0:T(8,128)S(1)}, u32[]{:S(2)}, u32[]{:S(2)}) collective-permute-start(f32[2,8,768]{2,1,0:T(8,128)S(1)} %get-tuple-element.198), channel_id=1, source_target_pairs={{2,0},{4,2},{6,4},{8,6},{10,8},{12,10},{14,12},{16,14},{18,16},{20... | collective-permute-start | bytes 147464 | tf_op jit(solution)/shard_map/ppermute | solution.py:937
  28.1 25.1 %all-to-all-start = ((f32[16,104,128]{2,1,0:T(8,128)}), f32[16,104,128]{2,1,0:T(8,128)S(1)}, u32[]{:S(2)}, u32[]{:S(2)}) async-start(f32[16,104,128]{2,1,0:T(8,128)} %get-tuple-element.90), calls=%async_computation | async-start | bytes 1703936 | tf_op jit(solution)/shard_map/all_to_all | solution.py:1071
  54.2 7.5 %copy-start.41 = (f32[768]{0:T(1024)S(1)}, f32[768]{0:T(1024)}, u32[]{:S(2)}) copy-start(f32[768]{0:T(1024)} %param.31) | copy-start | bytes 9220
  54.2 8.1 %copy-start.42 = (f32[12]{0:T(128)S(1)}, f32[12]{0:T(128)}, u32[]{:S(2)}) copy-start(f32[12]{0:T(128)} %param.30) | copy-start | bytes 148
  56.6 23.8 %all-to-all-start.1 = ((f32[16,96,128]{2,1,0:T(8,128)}), f32[16,96,128]{2,1,0:T(8,128)S(1)}, u32[]{:S(2)}, u32[]{:S(2)}) async-start(f32[16,96,128]{2,1,0:T(8,128)} %prefix.2), calls=%async_computation.1 | async-start | bytes 1572864 | tf_op jit(solution)/shard_map/all_to_all | solution.py:1071
  68.3 5.9 %copy-start.2 = (f32[2,272,768]{2,1,0:T(8,128)S(1)}, f32[2,272,768]{2,1,0:T(8,128)}, u32[]{:S(2)}) copy-start(f32[2,272,768]{2,1,0:T(8,128)} %get-tuple-element.92) | copy-start | bytes 5013508
  86.4 3.6 %collective-permute-start.2 = (f32[2,256,128]{2,1,0:T(8,128)}, f32[2,256,128]{2,1,0:T(8,128)S(1)}, u32[]{:S(2)}, u32[]{:S(2)}) collective-permute-start(f32[2,256,128]{2,1,0:T(8,128)} %get-tuple-element.93.sums), channel_id=1, source_target_pairs={{0,1},{1,0},{2,3},{3,2},{4,5},{5,4},{6,7},{7,6},{8,9},{9,8},{10,11... | collective-permute-start | bytes 786440 | tf_op jit(solution)/shard_map/ppermute | solution.py:1106
  95.7 23.6 %all-to-all-start.2 = ((f32[16,96,128]{2,1,0:T(8,128)}), f32[16,96,128]{2,1,0:T(8,128)S(1)}, u32[]{:S(2)}, u32[]{:S(2)}) async-start(f32[16,96,128]{2,1,0:T(8,128)} %get-tuple-element.99), calls=%async_computation.2 | async-start | bytes 1572864 | tf_op jit(solution)/shard_map/all_to_all | solution.py:1071
  100.5 5.3 %copy-start.3 = (f32[2,272,768]{2,1,0:T(8,128)S(1)}, f32[2,272,768]{2,1,0:T(8,128)}, u32[]{:S(2)}) copy-start(f32[2,272,768]{2,1,0:T(8,128)} %get-tuple-element.92) | copy-start | bytes 5013508
  105.8 6.8 %copy-start.20 = (f32[2,256,768]{2,1,0:T(8,128)S(1)}, f32[2,256,768]{2,1,0:T(8,128)}, u32[]{:S(2)}) copy-start(f32[2,256,768]{2,1,0:T(8,128)} %get-tuple-element.96) | copy-start | bytes 4718596
  110.8 2.6 copy-start.7
  122.7 26.4 %all-to-all-start.3 = ((f32[16,96,128]{2,1,0:T(8,128)}), f32[16,96,128]{2,1,0:T(8,128)S(1)}, u32[]{:S(2)}, u32[]{:S(2)}) async-start(f32[16,96,128]{2,1,0:T(8,128)} %prefix.3), calls=%async_computation.3 | async-start | bytes 1572864 | tf_op jit(solution)/shard_map/all_to_all | solution.py:1071
  128.3 38.1 %collective-permute-start.4 = (f32[384,768]{1,0:T(8,128)}, f32[384,768]{1,0:T(8,128)}, u32[]{:S(2)}, u32[]{:S(2)}) collective-permute-start(f32[384,768]{1,0:T(8,128)} %constant_dynamic-slice_fusion.8), channel_id=1, source_target_pairs={{0,4},{2,6},{4,0},{6,2},{8,12},{10,14},{12,8},{14,10},{16,20},{18,... | collective-permute-start | bytes 3538952 | tf_op jit(solution)/shard_map/ppermute | solution.py:799
  129.5 36.9 %collective-permute-start.3 = (f32[384,768]{1,0:T(8,128)}, f32[384,768]{1,0:T(8,128)}, u32[]{:S(2)}, u32[]{:S(2)}) collective-permute-start(f32[384,768]{1,0:T(8,128)} %constant_dynamic-slice_fusion.9), channel_id=1, source_target_pairs={{0,2},{2,0},{4,6},{6,4},{8,10},{10,8},{12,14},{14,12},{16,18},{18,... | collective-permute-start | bytes 3538952 | tf_op jit(solution)/shard_map/ppermute | solution.py:799
  150.0 16.4 %copy-start.14 = (f32[768,768]{1,0:T(8,128)S(1)}, f32[768,768]{1,0:T(8,128)}, u32[]{:S(2)}) copy-start(f32[768,768]{1,0:T(8,128)} %copy-done.13) | copy-start | bytes 7077892
  168.1 2.4 copy-start.5
  168.1 2.6 copy-start.10
  168.1 15.7 %collective-permute-start.6 = (f32[192,768]{1,0:T(8,128)S(1)}, f32[192,768]{1,0:T(8,128)S(1)}, u32[]{:S(2)}, u32[]{:S(2)}) collective-permute-start(f32[192,768]{1,0:T(8,128)S(1)} %constant_dynamic-slice_fusion.6), channel_id=1, source_target_pairs={{0,2},{2,0},{4,6},{6,4},{8,10},{10,8},{12,14},{14,12},{16,18},{18,... | collective-permute-start | bytes 1769480 | tf_op jit(solution)/shard_map/ppermute | solution.py:799
  170.1 13.7 %collective-permute-start.5 = (f32[192,768]{1,0:T(8,128)S(1)}, f32[192,768]{1,0:T(8,128)S(1)}, u32[]{:S(2)}, u32[]{:S(2)}) collective-permute-start(f32[192,768]{1,0:T(8,128)S(1)} %constant_dynamic-slice_fusion.7), channel_id=1, source_target_pairs={{0,4},{2,6},{4,0},{6,2},{8,12},{10,14},{12,8},{14,10},{16,20},{18,... | collective-permute-start | bytes 1769480 | tf_op jit(solution)/shard_map/ppermute | solution.py:799
  170.7 2.4 copy-start.31
  170.7 3.2 copy-start.29
  170.7 5.9 %copy-start.17 = (f32[544,768]{1,0:T(8,128)S(1)}, f32[544,768]{1,0:T(8,128)}, u32[]{:S(2)}) copy-start(f32[544,768]{1,0:T(8,128)} %fusion.17) | copy-start | bytes 5013508
  170.7 5.9 %copy-start.23 = (f32[768,4,64]{0,2,1:T(8,128)S(1)}, f32[768,4,64]{0,2,1:T(8,128)}, u32[]{:S(2)}) copy-start(f32[768,4,64]{0,2,1:T(8,128)} %param.22) | copy-start | bytes 2359300
  173.0 3.6 %copy-start.4 = (f32[2,272,768]{2,1,0:T(8,128)S(1)}, f32[2,272,768]{2,1,0:T(8,128)}, u32[]{:S(2)}) copy-start(f32[2,272,768]{2,1,0:T(8,128)} %get-tuple-element.92) | copy-start | bytes 5013508
  173.9 10.4 %collective-permute-start.7 = (f32[544,256]{1,0:T(8,128)S(1)}, f32[544,256]{1,0:T(8,128)S(1)}, u32[]{:S(2)}, u32[]{:S(2)}) collective-permute-start(f32[544,256]{1,0:T(8,128)S(1)} %bitcast.65), channel_id=1, source_target_pairs={{0,1},{1,0},{2,3},{3,2},{4,5},{5,4},{6,7},{7,6},{8,9},{9,8},{10,11... | collective-permute-start | bytes 1671176 | tf_op jit(solution)/shard_map/ppermute | solution.py:1228
  181.3 2.6 copy-start.18
  182.9 32.7 %collective-permute-start.12 = (f32[256,768]{1,0:T(8,128)}, f32[256,768]{1,0:T(8,128)S(1)}, u32[]{:S(2)}, u32[]{:S(2)}) collective-permute-start(f32[256,768]{1,0:T(8,128)} %constant_dynamic-slice_fusion.5), channel_id=1, source_target_pairs={{0,2},{2,0},{4,6},{6,4},{8,10},{10,8},{12,14},{14,12},{16,18},{18,... | collective-permute-start | bytes 2359304 | tf_op jit(solution)/shard_map/ppermute | solution.py:799
  183.9 12.7 %collective-permute-start.14 = (f32[192,768]{1,0:T(8,128)S(1)}, f32[192,768]{1,0:T(8,128)S(1)}, u32[]{:S(2)}, u32[]{:S(2)}) collective-permute-start(f32[192,768]{1,0:T(8,128)S(1)} %broadcast_select_fusion.2), channel_id=1, source_target_pairs={{0,8},{2,10},{4,12},{6,14},{8,0},{10,2},{12,4},{14,6},{16,24},{18,... | collective-permute-start | bytes 1769480 | tf_op jit(solution)/shard_map/ppermute | solution.py:799
  193.8 22.6 %collective-permute-start.13 = (f32[256,768]{1,0:T(8,128)}, f32[256,768]{1,0:T(8,128)}, u32[]{:S(2)}, u32[]{:S(2)}) collective-permute-start(f32[256,768]{1,0:T(8,128)} %constant_dynamic-slice_fusion.4), channel_id=1, source_target_pairs={{0,4},{2,6},{4,0},{6,2},{8,12},{10,14},{12,8},{14,10},{16,20},{18,... | collective-permute-start | bytes 2359304 | tf_op jit(solution)/shard_map/ppermute | solution.py:799
  196.9 14.8 %collective-permute-start.15 = (f32[96,768]{1,0:T(8,128)S(1)}, f32[96,768]{1,0:T(8,128)S(1)}, u32[]{:S(2)}, u32[]{:S(2)}) collective-permute-start(f32[96,768]{1,0:T(8,128)S(1)} %constant_dynamic-slice_fusion.3), channel_id=1, source_target_pairs={{0,16},{2,18},{4,20},{6,22},{8,24},{10,26},{12,28},{14,30},{16,0},... | collective-permute-start | bytes 884744 | tf_op jit(solution)/shard_map/ppermute | solution.py:799
  212.5 6.3 %copy-start.19 = (f32[512,768]{1,0:T(8,128)S(1)}, f32[512,768]{1,0:T(8,128)}, u32[]{:S(2)}) copy-start(f32[512,768]{1,0:T(8,128)} %copy-done.18) | copy-start | bytes 4718596
  212.5 13.7 %collective-permute-start.18 = (f32[96,768]{1,0:T(8,128)}, f32[96,768]{1,0:T(8,128)}, u32[]{:S(2)}, u32[]{:S(2)}) collective-permute-start(f32[96,768]{1,0:T(8,128)} %dynamic-slice_add_fusion.8), channel_id=1, source_target_pairs={{0,16},{2,18},{4,20},{6,22},{8,24},{10,26},{12,28},{14,30},{16,0},... | collective-permute-start | bytes 884744 | tf_op jit(solution)/shard_map/ppermute | solution.py:799
  218.8 10.9 %collective-permute-start.17 = (f32[128,768]{1,0:T(8,128)}, f32[128,768]{1,0:T(8,128)S(1)}, u32[]{:S(2)}, u32[]{:S(2)}) collective-permute-start(f32[128,768]{1,0:T(8,128)} %constant_dynamic-slice_fusion.1), channel_id=1, source_target_pairs={{0,2},{2,0},{4,6},{6,4},{8,10},{10,8},{12,14},{14,12},{16,18},{18,... | collective-permute-start | bytes 1179656 | tf_op jit(solution)/shard_map/ppermute | solution.py:799
  218.9 3.5 %copy-start.21 = (f32[256,768]{1,0:T(8,128)}, f32[256,768]{1,0:T(8,128)S(1)}, u32[]{:S(2)}) copy-start(f32[256,768]{1,0:T(8,128)S(1)} %dynamic-slice_add_fusion.3) | copy-start | bytes 2359300
  219.7 11.3 %collective-permute-start.16 = (f32[128,768]{1,0:T(8,128)}, f32[128,768]{1,0:T(8,128)}, u32[]{:S(2)}, u32[]{:S(2)}) collective-permute-start(f32[128,768]{1,0:T(8,128)} %constant_dynamic-slice_fusion.2), channel_id=1, source_target_pairs={{0,4},{2,6},{4,0},{6,2},{8,12},{10,14},{12,8},{14,10},{16,20},{18,... | collective-permute-start | bytes 1179656 | tf_op jit(solution)/shard_map/ppermute | solution.py:799
  222.3 10.0 %copy-start.15 = (f32[768,768]{1,0:T(8,128)S(1)}, f32[768,768]{1,0:T(8,128)}, u32[]{:S(2)}) copy-start(f32[768,768]{1,0:T(8,128)} %param.32) | copy-start | bytes 7077892
  227.5 13.9 %collective-permute-start.20 = (f32[192,768]{1,0:T(8,128)S(1)}, f32[192,768]{1,0:T(8,128)S(1)}, u32[]{:S(2)}, u32[]{:S(2)}) collective-permute-start(f32[192,768]{1,0:T(8,128)S(1)} %maximum_select_fusion.9), channel_id=1, source_target_pairs={{0,8},{2,10},{4,12},{6,14},{8,0},{10,2},{12,4},{14,6},{16,24},{18,... | collective-permute-start | bytes 1769480 | tf_op jit(solution)/shard_map/ppermute | solution.py:799
  232.3 17.7 %collective-permute-start.19 = (f32[128,768]{1,0:T(8,128)S(1)}, f32[128,768]{1,0:T(8,128)S(1)}, u32[]{:S(2)}, u32[]{:S(2)}) collective-permute-start(f32[128,768]{1,0:T(8,128)S(1)} %broadcast_select_fusion.5), channel_id=1, source_target_pairs={{0,8},{2,10},{4,12},{6,14},{8,0},{10,2},{12,4},{14,6},{16,24},{18,... | collective-permute-start | bytes 1179656 | tf_op jit(solution)/shard_map/ppermute | solution.py:799
  237.3 12.7 %copy-start.22 = (f32[256,768]{1,0:T(8,128)S(1)}, f32[256,768]{1,0:T(8,128)}, u32[]{:S(2)}) copy-start(f32[256,768]{1,0:T(8,128)} %copy-done.21) | copy-start | bytes 2359300
  237.3 36.9 %collective-permute-start.8 = (f32[512,768]{1,0:T(8,128)}, f32[512,768]{1,0:T(8,128)}, u32[]{:S(2)}, u32[]{:S(2)}) collective-permute-start(f32[512,768]{1,0:T(8,128)} %fusion.21), channel_id=1, source_target_pairs={{0,1},{1,0},{2,3},{3,2},{4,5},{5,4},{6,7},{7,6},{8,9},{9,8},{10,11... | collective-permute-start | bytes 4718600 | tf_op jit(solution)/shard_map/ppermute | solution.py:1284
  239.0 37.3 %collective-permute-start.9 = (f32[2,272,768]{2,1,0:T(8,128)}, f32[2,272,768]{2,1,0:T(8,128)}, u32[]{:S(2)}, u32[]{:S(2)}) collective-permute-start(f32[2,272,768]{2,1,0:T(8,128)} %bitcast.15), channel_id=1, source_target_pairs={{0,1},{1,0},{2,3},{3,2},{4,5},{5,4},{6,7},{7,6},{8,9},{9,8},{10,11... | collective-permute-start | bytes 5013512 | tf_op jit(solution)/shard_map/ppermute | solution.py:1268
  241.5 25.3 %collective-permute-start.23 = (f32[192,768]{1,0:T(8,128)S(1)}, f32[192,768]{1,0:T(8,128)}, u32[]{:S(2)}, u32[]{:S(2)}) collective-permute-start(f32[192,768]{1,0:T(8,128)S(1)} %get-tuple-element.201), channel_id=1, source_target_pairs={{0,4},{2,6},{4,0},{6,2},{8,12},{10,14},{12,8},{14,10},{16,20},{18,... | collective-permute-start | bytes 1769480 | tf_op jit(solution)/shard_map/ppermute | solution.py:799
  250.0 16.9 %collective-permute-start.24 = (f32[192,768]{1,0:T(8,128)S(1)}, f32[192,768]{1,0:T(8,128)}, u32[]{:S(2)}, u32[]{:S(2)}) collective-permute-start(f32[192,768]{1,0:T(8,128)S(1)} %get-tuple-element.200), channel_id=1, source_target_pairs={{0,2},{2,0},{4,6},{6,4},{8,10},{10,8},{12,14},{14,12},{16,18},{18,... | collective-permute-start | bytes 1769480 | tf_op jit(solution)/shard_map/ppermute | solution.py:799
  251.1 12.5 %collective-permute-start.21 = (f32[64,768]{1,0:T(8,128)S(1)}, f32[64,768]{1,0:T(8,128)S(1)}, u32[]{:S(2)}, u32[]{:S(2)}) collective-permute-start(f32[64,768]{1,0:T(8,128)S(1)} %constant_dynamic-slice_fusion), channel_id=1, source_target_pairs={{0,16},{2,18},{4,20},{6,22},{8,24},{10,26},{12,28},{14,30},{16,0},... | collective-permute-start | bytes 589832 | tf_op jit(solution)/shard_map/ppermute | solution.py:799
  263.7 9.6 %collective-permute-start.22 = (f32[64,768]{1,0:T(8,128)S(1)}, f32[64,768]{1,0:T(8,128)S(1)}, u32[]{:S(2)}, u32[]{:S(2)}) collective-permute-start(f32[64,768]{1,0:T(8,128)S(1)} %dynamic-slice_add_fusion.11), channel_id=1, source_target_pairs={{0,16},{2,18},{4,20},{6,22},{8,24},{10,26},{12,28},{14,30},{16,0},... | collective-permute-start | bytes 589832 | tf_op jit(solution)/shard_map/ppermute | solution.py:799
  268.2 28.9 %collective-permute-start.29 = (f32[384,768]{1,0:T(8,128)S(1)}, f32[384,768]{1,0:T(8,128)S(1)}, u32[]{:S(2)}, u32[]{:S(2)}) collective-permute-start(f32[384,768]{1,0:T(8,128)S(1)} %maximum_select_fusion.5), channel_id=1, source_target_pairs={{0,4},{2,6},{4,0},{6,2},{8,12},{10,14},{12,8},{14,10},{16,20},{18,... | collective-permute-start | bytes 3538952 | tf_op jit(solution)/shard_map/ppermute | solution.py:799
  271.9 27.1 %collective-permute-start.28 = (f32[384,768]{1,0:T(8,128)S(1)}, f32[384,768]{1,0:T(8,128)S(1)}, u32[]{:S(2)}, u32[]{:S(2)}) collective-permute-start(f32[384,768]{1,0:T(8,128)S(1)} %maximum_select_fusion.4), channel_id=1, source_target_pairs={{0,2},{2,0},{4,6},{6,4},{8,10},{10,8},{12,14},{14,12},{16,18},{18,... | collective-permute-start | bytes 3538952 | tf_op jit(solution)/shard_map/ppermute | solution.py:799
  273.3 9.3 %collective-permute-start.25 = (f32[128,768]{1,0:T(8,128)S(1)}, f32[128,768]{1,0:T(8,128)S(1)}, u32[]{:S(2)}, u32[]{:S(2)}) collective-permute-start(f32[128,768]{1,0:T(8,128)S(1)} %maximum_select_fusion.10), channel_id=1, source_target_pairs={{0,8},{2,10},{4,12},{6,14},{8,0},{10,2},{12,4},{14,6},{16,24},{18,... | collective-permute-start | bytes 1179656 | tf_op jit(solution)/shard_map/ppermute | solution.py:799
  282.7 22.9 %collective-permute-start.26 = (f32[128,768]{1,0:T(8,128)S(1)}, f32[128,768]{1,0:T(8,128)S(1)}, u32[]{:S(2)}, u32[]{:S(2)}) collective-permute-start(f32[128,768]{1,0:T(8,128)S(1)} %get-tuple-element.203), channel_id=1, source_target_pairs={{0,4},{2,6},{4,0},{6,2},{8,12},{10,14},{12,8},{14,10},{16,20},{18,... | collective-permute-start | bytes 1179656 | tf_op jit(solution)/shard_map/ppermute | solution.py:799
  283.7 23.2 %collective-permute-start.27 = (f32[128,768]{1,0:T(8,128)S(1)}, f32[128,768]{1,0:T(8,128)S(1)}, u32[]{:S(2)}, u32[]{:S(2)}) collective-permute-start(f32[128,768]{1,0:T(8,128)S(1)} %get-tuple-element.202), channel_id=1, source_target_pairs={{0,2},{2,0},{4,6},{6,4},{8,10},{10,8},{12,14},{14,12},{16,18},{18,... | collective-permute-start | bytes 1179656 | tf_op jit(solution)/shard_map/ppermute | solution.py:799
  285.0 24.4 %collective-permute-start.10 = (f32[2,8,768]{2,1,0:T(8,128)S(1)}, f32[2,8,768]{2,1,0:T(8,128)S(1)}, u32[]{:S(2)}, u32[]{:S(2)}) collective-permute-start(f32[2,8,768]{2,1,0:T(8,128)S(1)} %get-tuple-element.192), channel_id=1, source_target_pairs={{0,2},{2,4},{4,6},{6,8},{8,10},{10,12},{12,14},{14,16},{16,18},{18... | collective-permute-start | bytes 147464 | tf_op jit(solution)/shard_map/ppermute | solution.py:1270
  297.1 12.3 %collective-permute-start.11 = (f32[2,8,768]{2,1,0:T(8,128)S(1)}, f32[2,8,768]{2,1,0:T(8,128)S(1)}, u32[]{:S(2)}, u32[]{:S(2)}) collective-permute-start(f32[2,8,768]{2,1,0:T(8,128)S(1)} %get-tuple-element.193), channel_id=1, source_target_pairs={{2,0},{4,2},{6,4},{8,6},{10,8},{12,10},{14,12},{16,14},{18,16},{20... | collective-permute-start | bytes 147464 | tf_op jit(solution)/shard_map/ppermute | solution.py:1269
  300.7 8.7 %copy-start.6 = (f32[2,256,768]{2,1,0:T(8,128)S(1)}, f32[2,256,768]{2,1,0:T(8,128)}, u32[]{:S(2)}) copy-start(f32[2,256,768]{2,1,0:T(8,128)} %hidden.1) | copy-start | bytes 4718596
  307.0 16.2 %collective-permute-start.31 = (f32[256,768]{1,0:T(8,128)S(1)}, f32[256,768]{1,0:T(8,128)S(1)}, u32[]{:S(2)}, u32[]{:S(2)}) collective-permute-start(f32[256,768]{1,0:T(8,128)S(1)} %maximum_select_fusion.6), channel_id=1, source_target_pairs={{0,4},{2,6},{4,0},{6,2},{8,12},{10,14},{12,8},{14,10},{16,20},{18,... | collective-permute-start | bytes 2359304 | tf_op jit(solution)/shard_map/ppermute | solution.py:799
  308.4 16.6 %collective-permute-start.30 = (f32[256,768]{1,0:T(8,128)S(1)}, f32[256,768]{1,0:T(8,128)S(1)}, u32[]{:S(2)}, u32[]{:S(2)}) collective-permute-start(f32[256,768]{1,0:T(8,128)S(1)} %maximum_select_fusion.7), channel_id=1, source_target_pairs={{0,2},{2,0},{4,6},{6,4},{8,10},{10,8},{12,14},{14,12},{16,18},{18,... | collective-permute-start | bytes 2359304 | tf_op jit(solution)/shard_map/ppermute | solution.py:799
  325.8 7.9 %copy-start.16 = (f32[512,768]{1,0:T(8,128)}, f32[512,768]{1,0:T(8,128)S(1)}, u32[]{:S(2)}) copy-start(f32[512,768]{1,0:T(8,128)S(1)} %maximum_select_fusion.2) | copy-start | bytes 4718596
  326.9 11.1 %collective-permute-start.32 = (f32[256,768]{1,0:T(8,128)}, f32[256,768]{1,0:T(8,128)}, u32[]{:S(2)}, u32[]{:S(2)}) collective-permute-start(f32[256,768]{1,0:T(8,128)} %get-tuple-element.195.mine), channel_id=1, source_target_pairs={{0,1},{1,0},{2,3},{3,2},{4,5},{5,4},{6,7},{7,6},{8,9},{9,8},{10,11... | collective-permute-start | bytes 2359304 | tf_op jit(solution)/shard_map/ppermute | solution.py:1299
  336.4 2.8 slice-start
  338.0 4.4 %copy-start.1 = (f32[768,768]{1,0:T(8,128)S(1)}, f32[768,768]{1,0:T(8,128)}, u32[]{:S(2)}) copy-start(f32[768,768]{1,0:T(8,128)} %param.20) | copy-start | bytes 7077892
  (17 other events, 21.1 us)
where the time goes:
time: 349 us; the launch traced here: 343 us
  waiting for transfers between devices  96.4 us (28%)
  Pallas kernels  75.2 us (22%)
  starting transfers between devices  74.5 us (21%)
  matrix products  38.8 us (11%)
  other arithmetic  28.5 us (8%)
  local copies, waits for them, and re-layouts  27.6 us (8%)
    ppermute x24, waiting for transfers between devices, exchange(): return lax.ppermute(x, axis, [(i, i ^ 1 << bit) for i in range(peers)])  71 us
    dot_general x13, matrix products, dot(): lax.dot_general(left, right, (((over_left,), (over_right,)), ((), ())), p...  38.8 us
    ppermute x24, starting transfers between devices, exchange(): return lax.ppermute(x, axis, [(i, i ^ 1 << bit) for i in range(peers)])  33.2 us
    all_to_all x4, waiting for transfers between devices, swap_all(): return lax.all_to_all(x, 'seq', 0, 0, tiled=True)  24 us
    all_to_all x4, starting transfers between devices, swap_all(): return lax.all_to_all(x, 'seq', 0, 0, tiled=True)  20.2 us
    pallas_call x1, Pallas kernels, local(): pl.pallas_call(partial(end_kernel, dims), grid=(micro,), in_specs=[smem,...  16.4 us
    pallas_call x1, Pallas kernels, local(): pl.pallas_call(partial(front_kernel, dims), grid=(micro,), in_specs=[smem...  14.3 us
    pallas_call x1, Pallas kernels, local(): pl.pallas_call(partial(inside_back_kernel, dims), grid=(micro,), in_specs...  13.6 us
  transfers between devices with their start and end apart: 37, of which 17 were waited for; matrix products, arithmetic and copies ran while one was open for 23% of the time, Pallas kernels for 13%

commit v1 on v0

--- a/solution.py
+++ b/solution.py
@@ -182,7 +182,7 @@
     first = place[0] * length
     fill_masks(masks, documents, first, ends, EDGE, length, reach_cells)
 
-    gain = prenorm[...]
+    gain = prenorm[...][None]
 
     def norm(x):
         mean = jnp.sum(x * x, axis=1, keepdims=True) / x.shape[1]
@@ -201,7 +201,7 @@
     raw = dot(normed[0, EDGE : EDGE + length], stepper[...])
 
     taps[:offsets_count, :inner] = filters[...]
-    taps[offsets_count:, :inner] = shifts[...]
+    taps[offsets_count:, :inner] = shifts[...][None]
     for k in range(4):
         at = slice(inner + k * state, inner + (k + 1) * state)
         taps[:offsets_count, at] = kernels[:, k, :]
@@ -794,6 +794,16 @@
     prenorm[...] = mine[at + 4] + peer[at + 4]
 
 
+def finish_kernel(bits, own_first, came_first, own_second, came_second, values, last):
+    half = own_first.shape[0]
+    low = bits[0] == 0
+    values[:half] = jnp.where(low, own_first[...], came_first[...])
+    values[half : 2 * half] = jnp.where(low, came_first[...], own_first[...])
+    low = bits[1] == 0
+    values[2 * half :] = jnp.where(low, own_second[...], came_second[...])
+    last[...] = jnp.where(low, came_second[...], own_second[...])
+
+
 def exchange(x, axis, bit):
     peers = lax.axis_size(axis)
     return lax.ppermute(x, axis, [(i, i ^ (1 << bit)) for i in range(peers)])
@@ -985,13 +995,13 @@
             spec(EDGE, model),
             spec(length, model),
             spec(EDGE, model),
-            fixed(1, model),
+            fixed(model),
             fixed(model, inner),
             fixed(model, maps_width),
             fixed(model, both),
             fixed(count, inner),
             fixed(count, 4, state),
-            fixed(1, inner),
+            fixed(inner),
             fixed(4, state),
             fixed(2, heads),
             fixed(2, heads),
@@ -1042,13 +1052,13 @@
         before,
         hidden,
         after,
-        prenorm[None],
+        prenorm,
         values,
         states_flat,
         stepper_flat,
         filters,
         kernels,
-        shifts[None],
+        shifts,
         biases,
         offsets,
         decays,
@@ -1234,6 +1244,7 @@
     grad_raw = grad_raw.reshape(micro * long, both)
     cut = maps_width // 2
     most = (model + cut + cut) // 2
+    assert 3 * (most // 2) == model
     late_total = PairTotal("seq")
     late_total.now = [dot(normed_flat[:, :most], grad_mixed, 0, 0), None]
     grad_normed = (
@@ -1284,7 +1295,7 @@
     result = hidden + (projected + lax.ppermute(projected, "head", swap)).reshape(hidden.shape)
 
     held = second_late
-    for mine in "eelelellellel":
+    for mine in "eelelelelllel":
         total = late_total if mine == "l" else early
         held = total.turn(held)
     while late_total.at < len(late_total.steps) - 1:
@@ -1292,10 +1303,26 @@
         held = early.turn(held)
     while not early.done:
         held = early.turn(held)
-    late_total.take(held, grad_hidden, result)
-    late_done = late_total.now
+    came = tie(*late_total.came, held, grad_hidden, result)[:2]
+    _, order = late_total.steps[late_total.at]
+    quarter = most // 2
+    part = pl.BlockSpec((quarter, WIDE), lambda i: (0, i))
+    late_done, last = pl.pallas_call(
+        finish_kernel,
+        grid=(inner // WIDE,),
+        in_specs=[smem] + [part] * 4,
+        out_specs=[pl.BlockSpec((3 * quarter, WIDE), lambda i: (0, i)), part],
+        out_shape=[shape(3 * quarter, inner), shape(quarter, inner)],
+        compiler_params=PARAMS,
+        name="finish",
+    )(
+        jnp.stack([late_total.mine(bit) for bit in order]).astype(jnp.int32),
+        late_total.now[0],
+        came[0],
+        late_total.now[1],
+        came[1],
+    )
     grad_output, grad_gating = early.now
-    last = late_done[1][model - most :]
     peer_last = lax.ppermute(last, "head", swap)
     own_states, other_states = last[:cut], peer_last[:cut]
     grad_states = jnp.where(
@@ -1332,7 +1359,6 @@
         compiler_params=PARAMS,
         name="unpack",
     )(last, peer_last)
-    late_done = jnp.concatenate([late_done[0], late_done[1][: model - most]], axis=0)
     return (
         result,
         grad_hidden,

time: 349 us -> 344 us (0.986)
  Pallas kernels: 75.2 us -> 79.7 us
  waiting for transfers between devices: 96.4 us -> 92.1 us
  other arithmetic: 28.5 us -> 24.5 us
    ppermute x24, starting transfers between devices: 33.2 us -> 28.6 us  [exchange(): return lax.ppermute(x, axis, [(i, i ^ 1 << bit) for i in range(peers)])]
    pallas_call x0 -> x1, Pallas kernels: none -> 4.48 us  [local(): pl.pallas_call(finish_kernel, grid=(inner // WIDE,), in_specs=[smem] + [p...]
    ppermute x24, waiting for transfers between devices: 71 us -> 66.8 us  [exchange(): return lax.ppermute(x, axis, [(i, i ^ 1 << bit) for i in range(peers)])]
    ppermute x1, starting transfers between devices: 1.67 us -> 5.73 us  [local(): lax.ppermute(projected, 'head', swap)]
    select_n x10 -> x8, other arithmetic: 10.8 us -> 7.75 us  [join_halves(): jnp.where(mine == 0, jnp.concatenate([own, other]), jnp.concatenate([othe...]
    unnamed x88 -> x92, local copies, waits for them, and re-layouts: 10.9 us -> 11.2 us
  transfers between devices with their start and end apart: 37 -> 37, of which waited for: 17 -> 15; matrix products, arithmetic and copies ran while one was open for 23% -> 21% of each run, Pallas kernels for 13% -> 13%
where the time goes in v1:
time: 344 us; the launch traced here: 338 us
  waiting for transfers between devices  92.1 us (27%)
  Pallas kernels  79.7 us (23%)
  starting transfers between devices  77.8 us (23%)
  matrix products  37.4 us (11%)
  local copies, waits for them, and re-layouts  24.9 us (7%)
  other arithmetic  24.5 us (7%)
    ppermute x24, waiting for transfers between devices, exchange(): return lax.ppermute(x, axis, [(i, i ^ 1 << bit) for i in range(peers)])  66.8 us
    dot_general x13, matrix products, dot(): lax.dot_general(left, right, (((over_left,), (over_right,)), ((), ())), p...  37.4 us
    ppermute x24, starting transfers between devices, exchange(): return lax.ppermute(x, axis, [(i, i ^ 1 << bit) for i in range(peers)])  28.6 us
    all_to_all x4, waiting for transfers between devices, swap_all(): return lax.all_to_all(x, 'seq', 0, 0, tiled=True)  23.9 us
    all_to_all x4, starting transfers between devices, swap_all(): return lax.all_to_all(x, 'seq', 0, 0, tiled=True)  20.4 us
    pallas_call x1, Pallas kernels, local(): pl.pallas_call(partial(end_kernel, dims), grid=(micro,), in_specs=[smem,...  16.4 us
    pallas_call x1, Pallas kernels, local(): pl.pallas_call(partial(front_kernel, dims), grid=(micro,), in_specs=[smem...  14.3 us
    pallas_call x1, Pallas kernels, local(): pl.pallas_call(partial(inside_back_kernel, dims), grid=(micro,), in_specs...  13.6 us
  transfers between devices with their start and end apart: 37, of which 15 were waited for; matrix products, arithmetic and copies ran while one was open for 21% of the time, Pallas kernels for 13%

profile of v1, /device:TPU:9, one launch (start us, length us, event | category | flops | bytes accessed | tf_op | source)
XLA Modules:
  0.0 338.2 jit_solution(8642500482201062862)
XLA Ops:
  1.7 3.1 collective-permute-start
  4.8 4.0 %collective-permute-start.1 = (f32[2,8,768]{2,1,0:T(8,128)S(1)}, f32[2,8,768]{2,1,0:T(8,128)S(1)}, u32[]{:S(2)}, u32[]{:S(2)}) collective-permute-start(f32[2,8,768]{2,1,0:T(8,128)S(1)} %get-tuple-element.200), channel_id=1, source_target_pairs={{2,0},{4,2},{6,4},{8,6},{10,8},{12,10},{14,12},{16,14},{18,16},{20... | collective-permute-start | bytes 147464 | tf_op jit(solution)/shard_map/ppermute | solution.py:947
  8.8 2.3 copy.38.states
  12.6 14.3 %front.1 = (f32[2,272,768]{2,1,0:T(8,128)}, f32[2,272,1024]{2,1,0:T(8,128)}, f32[2,256,1024]{2,1,0:T(8,128)}, f32[2,256,1024]{2,1,0:T(8,128)}, f32[2,256,256]{2,...) custom-call(s32[1]{0:T(128)} %bitcast.place, ...), custom_call_target="tpu_custom_call" | custom-call | tf_op jit(solution)/shard_map/front/pallas_call | solution.py:989
  27.0 5.1 %all-to-all-start = ((f32[16,104,128]{2,1,0:T(8,128)}), f32[16,104,128]{2,1,0:T(8,128)S(1)}, u32[]{:S(2)}, u32[]{:S(2)}) async-start(f32[16,104,128]{2,1,0:T(8,128)} %get-tuple-element.92), calls=%async_computation | async-start | bytes 1703936 | tf_op jit(solution)/shard_map/all_to_all | solution.py:1081
  32.0 20.1 %all-to-all-done.terms.keeps = f32[16,104,128]{2,1,0:T(8,128)S(1)} async-done(((f32[16,104,128]{2,1,0:T(8,128)}), f32[16,104,128]{2,1,0:T(8,128)S(1)}, u32[]{:S(2)}, u32[]{:S(2)}) %all-to-all-start) | async-done | bytes 852000 | tf_op jit(solution)/shard_map/all_to_all | solution.py:1081
  53.1 2.4 prefix.2
  55.6 5.1 %all-to-all-start.1 = ((f32[16,96,128]{2,1,0:T(8,128)}), f32[16,96,128]{2,1,0:T(8,128)S(1)}, u32[]{:S(2)}, u32[]{:S(2)}) async-start(f32[16,96,128]{2,1,0:T(8,128)} %prefix.2), calls=%async_computation.1 | async-start | bytes 1572864 | tf_op jit(solution)/shard_map/all_to_all | solution.py:1081
  62.0 5.4 %fusion.back = f32[2,256,768]{2,1,0:T(8,128)} fusion(f32[2,256,768]{2,1,0:T(8,128)} %param.33, f32[768,768]{1,0:T(8,128)} %param.32), kind=kOutput, calls=%fused_computation.2 | convolution fusion | flops 1811939328 | bytes 5505024 | tf_op jit(solution)/shard_map/dot_general | solution.py:22
  67.4 5.9 %inside.1 = f32[2,256,768]{2,1,0:T(8,128)} custom-call(s32[1]{0:T(128)} %bitcast.place, s32[2,8]{1,0:T(2,128)} %lengths.7, f32[2,256,1024]{2,1,0:T(8,128)} %get-tuple-element.89.act, f32[2,256,24]{2,1,0:T(8,128)} %get-tuple-element.90.run, f32[2,24,256]{2,1,0:T(8,128)} %get-tuple-element.91.late_rows), custom_call_target="tpu_custom_call" | custom-call | tf_op jit(solution)/shard_map/inside/pallas_call | solution.py:1089
  73.3 3.4 %fusion.2.gate = f32[2,272,768]{2,1,0:T(8,128)} fusion(f32[2,272,768]{2,1,0:T(8,128)S(1)} %copy-done.2, f32[768,768]{1,0:T(8,128)S(1)} %copy-done), kind=kOutput, calls=%fused_computation.4 | convolution fusion | flops 1925185536 | bytes 5701632 | tf_op jit(solution)/shard_map/dot_general | solution.py:22
  76.7 2.7 all-to-all-done.1.pay
  80.3 5.1 %join.1 = (f32[2,256,768]{2,1,0:T(8,128)}, f32[2,256,128]{2,1,0:T(8,128)}, f32[2,2,64,768]{3,2,1,0:T(8,128)}) custom-call(f32[2,256,768]{2,1,0:T(8,128)} %inside.1, f32[16,96,128]{2,1,0:T(8,128)} %copy-done.28, f32[2,256,1024]{2,1,0:T(8,128)} %get-tuple-element.89.act, f32[2,256,24]{2,1,0:T(8,128)} %get-tuple-element.93.reach, f32[2,272,768]{2,1,0:T(8,128)} %fusion.2.gate, ...), custom_call_target="tpu_custom_call" | custom-call | tf_op jit(solution)/shard_map/join/pallas_call | solution.py:1103
  85.4 2.3 collective-permute-start.2
  89.8 5.0 %turn.1 = (f32[2,256,768]{2,1,0:T(8,128)}, f32[2,256,768]{2,1,0:T(8,128)}, f32[16,96,128]{2,1,0:T(8,128)}) custom-call(f32[2,256,128]{2,1,0:T(8,128)} %get-tuple-element.95.sums, f32[2,256,128]{2,1,0:T(8,128)} %copy-done.36, f32[2,256,768]{2,1,0:T(8,128)} %get-tuple-element.96.mixed_y, f32[2,272,768]{2,1,0:T(8,128)} %fusion.2.gate, ...), custom_call_target="tpu_custom_call" | custom-call | tf_op jit(solution)/shard_map/turn/pallas_call | solution.py:1118
  94.8 4.7 %all-to-all-start.2 = ((f32[16,96,128]{2,1,0:T(8,128)}), f32[16,96,128]{2,1,0:T(8,128)S(1)}, u32[]{:S(2)}, u32[]{:S(2)}) async-start(f32[16,96,128]{2,1,0:T(8,128)} %get-tuple-element.101), calls=%async_computation.2 | async-start | bytes 1572864 | tf_op jit(solution)/shard_map/all_to_all | solution.py:1081
  99.5 5.3 %side.1 = (f32[2,272,768]{2,1,0:T(8,128)}, f32[2,8,768]{2,1,0:T(8,128)}) custom-call(f32[2,256,128]{2,1,0:T(8,128)} %get-tuple-element.95.sums, f32[2,256,128]{2,1,0:T(8,128)} %copy-done.36, f32[2,256,768]{2,1,0:T(8,128)} %get-tuple-element.96.mixed_y, f32[2,272,768]{2,1,0:T(8,128)} %fusion.2.gate, f32[2,256,768]{2,1,0:T(8,128)} %fusion.back, ...), custom_call_target="tpu_custom_call" | custom-call | tf_op jit(solution)/shard_map/side/pallas_call | solution.py:1146
  104.8 5.0 %convolution_bitcast_fusion = f32[768,768]{1,0:T(8,128)S(1)} fusion(f32[2,272,768]{2,1,0:T(8,128)S(1)} %copy-done.3, f32[2,272,768]{2,1,0:T(8,128)} %get-tuple-element.100), kind=kOutput, calls=%fused_computation.6 | convolution fusion | flops 1925185536 | bytes 5701632 | tf_op jit(solution)/shard_map/dot_general | solution.py:22
  112.4 2.4 convolution_bitcast_fusion.1
  119.3 2.4 prefix.3
  121.7 5.6 %all-to-all-start.3 = ((f32[16,96,128]{2,1,0:T(8,128)}), f32[16,96,128]{2,1,0:T(8,128)S(1)}, u32[]{:S(2)}, u32[]{:S(2)}) async-start(f32[16,96,128]{2,1,0:T(8,128)} %prefix.3), calls=%async_computation.3 | async-start | bytes 1572864 | tf_op jit(solution)/shard_map/all_to_all | solution.py:1081
  129.7 4.8 %fusion.16 = f32[544,768]{1,0:T(8,128)} fusion(f32[544,768]{1,0:T(8,128)} %bitcast.62, f32[768,768]{1,0:T(8,128)S(1)} %copy-done), kind=kOutput, calls=%fused_computation.66 | convolution fusion | flops 1925185536 | bytes 5701632 | tf_op jit(solution)/shard_map/dot_general | solution.py:22
  134.5 13.6 %inside_back.1 = (f32[2,256,768]{2,1,0:T(8,128)}, f32[2,256,256]{2,1,0:T(8,128)}, f32[2,256,24]{2,1,0:T(8,128)}, f32[2,256,24]{2,1,0:T(8,128)}) custom-call(s32[1]{0:T(128)} %bitcast.place, s32[2,8]{1,0:T(2,128)} %lengths.7, f32[2,256,1024]{2,1,0:T(8,128)} %get-tuple-element.89.act, f32[2,256,768]{2,1,0:T(8,128)} %get-tuple-element.103.grad_y, ...), custom_call_target="tpu_custom_call" | custom-call | tf_op jit(solution)/shard_map/inside_back/pallas_call | solution.py:1164
  149.0 16.4 %end.1 = (f32[2,272,768]{2,1,0:T(8,128)}, f32[2,272,256]{2,1,0:T(8,128)}, f32[2,272,24]{2,1,0:T(8,128)}, f32[2,16,1024]{2,1,0:T(8,128)}) custom-call(s32[1]{0:T(128)} %bitcast.place, s32[2,8]{1,0:T(2,128)} %lengths.7, f32[16,96,128]{2,1,0:T(8,128)} %copy-done.24, f32[2,256,1024]{2,1,0:T(8,128)} %get-tuple-element.89.act, ...), custom_call_target="tpu_custom_call" | custom-call | tf_op jit(solution)/shard_map/end/pallas_call | solution.py:1183
  167.5 1.6 dynamic-slice_add_fusion
  169.7 2.3 fusion.17
  172.9 2.7 collective-permute-start.7
  175.6 2.4 multiply_reduce_fusion
  178.0 2.3 fusion.5
  186.2 2.1 fusion.7.rest
  188.3 2.6 pack.1
  190.8 2.1 constant_dynamic-slice_fusion.4
  194.1 1.8 collective-permute-done.14
  196.1 2.1 collective-permute-start.15
  198.2 12.9 %collective-permute-done.15 = f32[96,768]{1,0:T(8,128)S(1)} collective-permute-done((f32[96,768]{1,0:T(8,128)S(1)}, f32[96,768]{1,0:T(8,128)S(1)}, u32[]{:S(2)}, u32[]{:S(2)}) %collective-permute-start.15) | collective-permute-done | bytes 294944 | tf_op jit(solution)/shard_map/ppermute | solution.py:809
  211.2 3.2 collective-permute-start.18
  217.9 2.5 collective-permute-start.16
  220.3 4.1 %collective-permute-done.18 = f32[96,768]{1,0:T(8,128)S(1)} collective-permute-done((f32[96,768]{1,0:T(8,128)S(1)}, f32[96,768]{1,0:T(8,128)S(1)}, u32[]{:S(2)}, u32[]{:S(2)}) %collective-permute-start.18) | collective-permute-done | bytes 294944 | tf_op jit(solution)/shard_map/ppermute | solution.py:809
  225.3 1.8 collective-permute-start.20
  227.2 2.3 collective-permute-start.9
  230.4 8.7 %collective-permute-done.20 = f32[192,768]{1,0:T(8,128)} collective-permute-done((f32[192,768]{1,0:T(8,128)}, f32[192,768]{1,0:T(8,128)}, u32[]{:S(2)}, u32[]{:S(2)}) %collective-permute-start.20) | collective-permute-done | bytes 589856 | tf_op jit(solution)/shard_map/ppermute | solution.py:809
  239.1 2.3 broadcast_select_fusion
  241.4 1.9 collective-permute-start.22
  243.5 3.6 %fusion.20 = f32[512,768]{1,0:T(8,128)} fusion(f32[512,768]{1,0:T(8,128)S(1)} %bitcast.63, f32[768,768]{1,0:T(8,128)S(1)} %copy-done.15), kind=kOutput, calls=%fused_computation.70 | convolution fusion | flops 1811939328 | bytes 5505024 | tf_op jit(solution)/shard_map/dot_general | solution.py:22
  247.1 5.7 %collective-permute-start.8 = (f32[512,768]{1,0:T(8,128)}, f32[512,768]{1,0:T(8,128)S(1)}, u32[]{:S(2)}, u32[]{:S(2)}) collective-permute-start(f32[512,768]{1,0:T(8,128)} %fusion.20), channel_id=1, source_target_pairs={{0,1},{1,0},{2,3},{3,2},{4,5},{5,4},{6,7},{7,6},{8,9},{9,8},{10,11... | collective-permute-start | bytes 4718600 | tf_op jit(solution)/shard_map/ppermute | solution.py:1295
  254.4 1.8 maximum_select_fusion.2
  256.3 6.9 %collective-permute-done.21 = f32[64,768]{1,0:T(8,128)S(1)} collective-permute-done((f32[64,768]{1,0:T(8,128)S(1)}, f32[64,768]{1,0:T(8,128)S(1)}, u32[]{:S(2)}, u32[]{:S(2)}) %collective-permute-start.21) | collective-permute-done | bytes 196640 | tf_op jit(solution)/shard_map/ppermute | solution.py:809
  263.2 3.2 collective-permute-start.24
  266.4 1.7 maximum_select_fusion.3
  269.6 5.3 %collective-permute-done.24 = f32[64,768]{1,0:T(8,128)S(1)} collective-permute-done((f32[64,768]{1,0:T(8,128)S(1)}, f32[64,768]{1,0:T(8,128)S(1)}, u32[]{:S(2)}, u32[]{:S(2)}) %collective-permute-start.24) | collective-permute-done | bytes 196640 | tf_op jit(solution)/shard_map/ppermute | solution.py:809
  274.9 2.3 collective-permute-start.25
  279.5 2.1 add.164
  281.7 4.6 %collective-permute-done.25 = f32[128,768]{1,0:T(8,128)S(1)} collective-permute-done((f32[128,768]{1,0:T(8,128)S(1)}, f32[128,768]{1,0:T(8,128)S(1)}, u32[]{:S(2)}, u32[]{:S(2)}) %collective-permute-start.25) | collective-permute-done | bytes 393248 | tf_op jit(solution)/shard_map/ppermute | solution.py:809
  287.8 2.1 collective-permute-start.10
  289.9 5.4 %collective-permute-done.29 = f32[384,768]{1,0:T(8,128)S(1)} collective-permute-done((f32[384,768]{1,0:T(8,128)S(1)}, f32[384,768]{1,0:T(8,128)S(1)}, u32[]{:S(2)}, u32[]{:S(2)}) %collective-permute-start.29) | collective-permute-done | bytes 1179680 | tf_op jit(solution)/shard_map/ppermute | solution.py:809
  295.4 2.8 collective-permute-start.11
  298.2 1.6 maximum_select_fusion
  299.8 4.5 %collective-permute-done.26 = f32[128,768]{1,0:T(8,128)S(1)} collective-permute-done((f32[128,768]{1,0:T(8,128)S(1)}, f32[128,768]{1,0:T(8,128)S(1)}, u32[]{:S(2)}, u32[]{:S(2)}) %collective-permute-start.26) | collective-permute-done | bytes 393248 | tf_op jit(solution)/shard_map/ppermute | solution.py:809
  307.4 2.2 multiply_subtract_fusion
  309.6 11.9 %collective-permute-done.31.came_second = f32[256,768]{1,0:T(8,128)S(1)} collective-permute-done((f32[256,768]{1,0:T(8,128)S(1)}, f32[256,768]{1,0:T(8,128)S(1)}, u32[]{:S(2)}, u32[]{:S(2)}) %collective-permute-start.31) | collective-permute-done | bytes 786464 | tf_op jit(solution)/shard_map/ppermute | solution.py:809
  322.8 4.5 %finish.1 = (f32[768,768]{1,0:T(8,128)}, f32[256,768]{1,0:T(8,128)}) custom-call(s32[2]{0:T(128)} %pad_add_fusion.bits, f32[256,768]{1,0:T(8,128)} %copy-done.27, f32[256,768]{1,0:T(8,128)} %copy-done.38, f32[256,768]{1,0:T(8,128)} %copy-done.26, f32[256,768]{1,0:T(8,128)} %copy-done.37), custom_call_target="tpu_custom_call" | custom-call | tf_op jit(solution)/shard_map/finish/pallas_call | solution.py:1310
  327.3 3.8 %collective-permute-start.32 = (f32[256,768]{1,0:T(8,128)}, f32[256,768]{1,0:T(8,128)}, u32[]{:S(2)}, u32[]{:S(2)}) collective-permute-start(f32[256,768]{1,0:T(8,128)} %get-tuple-element.150.mine), channel_id=1, source_target_pairs={{0,1},{1,0},{2,3},{3,2},{4,5},{5,4},{6,7},{7,6},{8,9},{9,8},{10,11... | collective-permute-start | bytes 2359304 | tf_op jit(solution)/shard_map/ppermute | solution.py:1326
  331.1 1.6 maximum_select_fusion.1
  335.6 2.2 unpack.1
  (180 shorter events, 48.3 us)
Async XLA Ops:
  0.6 72.6 %copy-start = (f32[768,768]{1,0:T(8,128)S(1)}, f32[768,768]{1,0:T(8,128)}, u32[]{:S(2)}) copy-start(f32[768,768]{1,0:T(8,128)} %param.20) | copy-start | bytes 7077892
  0.7 10.4 %copy-start.39 = (f32[768,2,12]{0,1,2:T(2,128)S(1)}, f32[768,2,12]{0,1,2:T(2,128)}, u32[]{:S(2)}) copy-start(f32[768,2,12]{0,1,2:T(2,128)} %param.23) | copy-start | bytes 221188
  1.7 10.3 %collective-permute-start = (f32[2,8,768]{2,1,0:T(8,128)S(1)}, f32[2,8,768]{2,1,0:T(8,128)S(1)}, u32[]{:S(2)}, u32[]{:S(2)}) collective-permute-start(f32[2,8,768]{2,1,0:T(8,128)S(1)} %get-tuple-element.201), channel_id=1, source_target_pairs={{0,2},{2,4},{4,6},{6,8},{8,10},{10,12},{12,14},{14,16},{16,18},{18... | collective-permute-start | bytes 147464 | tf_op jit(solution)/shard_map/ppermute | solution.py:946
  4.8 7.2 %collective-permute-start.1 = (f32[2,8,768]{2,1,0:T(8,128)S(1)}, f32[2,8,768]{2,1,0:T(8,128)S(1)}, u32[]{:S(2)}, u32[]{:S(2)}) collective-permute-start(f32[2,8,768]{2,1,0:T(8,128)S(1)} %get-tuple-element.200), channel_id=1, source_target_pairs={{2,0},{4,2},{6,4},{8,6},{10,8},{12,10},{14,12},{16,14},{18,16},{20... | collective-permute-start | bytes 147464 | tf_op jit(solution)/shard_map/ppermute | solution.py:947
  27.0 25.2 %all-to-all-start = ((f32[16,104,128]{2,1,0:T(8,128)}), f32[16,104,128]{2,1,0:T(8,128)S(1)}, u32[]{:S(2)}, u32[]{:S(2)}) async-start(f32[16,104,128]{2,1,0:T(8,128)} %get-tuple-element.92), calls=%async_computation | async-start | bytes 1703936 | tf_op jit(solution)/shard_map/all_to_all | solution.py:1081
  53.1 7.5 %copy-start.43 = (f32[768]{0:T(1024)S(1)}, f32[768]{0:T(1024)}, u32[]{:S(2)}) copy-start(f32[768]{0:T(1024)} %param.31) | copy-start | bytes 9220
  53.1 8.1 %copy-start.44 = (f32[12]{0:T(128)S(1)}, f32[12]{0:T(128)}, u32[]{:S(2)}) copy-start(f32[12]{0:T(128)} %param.30) | copy-start | bytes 148
  55.6 23.9 %all-to-all-start.1 = ((f32[16,96,128]{2,1,0:T(8,128)}), f32[16,96,128]{2,1,0:T(8,128)S(1)}, u32[]{:S(2)}, u32[]{:S(2)}) async-start(f32[16,96,128]{2,1,0:T(8,128)} %prefix.2), calls=%async_computation.1 | async-start | bytes 1572864 | tf_op jit(solution)/shard_map/all_to_all | solution.py:1081
  67.4 5.9 %copy-start.2 = (f32[2,272,768]{2,1,0:T(8,128)S(1)}, f32[2,272,768]{2,1,0:T(8,128)}, u32[]{:S(2)}) copy-start(f32[2,272,768]{2,1,0:T(8,128)} %get-tuple-element.94) | copy-start | bytes 5013508
  85.4 3.7 %collective-permute-start.2 = (f32[2,256,128]{2,1,0:T(8,128)}, f32[2,256,128]{2,1,0:T(8,128)S(1)}, u32[]{:S(2)}, u32[]{:S(2)}) collective-permute-start(f32[2,256,128]{2,1,0:T(8,128)} %get-tuple-element.95.sums), channel_id=1, source_target_pairs={{0,1},{1,0},{2,3},{3,2},{4,5},{5,4},{6,7},{7,6},{8,9},{9,8},{10,11... | collective-permute-start | bytes 786440 | tf_op jit(solution)/shard_map/ppermute | solution.py:1116
  94.8 23.6 %all-to-all-start.2 = ((f32[16,96,128]{2,1,0:T(8,128)}), f32[16,96,128]{2,1,0:T(8,128)S(1)}, u32[]{:S(2)}, u32[]{:S(2)}) async-start(f32[16,96,128]{2,1,0:T(8,128)} %get-tuple-element.101), calls=%async_computation.2 | async-start | bytes 1572864 | tf_op jit(solution)/shard_map/all_to_all | solution.py:1081
  99.5 5.3 %copy-start.3 = (f32[2,272,768]{2,1,0:T(8,128)S(1)}, f32[2,272,768]{2,1,0:T(8,128)}, u32[]{:S(2)}) copy-start(f32[2,272,768]{2,1,0:T(8,128)} %get-tuple-element.94) | copy-start | bytes 5013508
  104.8 6.8 %copy-start.19 = (f32[2,256,768]{2,1,0:T(8,128)S(1)}, f32[2,256,768]{2,1,0:T(8,128)}, u32[]{:S(2)}) copy-start(f32[2,256,768]{2,1,0:T(8,128)} %get-tuple-element.98) | copy-start | bytes 4718596
  109.8 2.6 copy-start.7
  121.7 26.4 %all-to-all-start.3 = ((f32[16,96,128]{2,1,0:T(8,128)}), f32[16,96,128]{2,1,0:T(8,128)S(1)}, u32[]{:S(2)}, u32[]{:S(2)}) async-start(f32[16,96,128]{2,1,0:T(8,128)} %prefix.3), calls=%async_computation.3 | async-start | bytes 1572864 | tf_op jit(solution)/shard_map/all_to_all | solution.py:1081
  127.3 38.1 %collective-permute-start.4 = (f32[384,768]{1,0:T(8,128)}, f32[384,768]{1,0:T(8,128)}, u32[]{:S(2)}, u32[]{:S(2)}) collective-permute-start(f32[384,768]{1,0:T(8,128)} %constant_dynamic-slice_fusion.8), channel_id=1, source_target_pairs={{0,4},{2,6},{4,0},{6,2},{8,12},{10,14},{12,8},{14,10},{16,20},{18,... | collective-permute-start | bytes 3538952 | tf_op jit(solution)/shard_map/ppermute | solution.py:809
  128.5 36.9 %collective-permute-start.3 = (f32[384,768]{1,0:T(8,128)}, f32[384,768]{1,0:T(8,128)}, u32[]{:S(2)}, u32[]{:S(2)}) collective-permute-start(f32[384,768]{1,0:T(8,128)} %constant_dynamic-slice_fusion.9), channel_id=1, source_target_pairs={{0,2},{2,0},{4,6},{6,4},{8,10},{10,8},{12,14},{14,12},{16,18},{18,... | collective-permute-start | bytes 3538952 | tf_op jit(solution)/shard_map/ppermute | solution.py:809
  149.0 16.4 %copy-start.14 = (f32[768,768]{1,0:T(8,128)S(1)}, f32[768,768]{1,0:T(8,128)}, u32[]{:S(2)}) copy-start(f32[768,768]{1,0:T(8,128)} %copy-done.13) | copy-start | bytes 7077892
  167.1 2.4 copy-start.5
  167.1 2.6 copy-start.10
  167.1 15.7 %collective-permute-start.6 = (f32[192,768]{1,0:T(8,128)S(1)}, f32[192,768]{1,0:T(8,128)S(1)}, u32[]{:S(2)}, u32[]{:S(2)}) collective-permute-start(f32[192,768]{1,0:T(8,128)S(1)} %constant_dynamic-slice_fusion.6), channel_id=1, source_target_pairs={{0,2},{2,0},{4,6},{6,4},{8,10},{10,8},{12,14},{14,12},{16,18},{18,... | collective-permute-start | bytes 1769480 | tf_op jit(solution)/shard_map/ppermute | solution.py:809
  169.1 13.7 %collective-permute-start.5 = (f32[192,768]{1,0:T(8,128)S(1)}, f32[192,768]{1,0:T(8,128)S(1)}, u32[]{:S(2)}, u32[]{:S(2)}) collective-permute-start(f32[192,768]{1,0:T(8,128)S(1)} %constant_dynamic-slice_fusion.7), channel_id=1, source_target_pairs={{0,4},{2,6},{4,0},{6,2},{8,12},{10,14},{12,8},{14,10},{16,20},{18,... | collective-permute-start | bytes 1769480 | tf_op jit(solution)/shard_map/ppermute | solution.py:809
  169.7 3.2 copy-start.32
  169.7 5.9 %copy-start.16 = (f32[544,768]{1,0:T(8,128)S(1)}, f32[544,768]{1,0:T(8,128)}, u32[]{:S(2)}) copy-start(f32[544,768]{1,0:T(8,128)} %fusion.16) | copy-start | bytes 5013508
  169.7 5.9 %copy-start.23 = (f32[768,4,64]{0,2,1:T(8,128)S(1)}, f32[768,4,64]{0,2,1:T(8,128)}, u32[]{:S(2)}) copy-start(f32[768,4,64]{0,2,1:T(8,128)} %param.22) | copy-start | bytes 2359300
  172.0 3.6 %copy-start.4 = (f32[2,272,768]{2,1,0:T(8,128)S(1)}, f32[2,272,768]{2,1,0:T(8,128)}, u32[]{:S(2)}) copy-start(f32[2,272,768]{2,1,0:T(8,128)} %get-tuple-element.94) | copy-start | bytes 5013508
  172.9 10.5 %collective-permute-start.7 = (f32[544,256]{1,0:T(8,128)S(1)}, f32[544,256]{1,0:T(8,128)S(1)}, u32[]{:S(2)}, u32[]{:S(2)}) collective-permute-start(f32[544,256]{1,0:T(8,128)S(1)} %bitcast.67), channel_id=1, source_target_pairs={{0,1},{1,0},{2,3},{3,2},{4,5},{5,4},{6,7},{7,6},{8,9},{9,8},{10,11... | collective-permute-start | bytes 1671176 | tf_op jit(solution)/shard_map/ppermute | solution.py:1238
  178.0 2.4 copy-start.40
  180.3 2.6 copy-start.17
  181.9 32.4 %collective-permute-start.12 = (f32[256,768]{1,0:T(8,128)}, f32[256,768]{1,0:T(8,128)}, u32[]{:S(2)}, u32[]{:S(2)}) collective-permute-start(f32[256,768]{1,0:T(8,128)} %constant_dynamic-slice_fusion.5), channel_id=1, source_target_pairs={{0,2},{2,0},{4,6},{6,4},{8,10},{10,8},{12,14},{14,12},{16,18},{18,... | collective-permute-start | bytes 2359304 | tf_op jit(solution)/shard_map/ppermute | solution.py:809
  183.0 12.9 %collective-permute-start.14 = (f32[192,768]{1,0:T(8,128)S(1)}, f32[192,768]{1,0:T(8,128)S(1)}, u32[]{:S(2)}, u32[]{:S(2)}) collective-permute-start(f32[192,768]{1,0:T(8,128)S(1)} %broadcast_select_fusion.2), channel_id=1, source_target_pairs={{0,8},{2,10},{4,12},{6,14},{8,0},{10,2},{12,4},{14,6},{16,24},{18,... | collective-permute-start | bytes 1769480 | tf_op jit(solution)/shard_map/ppermute | solution.py:809
  192.9 21.4 %collective-permute-start.13 = (f32[256,768]{1,0:T(8,128)}, f32[256,768]{1,0:T(8,128)}, u32[]{:S(2)}, u32[]{:S(2)}) collective-permute-start(f32[256,768]{1,0:T(8,128)} %constant_dynamic-slice_fusion.4), channel_id=1, source_target_pairs={{0,4},{2,6},{4,0},{6,2},{8,12},{10,14},{12,8},{14,10},{16,20},{18,... | collective-permute-start | bytes 2359304 | tf_op jit(solution)/shard_map/ppermute | solution.py:809
  196.1 15.1 %collective-permute-start.15 = (f32[96,768]{1,0:T(8,128)S(1)}, f32[96,768]{1,0:T(8,128)S(1)}, u32[]{:S(2)}, u32[]{:S(2)}) collective-permute-start(f32[96,768]{1,0:T(8,128)S(1)} %constant_dynamic-slice_fusion.3), channel_id=1, source_target_pairs={{0,16},{2,18},{4,20},{6,22},{8,24},{10,26},{12,28},{14,30},{16,0},... | collective-permute-start | bytes 884744 | tf_op jit(solution)/shard_map/ppermute | solution.py:809
  211.2 5.4 %copy-start.18 = (f32[512,768]{1,0:T(8,128)S(1)}, f32[512,768]{1,0:T(8,128)}, u32[]{:S(2)}) copy-start(f32[512,768]{1,0:T(8,128)} %copy-done.17) | copy-start | bytes 4718596
  211.2 13.3 %collective-permute-start.18 = (f32[96,768]{1,0:T(8,128)S(1)}, f32[96,768]{1,0:T(8,128)S(1)}, u32[]{:S(2)}, u32[]{:S(2)}) collective-permute-start(f32[96,768]{1,0:T(8,128)S(1)} %dynamic-slice_add_fusion.8), channel_id=1, source_target_pairs={{0,16},{2,18},{4,20},{6,22},{8,24},{10,26},{12,28},{14,30},{16,0},... | collective-permute-start | bytes 884744 | tf_op jit(solution)/shard_map/ppermute | solution.py:809
  216.6 12.9 %collective-permute-start.17 = (f32[128,768]{1,0:T(8,128)}, f32[128,768]{1,0:T(8,128)S(1)}, u32[]{:S(2)}, u32[]{:S(2)}) collective-permute-start(f32[128,768]{1,0:T(8,128)} %constant_dynamic-slice_fusion.1), channel_id=1, source_target_pairs={{0,2},{2,0},{4,6},{6,4},{8,10},{10,8},{12,14},{14,12},{16,18},{18,... | collective-permute-start | bytes 1179656 | tf_op jit(solution)/shard_map/ppermute | solution.py:809
  217.8 11.7 %copy-start.21 = (f32[256,768]{1,0:T(8,128)}, f32[256,768]{1,0:T(8,128)S(1)}, u32[]{:S(2)}) copy-start(f32[256,768]{1,0:T(8,128)S(1)} %dynamic-slice_add_fusion.3) | copy-start | bytes 2359300
  217.9 11.6 %collective-permute-start.16 = (f32[128,768]{1,0:T(8,128)S(1)}, f32[128,768]{1,0:T(8,128)S(1)}, u32[]{:S(2)}, u32[]{:S(2)}) collective-permute-start(f32[128,768]{1,0:T(8,128)S(1)} %constant_dynamic-slice_fusion.2), channel_id=1, source_target_pairs={{0,4},{2,6},{4,0},{6,2},{8,12},{10,14},{12,8},{14,10},{16,20},{18,... | collective-permute-start | bytes 1179656 | tf_op jit(solution)/shard_map/ppermute | solution.py:809
  225.3 13.8 %collective-permute-start.20 = (f32[192,768]{1,0:T(8,128)}, f32[192,768]{1,0:T(8,128)}, u32[]{:S(2)}, u32[]{:S(2)}) collective-permute-start(f32[192,768]{1,0:T(8,128)} %maximum_select_fusion.7), channel_id=1, source_target_pairs={{0,8},{2,10},{4,12},{6,14},{8,0},{10,2},{12,4},{14,6},{16,24},{18,... | collective-permute-start | bytes 1769480 | tf_op jit(solution)/shard_map/ppermute | solution.py:809
  227.2 52.4 %collective-permute-start.9 = (f32[2,272,768]{2,1,0:T(8,128)}, f32[2,272,768]{2,1,0:T(8,128)}, u32[]{:S(2)}, u32[]{:S(2)}) collective-permute-start(f32[2,272,768]{2,1,0:T(8,128)} %bitcast.15), channel_id=1, source_target_pairs={{0,1},{1,0},{2,3},{3,2},{4,5},{5,4},{6,7},{7,6},{8,9},{9,8},{10,11... | collective-permute-start | bytes 5013512 | tf_op jit(solution)/shard_map/ppermute | solution.py:1279
  230.2 13.3 %copy-start.20 = (f32[2,256,768]{2,1,0:T(8,128)S(1)}, f32[2,256,768]{2,1,0:T(8,128)}, u32[]{:S(2)}) copy-start(f32[2,256,768]{2,1,0:T(8,128)} %get-tuple-element.98) | copy-start | bytes 4718596
  230.3 13.2 %copy-start.15 = (f32[768,768]{1,0:T(8,128)S(1)}, f32[768,768]{1,0:T(8,128)}, u32[]{:S(2)}) copy-start(f32[768,768]{1,0:T(8,128)} %param.32) | copy-start | bytes 7077892
  230.3 22.5 %collective-permute-start.19 = (f32[128,768]{1,0:T(8,128)S(1)}, f32[128,768]{1,0:T(8,128)S(1)}, u32[]{:S(2)}, u32[]{:S(2)}) collective-permute-start(f32[128,768]{1,0:T(8,128)S(1)} %broadcast_select_fusion.5), channel_id=1, source_target_pairs={{0,8},{2,10},{4,12},{6,14},{8,0},{10,2},{12,4},{14,6},{16,24},{18,... | collective-permute-start | bytes 1179656 | tf_op jit(solution)/shard_map/ppermute | solution.py:809
  241.4 13.0 %collective-permute-start.22 = (f32[192,768]{1,0:T(8,128)}, f32[192,768]{1,0:T(8,128)}, u32[]{:S(2)}, u32[]{:S(2)}) collective-permute-start(f32[192,768]{1,0:T(8,128)} %get-tuple-element.203), channel_id=1, source_target_pairs={{0,4},{2,6},{4,0},{6,2},{8,12},{10,14},{12,8},{14,10},{16,20},{18,... | collective-permute-start | bytes 1769480 | tf_op jit(solution)/shard_map/ppermute | solution.py:809
  243.3 9.5 %copy-start.22 = (f32[256,768]{1,0:T(8,128)S(1)}, f32[256,768]{1,0:T(8,128)}, u32[]{:S(2)}) copy-start(f32[256,768]{1,0:T(8,128)} %copy-done.21) | copy-start | bytes 2359300
  243.3 9.5 %copy-start.31 = (f32[128,768]{1,0:T(8,128)S(1)}, f32[128,768]{1,0:T(8,128)}, u32[]{:S(2)}) copy-start(f32[128,768]{1,0:T(8,128)} %copy-done.30) | copy-start | bytes 1179652
  243.3 11.1 %collective-permute-start.23 = (f32[192,768]{1,0:T(8,128)}, f32[192,768]{1,0:T(8,128)}, u32[]{:S(2)}, u32[]{:S(2)}) collective-permute-start(f32[192,768]{1,0:T(8,128)} %get-tuple-element.202), channel_id=1, source_target_pairs={{0,2},{2,0},{4,6},{6,4},{8,10},{10,8},{12,14},{14,12},{16,18},{18,... | collective-permute-start | bytes 1769480 | tf_op jit(solution)/shard_map/ppermute | solution.py:809
  247.1 30.9 %collective-permute-start.8 = (f32[512,768]{1,0:T(8,128)}, f32[512,768]{1,0:T(8,128)S(1)}, u32[]{:S(2)}, u32[]{:S(2)}) collective-permute-start(f32[512,768]{1,0:T(8,128)} %fusion.20), channel_id=1, source_target_pairs={{0,1},{1,0},{2,3},{3,2},{4,5},{5,4},{6,7},{7,6},{8,9},{9,8},{10,11... | collective-permute-start | bytes 4718600 | tf_op jit(solution)/shard_map/ppermute | solution.py:1295
  253.0 10.2 %collective-permute-start.21 = (f32[64,768]{1,0:T(8,128)S(1)}, f32[64,768]{1,0:T(8,128)S(1)}, u32[]{:S(2)}, u32[]{:S(2)}) collective-permute-start(f32[64,768]{1,0:T(8,128)S(1)} %constant_dynamic-slice_fusion), channel_id=1, source_target_pairs={{0,16},{2,18},{4,20},{6,22},{8,24},{10,26},{12,28},{14,30},{16,0},... | collective-permute-start | bytes 589832 | tf_op jit(solution)/shard_map/ppermute | solution.py:809
  263.2 11.7 %collective-permute-start.24 = (f32[64,768]{1,0:T(8,128)S(1)}, f32[64,768]{1,0:T(8,128)S(1)}, u32[]{:S(2)}, u32[]{:S(2)}) collective-permute-start(f32[64,768]{1,0:T(8,128)S(1)} %dynamic-slice_add_fusion.11), channel_id=1, source_target_pairs={{0,16},{2,18},{4,20},{6,22},{8,24},{10,26},{12,28},{14,30},{16,0},... | collective-permute-start | bytes 589832 | tf_op jit(solution)/shard_map/ppermute | solution.py:809
  268.1 27.2 %collective-permute-start.29 = (f32[384,768]{1,0:T(8,128)S(1)}, f32[384,768]{1,0:T(8,128)S(1)}, u32[]{:S(2)}, u32[]{:S(2)}) collective-permute-start(f32[384,768]{1,0:T(8,128)S(1)} %maximum_select_fusion.3), channel_id=1, source_target_pairs={{0,4},{2,6},{4,0},{6,2},{8,12},{10,14},{12,8},{14,10},{16,20},{18,... | collective-permute-start | bytes 3538952 | tf_op jit(solution)/shard_map/ppermute | solution.py:809
  268.2 29.9 %collective-permute-start.28 = (f32[384,768]{1,0:T(8,128)S(1)}, f32[384,768]{1,0:T(8,128)S(1)}, u32[]{:S(2)}, u32[]{:S(2)}) collective-permute-start(f32[384,768]{1,0:T(8,128)S(1)} %maximum_select_fusion.2), channel_id=1, source_target_pairs={{0,2},{2,0},{4,6},{6,4},{8,10},{10,8},{12,14},{14,12},{16,18},{18,... | collective-permute-start | bytes 3538952 | tf_op jit(solution)/shard_map/ppermute | solution.py:809
  274.9 11.4 %collective-permute-start.25 = (f32[128,768]{1,0:T(8,128)S(1)}, f32[128,768]{1,0:T(8,128)S(1)}, u32[]{:S(2)}, u32[]{:S(2)}) collective-permute-start(f32[128,768]{1,0:T(8,128)S(1)} %maximum_select_fusion.8), channel_id=1, source_target_pairs={{0,8},{2,10},{4,12},{6,14},{8,0},{10,2},{12,4},{14,6},{16,24},{18,... | collective-permute-start | bytes 1179656 | tf_op jit(solution)/shard_map/ppermute | solution.py:809
  286.4 17.9 %collective-permute-start.26 = (f32[128,768]{1,0:T(8,128)S(1)}, f32[128,768]{1,0:T(8,128)S(1)}, u32[]{:S(2)}, u32[]{:S(2)}) collective-permute-start(f32[128,768]{1,0:T(8,128)S(1)} %get-tuple-element.205), channel_id=1, source_target_pairs={{0,4},{2,6},{4,0},{6,2},{8,12},{10,14},{12,8},{14,10},{16,20},{18,... | collective-permute-start | bytes 1179656 | tf_op jit(solution)/shard_map/ppermute | solution.py:809
  286.5 17.9 %collective-permute-start.27 = (f32[128,768]{1,0:T(8,128)S(1)}, f32[128,768]{1,0:T(8,128)S(1)}, u32[]{:S(2)}, u32[]{:S(2)}) collective-permute-start(f32[128,768]{1,0:T(8,128)S(1)} %get-tuple-element.204), channel_id=1, source_target_pairs={{0,2},{2,0},{4,6},{6,4},{8,10},{10,8},{12,14},{14,12},{16,18},{18,... | collective-permute-start | bytes 1179656 | tf_op jit(solution)/shard_map/ppermute | solution.py:809
  287.8 18.2 %collective-permute-start.10 = (f32[2,8,768]{2,1,0:T(8,128)S(1)}, f32[2,8,768]{2,1,0:T(8,128)S(1)}, u32[]{:S(2)}, u32[]{:S(2)}) collective-permute-start(f32[2,8,768]{2,1,0:T(8,128)S(1)} %get-tuple-element.196), channel_id=1, source_target_pairs={{0,2},{2,4},{4,6},{6,8},{8,10},{10,12},{12,14},{14,16},{16,18},{18... | collective-permute-start | bytes 147464 | tf_op jit(solution)/shard_map/ppermute | solution.py:1281
  295.4 2.8 copy-start.33
  295.4 10.7 %collective-permute-start.11 = (f32[2,8,768]{2,1,0:T(8,128)S(1)}, f32[2,8,768]{2,1,0:T(8,128)S(1)}, u32[]{:S(2)}, u32[]{:S(2)}) collective-permute-start(f32[2,8,768]{2,1,0:T(8,128)S(1)} %get-tuple-element.197), channel_id=1, source_target_pairs={{2,0},{4,2},{6,4},{8,6},{10,8},{12,10},{14,12},{16,14},{18,16},{20... | collective-permute-start | bytes 147464 | tf_op jit(solution)/shard_map/ppermute | solution.py:1280
  299.8 6.2 %copy-start.6 = (f32[2,256,768]{2,1,0:T(8,128)S(1)}, f32[2,256,768]{2,1,0:T(8,128)}, u32[]{:S(2)}) copy-start(f32[2,256,768]{2,1,0:T(8,128)} %hidden.1) | copy-start | bytes 4718596
  304.4 17.1 %collective-permute-start.31 = (f32[256,768]{1,0:T(8,128)S(1)}, f32[256,768]{1,0:T(8,128)S(1)}, u32[]{:S(2)}, u32[]{:S(2)}) collective-permute-start(f32[256,768]{1,0:T(8,128)S(1)} %maximum_select_fusion.5.own_second), channel_id=1, source_target_pairs={{0,4},{2,6},{4,0},{6,2},{8,12},{10,14},{12,8},{14,10},{16,20},{18,... | collective-permute-start | bytes 2359304 | tf_op jit(solution)/shard_map/ppermute | solution.py:809
  305.7 16.2 %collective-permute-start.30 = (f32[256,768]{1,0:T(8,128)S(1)}, f32[256,768]{1,0:T(8,128)S(1)}, u32[]{:S(2)}, u32[]{:S(2)}) collective-permute-start(f32[256,768]{1,0:T(8,128)S(1)} %maximum_select_fusion.4.own_first), channel_id=1, source_target_pairs={{0,2},{2,0},{4,6},{6,4},{8,10},{10,8},{12,14},{14,12},{16,18},{18,... | collective-permute-start | bytes 2359304 | tf_op jit(solution)/shard_map/ppermute | solution.py:809
  322.8 8.3 %copy-start.34 = (f32[384,768]{1,0:T(8,128)S(1)}, f32[384,768]{1,0:T(8,128)}, u32[]{:S(2)}) copy-start(f32[384,768]{1,0:T(8,128)} %copy-done.33) | copy-start | bytes 3538948
  327.3 6.2 %collective-permute-start.32 = (f32[256,768]{1,0:T(8,128)}, f32[256,768]{1,0:T(8,128)}, u32[]{:S(2)}, u32[]{:S(2)}) collective-permute-start(f32[256,768]{1,0:T(8,128)} %get-tuple-element.150.mine), channel_id=1, source_target_pairs={{0,1},{1,0},{2,3},{3,2},{4,5},{5,4},{6,7},{7,6},{8,9},{9,8},{10,11... | collective-permute-start | bytes 2359304 | tf_op jit(solution)/shard_map/ppermute | solution.py:1326
  333.5 4.3 %copy-start.1 = (f32[768,768]{1,0:T(8,128)S(1)}, f32[768,768]{1,0:T(8,128)}, u32[]{:S(2)}) copy-start(f32[768,768]{1,0:T(8,128)} %param.20) | copy-start | bytes 7077892
  (18 other events, 21.9 us)

commit v2 on v1

--- a/solution.py
+++ b/solution.py
@@ -15,7 +15,7 @@
 WIDE = 256
 CHUNK = 128
 EDGE = 8
-PARAMS = pltpu.CompilerParams(vmem_limit_bytes=56 * 1024 * 1024)
+PARAMS = pltpu.CompilerParams(vmem_limit_bytes=53 * 1024 * 1024)
 
 
 def dot(left, right, over_left=1, over_right=0, precision=HIGH):

time: 344 us -> 341 us (level)
  local copies, waits for them, and re-layouts: 24.9 us -> 20.3 us
    unnamed x92 -> x124, local copies, waits for them, and re-layouts: 11.2 us -> 8.36 us
where the time goes in v2:
time: 341 us; the launch traced here: 335 us
  waiting for transfers between devices  94.2 us (28%)
  starting transfers between devices  77.7 us (23%)
  Pallas kernels  77.1 us (23%)
  matrix products  36 us (11%)
  other arithmetic  27.4 us (8%)
  local copies, waits for them, and re-layouts  20.3 us (6%)
    ppermute x24, waiting for transfers between devices, exchange(): return lax.ppermute(x, axis, [(i, i ^ 1 << bit) for i in range(peers)])  67.3 us
    dot_general x13, matrix products, dot(): lax.dot_general(left, right, (((over_left,), (over_right,)), ((), ())), p...  36 us
    ppermute x24, starting transfers between devices, exchange(): return lax.ppermute(x, axis, [(i, i ^ 1 << bit) for i in range(peers)])  28.5 us
    all_to_all x4, waiting for transfers between devices, swap_all(): return lax.all_to_all(x, 'seq', 0, 0, tiled=True)  25.7 us
    all_to_all x4, starting transfers between devices, swap_all(): return lax.all_to_all(x, 'seq', 0, 0, tiled=True)  20.1 us
    pallas_call x1, Pallas kernels, local(): pl.pallas_call(partial(end_kernel, dims), grid=(micro,), in_specs=[smem,...  15.7 us
    pallas_call x1, Pallas kernels, local(): pl.pallas_call(partial(front_kernel, dims), grid=(micro,), in_specs=[smem...  13.9 us
    pallas_call x1, Pallas kernels, local(): pl.pallas_call(partial(inside_back_kernel, dims), grid=(micro,), in_specs...  13.3 us
  transfers between devices with their start and end apart: 37, of which 15 were waited for; matrix products, arithmetic and copies ran while one was open for 21% of the time, Pallas kernels for 13%

profile of v2, /device:TPU:9, one launch (start us, length us, event | category | flops | bytes accessed | tf_op | source)
XLA Modules:
  0.0 334.7 jit_solution(11639147764586141173)
XLA Ops:
  1.7 3.1 collective-permute-start
  4.9 4.0 %collective-permute-start.1 = (f32[2,8,768]{2,1,0:T(8,128)S(1)}, f32[2,8,768]{2,1,0:T(8,128)S(1)}, u32[]{:S(2)}, u32[]{:S(2)}) collective-permute-start(f32[2,8,768]{2,1,0:T(8,128)S(1)} %get-tuple-element.200), channel_id=1, source_target_pairs={{2,0},{4,2},{6,4},{8,6},{10,8},{12,10},{14,12},{16,14},{18,16},{20... | collective-permute-start | bytes 147464 | tf_op jit(solution)/shard_map/ppermute | solution.py:947
  8.8 2.3 copy.38.states
  12.2 13.9 %front.1 = (f32[2,272,768]{2,1,0:T(8,128)}, f32[2,272,1024]{2,1,0:T(8,128)}, f32[2,256,1024]{2,1,0:T(8,128)}, f32[2,256,1024]{2,1,0:T(8,128)}, f32[2,256,256]{2,...) custom-call(s32[1]{0:T(128)} %bitcast.place, ...), custom_call_target="tpu_custom_call" | custom-call | tf_op jit(solution)/shard_map/front/pallas_call | solution.py:989
  26.1 5.0 %all-to-all-start = ((f32[16,104,128]{2,1,0:T(8,128)}), f32[16,104,128]{2,1,0:T(8,128)}, u32[]{:S(2)}, u32[]{:S(2)}) async-start(f32[16,104,128]{2,1,0:T(8,128)} %get-tuple-element.92), calls=%async_computation | async-start | bytes 1703936 | tf_op jit(solution)/shard_map/all_to_all | solution.py:1081
  31.2 20.3 %all-to-all-done.terms.keeps = f32[16,104,128]{2,1,0:T(8,128)} async-done(((f32[16,104,128]{2,1,0:T(8,128)}), f32[16,104,128]{2,1,0:T(8,128)}, u32[]{:S(2)}, u32[]{:S(2)}) %all-to-all-start) | async-done | bytes 852000 | tf_op jit(solution)/shard_map/all_to_all | solution.py:1081
  51.4 2.5 prefix.2
  53.9 5.1 %all-to-all-start.1 = ((f32[16,96,128]{2,1,0:T(8,128)}), f32[16,96,128]{2,1,0:T(8,128)}, u32[]{:S(2)}, u32[]{:S(2)}) async-start(f32[16,96,128]{2,1,0:T(8,128)} %prefix.2), calls=%async_computation.1 | async-start | bytes 1572864 | tf_op jit(solution)/shard_map/all_to_all | solution.py:1081
  59.2 5.4 %fusion.back = f32[2,256,768]{2,1,0:T(8,128)} fusion(f32[2,256,768]{2,1,0:T(8,128)} %param.33, f32[768,768]{1,0:T(8,128)} %param.32), kind=kOutput, calls=%fused_computation.2 | convolution fusion | flops 1811939328 | bytes 5505024 | tf_op jit(solution)/shard_map/dot_general | solution.py:22
  64.6 5.9 %inside.1 = f32[2,256,768]{2,1,0:T(8,128)} custom-call(s32[1]{0:T(128)} %bitcast.place, s32[2,8]{1,0:T(2,128)S(1)} %copy-done.8, f32[2,256,1024]{2,1,0:T(8,128)} %get-tuple-element.89.act, f32[2,256,24]{2,1,0:T(8,128)S(1)} %get-tuple-element.90.run, f32[2,24,256]{2,1,0:T(8,128)S(1)} %get-tuple-element.91.late_rows), custom_call_target="tpu_custom_call" | custom-call | tf_op jit(solution)/shard_map/inside/pallas_call | solution.py:1089
  70.5 3.5 %fusion.2.gate = f32[2,272,768]{2,1,0:T(8,128)} fusion(f32[2,272,768]{2,1,0:T(8,128)S(1)} %copy-done.14, f32[768,768]{1,0:T(8,128)S(1)} %copy-done), kind=kOutput, calls=%fused_computation.4 | convolution fusion | flops 1925185536 | bytes 5701632 | tf_op jit(solution)/shard_map/dot_general | solution.py:22
  73.9 3.9 %all-to-all-done.1.pay = f32[16,96,128]{2,1,0:T(8,128)} async-done(((f32[16,96,128]{2,1,0:T(8,128)}), f32[16,96,128]{2,1,0:T(8,128)}, u32[]{:S(2)}, u32[]{:S(2)}) %all-to-all-start.1) | async-done | bytes 786464 | tf_op jit(solution)/shard_map/all_to_all | solution.py:1081
  77.9 5.0 %join.1 = (f32[2,256,768]{2,1,0:T(8,128)}, f32[2,256,128]{2,1,0:T(8,128)S(1)}, f32[2,2,64,768]{3,2,1,0:T(8,128)}) custom-call(f32[2,256,768]{2,1,0:T(8,128)} %inside.1, f32[16,96,128]{2,1,0:T(8,128)} %all-to-all-done.1.pay, f32[2,256,1024]{2,1,0:T(8,128)} %get-tuple-element.89.act, f32[2,256,24]{2,1,0:T(8,128)S(1)} %copy-done.2, f32[2,272,768]{2,1,0:T(8,128)} %fusion.2.gate, ...), custom_call_target="tpu_custom_call" | custom-call | tf_op jit(solution)/shard_map/join/pallas_call | solution.py:1103
  82.8 2.3 collective-permute-start.2
  86.3 4.6 %turn.1 = (f32[2,256,768]{2,1,0:T(8,128)}, f32[2,256,768]{2,1,0:T(8,128)}, f32[16,96,128]{2,1,0:T(8,128)}) custom-call(f32[2,256,128]{2,1,0:T(8,128)S(1)} %get-tuple-element.95.sums, f32[2,256,128]{2,1,0:T(8,128)S(1)} %collective-permute-done.2.peer_sums, f32[2,256,768]{2,1,0:T(8,128)} %get-tuple-element.96.mixed_y, f32[2,272,768]{2,1,0:T(8,128)} %fusion.2.gate, ...), custom_call_target="tpu_custom_call" | custom-call | tf_op jit(solution)/shard_map/turn/pallas_call | solution.py:1118
  90.9 4.8 %all-to-all-start.2 = ((f32[16,96,128]{2,1,0:T(8,128)}), f32[16,96,128]{2,1,0:T(8,128)}, u32[]{:S(2)}, u32[]{:S(2)}) async-start(f32[16,96,128]{2,1,0:T(8,128)} %get-tuple-element.101), calls=%async_computation.2 | async-start | bytes 1572864 | tf_op jit(solution)/shard_map/all_to_all | solution.py:1081
  95.7 5.1 %side.1 = (f32[2,272,768]{2,1,0:T(8,128)}, f32[2,8,768]{2,1,0:T(8,128)S(1)}) custom-call(f32[2,256,128]{2,1,0:T(8,128)S(1)} %get-tuple-element.95.sums, f32[2,256,128]{2,1,0:T(8,128)S(1)} %collective-permute-done.2.peer_sums, f32[2,256,768]{2,1,0:T(8,128)} %get-tuple-element.96.mixed_y, f32[2,272,768]{2,1,0:T(8,128)} %fusion.2.gate, ...), custom_call_target="tpu_custom_call" | custom-call | tf_op jit(solution)/shard_map/side/pallas_call | solution.py:1146
  100.8 4.7 %convolution_bitcast_fusion = f32[768,768]{1,0:T(8,128)S(1)} fusion(f32[2,272,768]{2,1,0:T(8,128)S(1)} %copy-done.15, f32[2,272,768]{2,1,0:T(8,128)} %get-tuple-element.100), kind=kOutput, calls=%fused_computation.6 | convolution fusion | flops 1925185536 | bytes 5701632 | tf_op jit(solution)/shard_map/dot_general | solution.py:22
  108.2 2.4 convolution_bitcast_fusion.1
  114.6 2.4 prefix.3
  117.0 5.2 %all-to-all-start.3 = ((f32[16,96,128]{2,1,0:T(8,128)}), f32[16,96,128]{2,1,0:T(8,128)}, u32[]{:S(2)}, u32[]{:S(2)}) async-start(f32[16,96,128]{2,1,0:T(8,128)} %prefix.3), calls=%async_computation.3 | async-start | bytes 1572864 | tf_op jit(solution)/shard_map/all_to_all | solution.py:1081
  124.6 5.0 %fusion.16 = f32[544,768]{1,0:T(8,128)} fusion(f32[544,768]{1,0:T(8,128)} %bitcast.62, f32[768,768]{1,0:T(8,128)S(1)} %copy-done), kind=kOutput, calls=%fused_computation.66 | convolution fusion | flops 1925185536 | bytes 5701632 | tf_op jit(solution)/shard_map/dot_general | solution.py:22
  129.6 13.3 %inside_back.1 = (f32[2,256,768]{2,1,0:T(8,128)}, f32[2,256,256]{2,1,0:T(8,128)}, f32[2,256,24]{2,1,0:T(8,128)S(1)}, f32[2,256,24]{2,1,0:T(8,128)S(1)}) custom-call(s32[1]{0:T(128)} %bitcast.place, s32[2,8]{1,0:T(2,128)S(1)} %copy-done.8, f32[2,256,1024]{2,1,0:T(8,128)} %get-tuple-element.89.act, f32[2,256,768]{2,1,0:T(8,128)} %get-tuple-element.103.grad_y, ...), custom_call_target="tpu_custom_call" | custom-call | tf_op jit(solution)/shard_map/inside_back/pallas_call | solution.py:1164
  143.6 15.7 %end.1 = (f32[2,272,768]{2,1,0:T(8,128)}, f32[2,272,256]{2,1,0:T(8,128)}, f32[2,272,24]{2,1,0:T(8,128)}, f32[2,16,1024]{2,1,0:T(8,128)S(1)}) custom-call(s32[1]{0:T(128)} %bitcast.place, s32[2,8]{1,0:T(2,128)S(1)} %copy-done.8, f32[16,96,128]{2,1,0:T(8,128)} %all-to-all-done.3.pay, f32[2,256,1024]{2,1,0:T(8,128)} %get-tuple-element.89.act, ...), custom_call_target="tpu_custom_call" | custom-call | tf_op jit(solution)/shard_map/end/pallas_call | solution.py:1183
  163.7 2.3 fusion.17
  166.9 3.2 collective-permute-start.7
  170.0 2.4 multiply_reduce_fusion
  172.5 2.3 fusion.5
  179.0 2.1 fusion.7.rest
  181.1 2.5 pack.1
  183.6 2.1 constant_dynamic-slice_fusion.4
  186.9 2.9 collective-permute-done.14
  190.9 2.1 collective-permute-start.15
  193.0 12.9 %collective-permute-done.15 = f32[96,768]{1,0:T(8,128)S(1)} collective-permute-done((f32[96,768]{1,0:T(8,128)S(1)}, f32[96,768]{1,0:T(8,128)S(1)}, u32[]{:S(2)}, u32[]{:S(2)}) %collective-permute-start.15) | collective-permute-done | bytes 294944 | tf_op jit(solution)/shard_map/ppermute | solution.py:809
  206.9 3.2 collective-permute-start.18
  213.7 2.2 collective-permute-start.16
  215.9 4.4 %collective-permute-done.18 = f32[96,768]{1,0:T(8,128)S(1)} collective-permute-done((f32[96,768]{1,0:T(8,128)S(1)}, f32[96,768]{1,0:T(8,128)S(1)}, u32[]{:S(2)}, u32[]{:S(2)}) %collective-permute-start.18) | collective-permute-done | bytes 294944 | tf_op jit(solution)/shard_map/ppermute | solution.py:809
  221.1 1.9 collective-permute-start.20
  223.0 2.3 collective-permute-start.9
  227.7 7.2 %collective-permute-done.20 = f32[192,768]{1,0:T(8,128)} collective-permute-done((f32[192,768]{1,0:T(8,128)}, f32[192,768]{1,0:T(8,128)}, u32[]{:S(2)}, u32[]{:S(2)}) %collective-permute-start.20) | collective-permute-done | bytes 589856 | tf_op jit(solution)/shard_map/ppermute | solution.py:809
  234.9 2.3 broadcast_select_fusion
  237.2 1.9 collective-permute-start.22
  239.3 3.7 %fusion.20 = f32[512,768]{1,0:T(8,128)} fusion(f32[512,768]{1,0:T(8,128)S(1)} %bitcast.65, f32[768,768]{1,0:T(8,128)S(1)} %copy-done.26), kind=kOutput, calls=%fused_computation.70 | convolution fusion | flops 1811939328 | bytes 5505024 | tf_op jit(solution)/shard_map/dot_general | solution.py:22
  242.9 5.7 %collective-permute-start.8 = (f32[512,768]{1,0:T(8,128)}, f32[512,768]{1,0:T(8,128)}, u32[]{:S(2)}, u32[]{:S(2)}) collective-permute-start(f32[512,768]{1,0:T(8,128)} %fusion.20), channel_id=1, source_target_pairs={{0,1},{1,0},{2,3},{3,2},{4,5},{5,4},{6,7},{7,6},{8,9},{9,8},{10,11... | collective-permute-start | bytes 4718600 | tf_op jit(solution)/shard_map/ppermute | solution.py:1295
  251.3 1.8 maximum_select_fusion.2
  253.0 7.0 %collective-permute-done.21 = f32[64,768]{1,0:T(8,128)S(1)} collective-permute-done((f32[64,768]{1,0:T(8,128)S(1)}, f32[64,768]{1,0:T(8,128)S(1)}, u32[]{:S(2)}, u32[]{:S(2)}) %collective-permute-start.21) | collective-permute-done | bytes 196640 | tf_op jit(solution)/shard_map/ppermute | solution.py:809
  260.0 3.2 collective-permute-start.24
  263.2 1.9 maximum_select_fusion.3
  266.6 5.1 %collective-permute-done.24 = f32[64,768]{1,0:T(8,128)S(1)} collective-permute-done((f32[64,768]{1,0:T(8,128)S(1)}, f32[64,768]{1,0:T(8,128)S(1)}, u32[]{:S(2)}, u32[]{:S(2)}) %collective-permute-start.24) | collective-permute-done | bytes 196640 | tf_op jit(solution)/shard_map/ppermute | solution.py:809
  271.7 2.3 collective-permute-start.25
  274.2 2.1 add.158
  276.3 1.6 add.164
  278.0 5.2 %collective-permute-done.25 = f32[128,768]{1,0:T(8,128)S(1)} collective-permute-done((f32[128,768]{1,0:T(8,128)S(1)}, f32[128,768]{1,0:T(8,128)S(1)}, u32[]{:S(2)}, u32[]{:S(2)}) %collective-permute-start.25) | collective-permute-done | bytes 393248 | tf_op jit(solution)/shard_map/ppermute | solution.py:809
  284.7 2.1 collective-permute-start.10
  286.7 5.6 %collective-permute-done.29 = f32[384,768]{1,0:T(8,128)S(1)} collective-permute-done((f32[384,768]{1,0:T(8,128)S(1)}, f32[384,768]{1,0:T(8,128)S(1)}, u32[]{:S(2)}, u32[]{:S(2)}) %collective-permute-start.29) | collective-permute-done | bytes 1179680 | tf_op jit(solution)/shard_map/ppermute | solution.py:809
  292.4 2.8 collective-permute-start.11
  295.2 1.6 maximum_select_fusion
  296.8 4.5 %collective-permute-done.26 = f32[128,768]{1,0:T(8,128)S(1)} collective-permute-done((f32[128,768]{1,0:T(8,128)S(1)}, f32[128,768]{1,0:T(8,128)S(1)}, u32[]{:S(2)}, u32[]{:S(2)}) %collective-permute-start.26) | collective-permute-done | bytes 393248 | tf_op jit(solution)/shard_map/ppermute | solution.py:809
  304.4 2.2 multiply_subtract_fusion
  306.5 11.9 %collective-permute-done.31.came_second = f32[256,768]{1,0:T(8,128)S(1)} collective-permute-done((f32[256,768]{1,0:T(8,128)S(1)}, f32[256,768]{1,0:T(8,128)S(1)}, u32[]{:S(2)}, u32[]{:S(2)}) %collective-permute-start.31) | collective-permute-done | bytes 786464 | tf_op jit(solution)/shard_map/ppermute | solution.py:809
  319.8 4.2 %finish.1 = (f32[768,768]{1,0:T(8,128)}, f32[256,768]{1,0:T(8,128)S(1)}) custom-call(s32[2]{0:T(128)S(1)} %pad_add_fusion.bits, f32[256,768]{1,0:T(8,128)} %copy-done.44, f32[256,768]{1,0:T(8,128)} %copy-done.55, f32[256,768]{1,0:T(8,128)} %copy-done.43, f32[256,768]{1,0:T(8,128)} %copy-done.54), custom_call_target="tpu_custom_call" | custom-call | tf_op jit(solution)/shard_map/finish/pallas_call | solution.py:1310
  324.0 3.8 %collective-permute-start.32 = (f32[256,768]{1,0:T(8,128)S(1)}, f32[256,768]{1,0:T(8,128)}, u32[]{:S(2)}, u32[]{:S(2)}) collective-permute-start(f32[256,768]{1,0:T(8,128)S(1)} %get-tuple-element.150.mine), channel_id=1, source_target_pairs={{0,1},{1,0},{2,3},{3,2},{4,5},{5,4},{6,7},{7,6},{8,9},{9,8},{10,11... | collective-permute-start | bytes 2359304 | tf_op jit(solution)/shard_map/ppermute | solution.py:1326
  327.8 1.6 maximum_select_fusion.1
  332.3 1.9 unpack.1
  (212 shorter events, 45.3 us)
Async XLA Ops:
  0.6 69.8 %copy-start = (f32[768,768]{1,0:T(8,128)S(1)}, f32[768,768]{1,0:T(8,128)}, u32[]{:S(2)}) copy-start(f32[768,768]{1,0:T(8,128)} %param.20) | copy-start | bytes 7077892
  0.7 10.5 %copy-start.58 = (f32[768,2,12]{0,1,2:T(2,128)S(1)}, f32[768,2,12]{0,1,2:T(2,128)}, u32[]{:S(2)}) copy-start(f32[768,2,12]{0,1,2:T(2,128)} %param.23) | copy-start | bytes 221188
  0.7 11.4 %copy-start.8 = (s32[2,8]{1,0:T(2,128)S(1)}, s32[2,8]{1,0:T(2,128)}, u32[]{:S(2)}) copy-start(s32[2,8]{1,0:T(2,128)} %lengths.7) | copy-start | bytes 196
  0.7 11.4 %copy-start.6 = (f32[768]{0:T(1024)S(1)}, f32[768]{0:T(1024)}, u32[]{:S(2)}) copy-start(f32[768]{0:T(1024)} %prenorm.1) | copy-start | bytes 9220
  0.7 11.4 %copy-start.13 = (f32[2,12]{1,0:T(2,128)S(1)}, f32[2,12]{1,0:T(2,128)}, u32[]{:S(2)}) copy-start(f32[2,12]{1,0:T(2,128)} %offsets.1) | copy-start | bytes 292
  0.7 11.4 %copy-start.11 = (f32[2,12]{1,0:T(2,128)S(1)}, f32[2,12]{1,0:T(2,128)}, u32[]{:S(2)}) copy-start(f32[2,12]{1,0:T(2,128)} %decays.3) | copy-start | bytes 292
  0.7 11.4 %copy-start.7 = (f32[7,768]{1,0:T(8,128)S(1)}, f32[7,768]{1,0:T(8,128)}, u32[]{:S(2)}) copy-start(f32[7,768]{1,0:T(8,128)} %filters.1) | copy-start | bytes 64516
  0.7 11.4 %copy-start.10 = (f32[768]{0:T(1024)S(1)}, f32[768]{0:T(1024)}, u32[]{:S(2)}) copy-start(f32[768]{0:T(1024)} %shifts.1) | copy-start | bytes 9220
  0.7 11.4 %copy-start.9 = (f32[7,4,64]{2,1,0:T(4,128)S(1)}, f32[7,4,64]{2,1,0:T(4,128)}, u32[]{:S(2)}) copy-start(f32[7,4,64]{2,1,0:T(4,128)} %kernels.1) | copy-start | bytes 21508
  0.7 11.4 %copy-start.12 = (f32[4,64]{1,0:T(4,128)S(1)}, f32[4,64]{1,0:T(4,128)}, u32[]{:S(2)}) copy-start(f32[4,64]{1,0:T(4,128)} %biases.1) | copy-start | bytes 3076
  1.7 10.3 %collective-permute-start = (f32[2,8,768]{2,1,0:T(8,128)S(1)}, f32[2,8,768]{2,1,0:T(8,128)S(1)}, u32[]{:S(2)}, u32[]{:S(2)}) collective-permute-start(f32[2,8,768]{2,1,0:T(8,128)S(1)} %get-tuple-element.201), channel_id=1, source_target_pairs={{0,2},{2,4},{4,6},{6,8},{8,10},{10,12},{12,14},{14,16},{16,18},{18... | collective-permute-start | bytes 147464 | tf_op jit(solution)/shard_map/ppermute | solution.py:946
  4.9 7.2 %collective-permute-start.1 = (f32[2,8,768]{2,1,0:T(8,128)S(1)}, f32[2,8,768]{2,1,0:T(8,128)S(1)}, u32[]{:S(2)}, u32[]{:S(2)}) collective-permute-start(f32[2,8,768]{2,1,0:T(8,128)S(1)} %get-tuple-element.200), channel_id=1, source_target_pairs={{2,0},{4,2},{6,4},{8,6},{10,8},{12,10},{14,12},{16,14},{18,16},{20... | collective-permute-start | bytes 147464 | tf_op jit(solution)/shard_map/ppermute | solution.py:947
  26.1 25.3 %all-to-all-start = ((f32[16,104,128]{2,1,0:T(8,128)}), f32[16,104,128]{2,1,0:T(8,128)}, u32[]{:S(2)}, u32[]{:S(2)}) async-start(f32[16,104,128]{2,1,0:T(8,128)} %get-tuple-element.92), calls=%async_computation | async-start | bytes 1703936 | tf_op jit(solution)/shard_map/all_to_all | solution.py:1081
  51.4 7.6 %copy-start.60 = (f32[12]{0:T(128)S(1)}, f32[12]{0:T(128)}, u32[]{:S(2)}) copy-start(f32[12]{0:T(128)} %param.30) | copy-start | bytes 148
  53.9 24.0 %all-to-all-start.1 = ((f32[16,96,128]{2,1,0:T(8,128)}), f32[16,96,128]{2,1,0:T(8,128)}, u32[]{:S(2)}, u32[]{:S(2)}) async-start(f32[16,96,128]{2,1,0:T(8,128)} %prefix.2), calls=%async_computation.1 | async-start | bytes 1572864 | tf_op jit(solution)/shard_map/all_to_all | solution.py:1081
  82.8 3.5 %collective-permute-start.2 = (f32[2,256,128]{2,1,0:T(8,128)S(1)}, f32[2,256,128]{2,1,0:T(8,128)S(1)}, u32[]{:S(2)}, u32[]{:S(2)}) collective-permute-start(f32[2,256,128]{2,1,0:T(8,128)S(1)} %get-tuple-element.95.sums), channel_id=1, source_target_pairs={{0,1},{1,0},{2,3},{3,2},{4,5},{5,4},{6,7},{7,6},{8,9},{9,8},{10,11... | collective-permute-start | bytes 786440 | tf_op jit(solution)/shard_map/ppermute | solution.py:1116
  90.9 23.7 %all-to-all-start.2 = ((f32[16,96,128]{2,1,0:T(8,128)}), f32[16,96,128]{2,1,0:T(8,128)}, u32[]{:S(2)}, u32[]{:S(2)}) async-start(f32[16,96,128]{2,1,0:T(8,128)} %get-tuple-element.101), calls=%async_computation.2 | async-start | bytes 1572864 | tf_op jit(solution)/shard_map/all_to_all | solution.py:1081
  117.0 26.6 %all-to-all-start.3 = ((f32[16,96,128]{2,1,0:T(8,128)}), f32[16,96,128]{2,1,0:T(8,128)}, u32[]{:S(2)}, u32[]{:S(2)}) async-start(f32[16,96,128]{2,1,0:T(8,128)} %prefix.3), calls=%async_computation.3 | async-start | bytes 1572864 | tf_op jit(solution)/shard_map/all_to_all | solution.py:1081
  122.2 37.2 %collective-permute-start.4 = (f32[384,768]{1,0:T(8,128)}, f32[384,768]{1,0:T(8,128)}, u32[]{:S(2)}, u32[]{:S(2)}) collective-permute-start(f32[384,768]{1,0:T(8,128)} %constant_dynamic-slice_fusion.8), channel_id=1, source_target_pairs={{0,4},{2,6},{4,0},{6,2},{8,12},{10,14},{12,8},{14,10},{16,20},{18,... | collective-permute-start | bytes 3538952 | tf_op jit(solution)/shard_map/ppermute | solution.py:809
  123.5 35.9 %collective-permute-start.3 = (f32[384,768]{1,0:T(8,128)}, f32[384,768]{1,0:T(8,128)}, u32[]{:S(2)}, u32[]{:S(2)}) collective-permute-start(f32[384,768]{1,0:T(8,128)} %constant_dynamic-slice_fusion.9), channel_id=1, source_target_pairs={{0,2},{2,0},{4,6},{6,4},{8,10},{10,8},{12,14},{14,12},{16,18},{18,... | collective-permute-start | bytes 3538952 | tf_op jit(solution)/shard_map/ppermute | solution.py:809
  129.6 14.0 %copy-start.3 = (f32[2,256,24]{2,1,0:T(8,128)S(1)}, f32[2,256,24]{2,1,0:T(8,128)}, u32[]{:S(2)}) copy-start(f32[2,256,24]{2,1,0:T(8,128)} %get-tuple-element.110.tail) | copy-start | bytes 147460
  143.6 15.8 %copy-start.25 = (f32[768,768]{1,0:T(8,128)S(1)}, f32[768,768]{1,0:T(8,128)}, u32[]{:S(2)}) copy-start(f32[768,768]{1,0:T(8,128)} %copy-done.24) | copy-start | bytes 7077892
  161.1 15.7 %collective-permute-start.6 = (f32[192,768]{1,0:T(8,128)S(1)}, f32[192,768]{1,0:T(8,128)S(1)}, u32[]{:S(2)}, u32[]{:S(2)}) collective-permute-start(f32[192,768]{1,0:T(8,128)S(1)} %constant_dynamic-slice_fusion.6), channel_id=1, source_target_pairs={{0,2},{2,0},{4,6},{6,4},{8,10},{10,8},{12,14},{14,12},{16,18},{18,... | collective-permute-start | bytes 1769480 | tf_op jit(solution)/shard_map/ppermute | solution.py:809
  163.0 13.7 %copy-start.27 = (f32[384,768]{1,0:T(8,128)}, f32[384,768]{1,0:T(8,128)S(1)}, u32[]{:S(2)}) copy-start(f32[384,768]{1,0:T(8,128)S(1)} %dynamic-slice_add_fusion) | copy-start | bytes 3538948
  163.1 13.7 %collective-permute-start.5 = (f32[192,768]{1,0:T(8,128)S(1)}, f32[192,768]{1,0:T(8,128)S(1)}, u32[]{:S(2)}, u32[]{:S(2)}) collective-permute-start(f32[192,768]{1,0:T(8,128)S(1)} %constant_dynamic-slice_fusion.7), channel_id=1, source_target_pairs={{0,4},{2,6},{4,0},{6,2},{8,12},{10,14},{12,8},{14,10},{16,20},{18,... | collective-permute-start | bytes 1769480 | tf_op jit(solution)/shard_map/ppermute | solution.py:809
  166.9 10.7 %collective-permute-start.7 = (f32[544,256]{1,0:T(8,128)S(1)}, f32[544,256]{1,0:T(8,128)S(1)}, u32[]{:S(2)}, u32[]{:S(2)}) collective-permute-start(f32[544,256]{1,0:T(8,128)S(1)} %bitcast.69), channel_id=1, source_target_pairs={{0,1},{1,0},{2,3},{3,2},{4,5},{5,4},{6,7},{7,6},{8,9},{9,8},{10,11... | collective-permute-start | bytes 1671176 | tf_op jit(solution)/shard_map/ppermute | solution.py:1238
  175.9 34.2 %collective-permute-start.12 = (f32[256,768]{1,0:T(8,128)}, f32[256,768]{1,0:T(8,128)}, u32[]{:S(2)}, u32[]{:S(2)}) collective-permute-start(f32[256,768]{1,0:T(8,128)} %constant_dynamic-slice_fusion.5), channel_id=1, source_target_pairs={{0,2},{2,0},{4,6},{6,4},{8,10},{10,8},{12,14},{14,12},{16,18},{18,... | collective-permute-start | bytes 2359304 | tf_op jit(solution)/shard_map/ppermute | solution.py:809
  177.0 12.9 %collective-permute-start.14 = (f32[192,768]{1,0:T(8,128)S(1)}, f32[192,768]{1,0:T(8,128)S(1)}, u32[]{:S(2)}, u32[]{:S(2)}) collective-permute-start(f32[192,768]{1,0:T(8,128)S(1)} %broadcast_select_fusion.2), channel_id=1, source_target_pairs={{0,8},{2,10},{4,12},{6,14},{8,0},{10,2},{12,4},{14,6},{16,24},{18,... | collective-permute-start | bytes 1769480 | tf_op jit(solution)/shard_map/ppermute | solution.py:809
  181.1 8.7 %copy-start.28 = (f32[384,768]{1,0:T(8,128)S(1)}, f32[384,768]{1,0:T(8,128)}, u32[]{:S(2)}) copy-start(f32[384,768]{1,0:T(8,128)} %copy-done.27) | copy-start | bytes 3538948
  181.1 8.7 %copy-start.47 = (f32[192,768]{1,0:T(8,128)S(1)}, f32[192,768]{1,0:T(8,128)}, u32[]{:S(2)}) copy-start(f32[192,768]{1,0:T(8,128)} %copy-done.46) | copy-start | bytes 1769476
  185.7 24.4 %collective-permute-start.13 = (f32[256,768]{1,0:T(8,128)}, f32[256,768]{1,0:T(8,128)}, u32[]{:S(2)}, u32[]{:S(2)}) collective-permute-start(f32[256,768]{1,0:T(8,128)} %constant_dynamic-slice_fusion.4), channel_id=1, source_target_pairs={{0,4},{2,6},{4,0},{6,2},{8,12},{10,14},{12,8},{14,10},{16,20},{18,... | collective-permute-start | bytes 2359304 | tf_op jit(solution)/shard_map/ppermute | solution.py:809
  189.8 20.3 %copy-start.33 = (f32[512,768]{1,0:T(8,128)S(1)}, f32[512,768]{1,0:T(8,128)}, u32[]{:S(2)}) copy-start(f32[512,768]{1,0:T(8,128)} %pack.1) | copy-start | bytes 4718596
  190.9 15.0 %collective-permute-start.15 = (f32[96,768]{1,0:T(8,128)S(1)}, f32[96,768]{1,0:T(8,128)S(1)}, u32[]{:S(2)}, u32[]{:S(2)}) collective-permute-start(f32[96,768]{1,0:T(8,128)S(1)} %constant_dynamic-slice_fusion.3), channel_id=1, source_target_pairs={{0,16},{2,18},{4,20},{6,22},{8,24},{10,26},{12,28},{14,30},{16,0},... | collective-permute-start | bytes 884744 | tf_op jit(solution)/shard_map/ppermute | solution.py:809
  206.9 13.3 %collective-permute-start.18 = (f32[96,768]{1,0:T(8,128)S(1)}, f32[96,768]{1,0:T(8,128)S(1)}, u32[]{:S(2)}, u32[]{:S(2)}) collective-permute-start(f32[96,768]{1,0:T(8,128)S(1)} %dynamic-slice_add_fusion.8), channel_id=1, source_target_pairs={{0,16},{2,18},{4,20},{6,22},{8,24},{10,26},{12,28},{14,30},{16,0},... | collective-permute-start | bytes 884744 | tf_op jit(solution)/shard_map/ppermute | solution.py:809
  211.4 13.9 %collective-permute-start.17 = (f32[128,768]{1,0:T(8,128)S(1)}, f32[128,768]{1,0:T(8,128)S(1)}, u32[]{:S(2)}, u32[]{:S(2)}) collective-permute-start(f32[128,768]{1,0:T(8,128)S(1)} %constant_dynamic-slice_fusion.1), channel_id=1, source_target_pairs={{0,2},{2,0},{4,6},{6,4},{8,10},{10,8},{12,14},{14,12},{16,18},{18,... | collective-permute-start | bytes 1179656 | tf_op jit(solution)/shard_map/ppermute | solution.py:809
  212.9 12.4 %copy-start.38 = (f32[256,768]{1,0:T(8,128)}, f32[256,768]{1,0:T(8,128)S(1)}, u32[]{:S(2)}) copy-start(f32[256,768]{1,0:T(8,128)S(1)} %dynamic-slice_add_fusion.3) | copy-start | bytes 2359300
  212.9 10.1 %copy-start.29 = (f32[544,768]{1,0:T(8,128)S(1)}, f32[544,768]{1,0:T(8,128)}, u32[]{:S(2)}) copy-start(f32[544,768]{1,0:T(8,128)} %get-tuple-element.130) | copy-start | bytes 5013508
  213.7 12.3 %collective-permute-start.16 = (f32[128,768]{1,0:T(8,128)}, f32[128,768]{1,0:T(8,128)}, u32[]{:S(2)}, u32[]{:S(2)}) collective-permute-start(f32[128,768]{1,0:T(8,128)} %constant_dynamic-slice_fusion.2), channel_id=1, source_target_pairs={{0,4},{2,6},{4,0},{6,2},{8,12},{10,14},{12,8},{14,10},{16,20},{18,... | collective-permute-start | bytes 1179656 | tf_op jit(solution)/shard_map/ppermute | solution.py:809
  221.1 13.8 %collective-permute-start.20 = (f32[192,768]{1,0:T(8,128)}, f32[192,768]{1,0:T(8,128)}, u32[]{:S(2)}, u32[]{:S(2)}) collective-permute-start(f32[192,768]{1,0:T(8,128)} %maximum_select_fusion.7), channel_id=1, source_target_pairs={{0,8},{2,10},{4,12},{6,14},{8,0},{10,2},{12,4},{14,6},{16,24},{18,... | collective-permute-start | bytes 1769480 | tf_op jit(solution)/shard_map/ppermute | solution.py:809
  223.0 53.3 %collective-permute-start.9 = (f32[2,272,768]{2,1,0:T(8,128)S(1)}, f32[2,272,768]{2,1,0:T(8,128)}, u32[]{:S(2)}, u32[]{:S(2)}) collective-permute-start(f32[2,272,768]{2,1,0:T(8,128)S(1)} %bitcast.63), channel_id=1, source_target_pairs={{0,1},{1,0},{2,3},{3,2},{4,5},{5,4},{6,7},{7,6},{8,9},{9,8},{10,11... | collective-permute-start | bytes 5013512 | tf_op jit(solution)/shard_map/ppermute | solution.py:1279
  226.0 13.3 %copy-start.35 = (f32[2,256,768]{2,1,0:T(8,128)S(1)}, f32[2,256,768]{2,1,0:T(8,128)}, u32[]{:S(2)}) copy-start(f32[2,256,768]{2,1,0:T(8,128)} %get-tuple-element.98) | copy-start | bytes 4718596
  227.6 11.7 %copy-start.26 = (f32[768,768]{1,0:T(8,128)S(1)}, f32[768,768]{1,0:T(8,128)}, u32[]{:S(2)}) copy-start(f32[768,768]{1,0:T(8,128)} %param.32) | copy-start | bytes 7077892
  227.6 21.0 %collective-permute-start.19 = (f32[128,768]{1,0:T(8,128)S(1)}, f32[128,768]{1,0:T(8,128)S(1)}, u32[]{:S(2)}, u32[]{:S(2)}) collective-permute-start(f32[128,768]{1,0:T(8,128)S(1)} %broadcast_select_fusion.5), channel_id=1, source_target_pairs={{0,8},{2,10},{4,12},{6,14},{8,0},{10,2},{12,4},{14,6},{16,24},{18,... | collective-permute-start | bytes 1179656 | tf_op jit(solution)/shard_map/ppermute | solution.py:809
  237.2 14.0 %collective-permute-start.22 = (f32[192,768]{1,0:T(8,128)}, f32[192,768]{1,0:T(8,128)}, u32[]{:S(2)}, u32[]{:S(2)}) collective-permute-start(f32[192,768]{1,0:T(8,128)} %get-tuple-element.203), channel_id=1, source_target_pairs={{0,4},{2,6},{4,0},{6,2},{8,12},{10,14},{12,8},{14,10},{16,20},{18,... | collective-permute-start | bytes 1769480 | tf_op jit(solution)/shard_map/ppermute | solution.py:809
  239.1 9.5 %copy-start.37 = (f32[256,768]{1,0:T(8,128)S(1)}, f32[256,768]{1,0:T(8,128)}, u32[]{:S(2)}) copy-start(f32[256,768]{1,0:T(8,128)} %copy-done.36) | copy-start | bytes 2359300
  239.1 9.5 %copy-start.39 = (f32[256,768]{1,0:T(8,128)S(1)}, f32[256,768]{1,0:T(8,128)}, u32[]{:S(2)}) copy-start(f32[256,768]{1,0:T(8,128)} %copy-done.38) | copy-start | bytes 2359300
  239.1 9.5 %copy-start.49 = (f32[128,768]{1,0:T(8,128)S(1)}, f32[128,768]{1,0:T(8,128)}, u32[]{:S(2)}) copy-start(f32[128,768]{1,0:T(8,128)} %copy-done.48) | copy-start | bytes 1179652
  239.1 12.1 %collective-permute-start.23 = (f32[192,768]{1,0:T(8,128)}, f32[192,768]{1,0:T(8,128)}, u32[]{:S(2)}, u32[]{:S(2)}) collective-permute-start(f32[192,768]{1,0:T(8,128)} %get-tuple-element.202), channel_id=1, source_target_pairs={{0,2},{2,0},{4,6},{6,4},{8,10},{10,8},{12,14},{14,12},{16,18},{18,... | collective-permute-start | bytes 1769480 | tf_op jit(solution)/shard_map/ppermute | solution.py:809
  242.9 31.3 %collective-permute-start.8 = (f32[512,768]{1,0:T(8,128)}, f32[512,768]{1,0:T(8,128)}, u32[]{:S(2)}, u32[]{:S(2)}) collective-permute-start(f32[512,768]{1,0:T(8,128)} %fusion.20), channel_id=1, source_target_pairs={{0,1},{1,0},{2,3},{3,2},{4,5},{5,4},{6,7},{7,6},{8,9},{9,8},{10,11... | collective-permute-start | bytes 4718600 | tf_op jit(solution)/shard_map/ppermute | solution.py:1295
  249.8 10.2 %collective-permute-start.21 = (f32[64,768]{1,0:T(8,128)S(1)}, f32[64,768]{1,0:T(8,128)S(1)}, u32[]{:S(2)}, u32[]{:S(2)}) collective-permute-start(f32[64,768]{1,0:T(8,128)S(1)} %constant_dynamic-slice_fusion), channel_id=1, source_target_pairs={{0,16},{2,18},{4,20},{6,22},{8,24},{10,26},{12,28},{14,30},{16,0},... | collective-permute-start | bytes 589832 | tf_op jit(solution)/shard_map/ppermute | solution.py:809
  260.0 11.7 %collective-permute-start.24 = (f32[64,768]{1,0:T(8,128)S(1)}, f32[64,768]{1,0:T(8,128)S(1)}, u32[]{:S(2)}, u32[]{:S(2)}) collective-permute-start(f32[64,768]{1,0:T(8,128)S(1)} %dynamic-slice_add_fusion.11), channel_id=1, source_target_pairs={{0,16},{2,18},{4,20},{6,22},{8,24},{10,26},{12,28},{14,30},{16,0},... | collective-permute-start | bytes 589832 | tf_op jit(solution)/shard_map/ppermute | solution.py:809
  265.1 11.2 %copy-start.40 = (f32[384,768]{1,0:T(8,128)}, f32[384,768]{1,0:T(8,128)S(1)}, u32[]{:S(2)}) copy-start(f32[384,768]{1,0:T(8,128)S(1)} %maximum_select_fusion.3) | copy-start | bytes 3538948
  265.1 27.2 %collective-permute-start.29 = (f32[384,768]{1,0:T(8,128)S(1)}, f32[384,768]{1,0:T(8,128)S(1)}, u32[]{:S(2)}, u32[]{:S(2)}) collective-permute-start(f32[384,768]{1,0:T(8,128)S(1)} %maximum_select_fusion.3), channel_id=1, source_target_pairs={{0,4},{2,6},{4,0},{6,2},{8,12},{10,14},{12,8},{14,10},{16,20},{18,... | collective-permute-start | bytes 3538952 | tf_op jit(solution)/shard_map/ppermute | solution.py:809
  265.2 29.9 %collective-permute-start.28 = (f32[384,768]{1,0:T(8,128)S(1)}, f32[384,768]{1,0:T(8,128)S(1)}, u32[]{:S(2)}, u32[]{:S(2)}) collective-permute-start(f32[384,768]{1,0:T(8,128)S(1)} %maximum_select_fusion.2), channel_id=1, source_target_pairs={{0,2},{2,0},{4,6},{6,4},{8,10},{10,8},{12,14},{14,12},{16,18},{18,... | collective-permute-start | bytes 3538952 | tf_op jit(solution)/shard_map/ppermute | solution.py:809
  271.7 11.4 %collective-permute-start.25 = (f32[128,768]{1,0:T(8,128)S(1)}, f32[128,768]{1,0:T(8,128)S(1)}, u32[]{:S(2)}, u32[]{:S(2)}) collective-permute-start(f32[128,768]{1,0:T(8,128)S(1)} %maximum_select_fusion.8), channel_id=1, source_target_pairs={{0,8},{2,10},{4,12},{6,14},{8,0},{10,2},{12,4},{14,6},{16,24},{18,... | collective-permute-start | bytes 1179656 | tf_op jit(solution)/shard_map/ppermute | solution.py:809
  283.2 18.1 %collective-permute-start.26 = (f32[128,768]{1,0:T(8,128)S(1)}, f32[128,768]{1,0:T(8,128)S(1)}, u32[]{:S(2)}, u32[]{:S(2)}) collective-permute-start(f32[128,768]{1,0:T(8,128)S(1)} %get-tuple-element.205), channel_id=1, source_target_pairs={{0,4},{2,6},{4,0},{6,2},{8,12},{10,14},{12,8},{14,10},{16,20},{18,... | collective-permute-start | bytes 1179656 | tf_op jit(solution)/shard_map/ppermute | solution.py:809
  283.3 18.0 %collective-permute-start.27 = (f32[128,768]{1,0:T(8,128)S(1)}, f32[128,768]{1,0:T(8,128)S(1)}, u32[]{:S(2)}, u32[]{:S(2)}) collective-permute-start(f32[128,768]{1,0:T(8,128)S(1)} %get-tuple-element.204), channel_id=1, source_target_pairs={{0,2},{2,0},{4,6},{6,4},{8,10},{10,8},{12,14},{14,12},{16,18},{18,... | collective-permute-start | bytes 1179656 | tf_op jit(solution)/shard_map/ppermute | solution.py:809
  284.7 18.4 %collective-permute-start.10 = (f32[2,8,768]{2,1,0:T(8,128)S(1)}, f32[2,8,768]{2,1,0:T(8,128)S(1)}, u32[]{:S(2)}, u32[]{:S(2)}) collective-permute-start(f32[2,8,768]{2,1,0:T(8,128)S(1)} %get-tuple-element.196), channel_id=1, source_target_pairs={{0,2},{2,4},{4,6},{6,8},{8,10},{10,12},{12,14},{14,16},{16,18},{18... | collective-permute-start | bytes 147464 | tf_op jit(solution)/shard_map/ppermute | solution.py:1281
  292.4 10.7 %collective-permute-start.11 = (f32[2,8,768]{2,1,0:T(8,128)S(1)}, f32[2,8,768]{2,1,0:T(8,128)S(1)}, u32[]{:S(2)}, u32[]{:S(2)}) collective-permute-start(f32[2,8,768]{2,1,0:T(8,128)S(1)} %get-tuple-element.197), channel_id=1, source_target_pairs={{2,0},{4,2},{6,4},{8,6},{10,8},{12,10},{14,12},{16,14},{18,16},{20... | collective-permute-start | bytes 147464 | tf_op jit(solution)/shard_map/ppermute | solution.py:1280
  301.4 17.1 %collective-permute-start.31 = (f32[256,768]{1,0:T(8,128)S(1)}, f32[256,768]{1,0:T(8,128)S(1)}, u32[]{:S(2)}, u32[]{:S(2)}) collective-permute-start(f32[256,768]{1,0:T(8,128)S(1)} %maximum_select_fusion.5.own_second), channel_id=1, source_target_pairs={{0,4},{2,6},{4,0},{6,2},{8,12},{10,14},{12,8},{14,10},{16,20},{18,... | collective-permute-start | bytes 2359304 | tf_op jit(solution)/shard_map/ppermute | solution.py:809
  302.7 16.2 %collective-permute-start.30 = (f32[256,768]{1,0:T(8,128)S(1)}, f32[256,768]{1,0:T(8,128)S(1)}, u32[]{:S(2)}, u32[]{:S(2)}) collective-permute-start(f32[256,768]{1,0:T(8,128)S(1)} %maximum_select_fusion.4.own_first), channel_id=1, source_target_pairs={{0,2},{2,0},{4,6},{6,4},{8,10},{10,8},{12,14},{14,12},{16,18},{18,... | collective-permute-start | bytes 2359304 | tf_op jit(solution)/shard_map/ppermute | solution.py:809
  319.8 8.0 %copy-start.41 = (f32[384,768]{1,0:T(8,128)S(1)}, f32[384,768]{1,0:T(8,128)}, u32[]{:S(2)}) copy-start(f32[384,768]{1,0:T(8,128)} %copy-done.40) | copy-start | bytes 3538948
  319.8 8.0 %copy-start.52 = (f32[384,768]{1,0:T(8,128)S(1)}, f32[384,768]{1,0:T(8,128)}, u32[]{:S(2)}) copy-start(f32[384,768]{1,0:T(8,128)} %copy-done.51) | copy-start | bytes 3538948
  324.0 6.2 %collective-permute-start.32 = (f32[256,768]{1,0:T(8,128)S(1)}, f32[256,768]{1,0:T(8,128)}, u32[]{:S(2)}, u32[]{:S(2)}) collective-permute-start(f32[256,768]{1,0:T(8,128)S(1)} %get-tuple-element.150.mine), channel_id=1, source_target_pairs={{0,1},{1,0},{2,3},{3,2},{4,5},{5,4},{6,7},{7,6},{8,9},{9,8},{10,11... | collective-permute-start | bytes 2359304 | tf_op jit(solution)/shard_map/ppermute | solution.py:1326
  (34 other events, 109.4 us)

commit v3 on v2

--- a/solution.py
+++ b/solution.py
@@ -1070,7 +1070,7 @@
         return pl.pallas_call(
             partial(prefix_kernel, tiles, rows),
             grid=(1,),
-            in_specs=[smem, fixed(*terms.shape), fixed(*keeps.shape)],
+            in_specs=[smem, vmem, vmem],
             out_specs=fixed(peers, tiles * rows, LANES),
             out_shape=shape(peers, tiles * rows, LANES),
             compiler_params=PARAMS,

time: 341 us -> 341 us (level)
  no operation moved by 1% of the time
where the time goes in v3:
time: 341 us; the launch traced here: 335 us
  waiting for transfers between devices  94.2 us (28%)
  starting transfers between devices  77.7 us (23%)
  Pallas kernels  77.1 us (23%)
  matrix products  36 us (11%)
  other arithmetic  27.4 us (8%)
  local copies, waits for them, and re-layouts  20.3 us (6%)
    ppermute x24, waiting for transfers between devices, exchange(): return lax.ppermute(x, axis, [(i, i ^ 1 << bit) for i in range(peers)])  67.3 us
    dot_general x13, matrix products, dot(): lax.dot_general(left, right, (((over_left,), (over_right,)), ((), ())), p...  36 us
    ppermute x24, starting transfers between devices, exchange(): return lax.ppermute(x, axis, [(i, i ^ 1 << bit) for i in range(peers)])  28.5 us
    all_to_all x4, waiting for transfers between devices, swap_all(): return lax.all_to_all(x, 'seq', 0, 0, tiled=True)  25.7 us
    all_to_all x4, starting transfers between devices, swap_all(): return lax.all_to_all(x, 'seq', 0, 0, tiled=True)  20.1 us
    pallas_call x1, Pallas kernels, local(): pl.pallas_call(partial(end_kernel, dims), grid=(micro,), in_specs=[smem,...  15.7 us
    pallas_call x1, Pallas kernels, local(): pl.pallas_call(partial(front_kernel, dims), grid=(micro,), in_specs=[smem...  13.9 us
    pallas_call x1, Pallas kernels, local(): pl.pallas_call(partial(inside_back_kernel, dims), grid=(micro,), in_specs...  13.3 us
  transfers between devices with their start and end apart: 37, of which 15 were waited for; matrix products, arithmetic and copies ran while one was open for 21% of the time, Pallas kernels for 13%

profile of v3, /device:TPU:9, one launch (start us, length us, event | category | flops | bytes accessed | tf_op | source)
XLA Modules:
  0.0 334.7 jit_solution(11639147764586141173)
XLA Ops:
  1.7 3.1 collective-permute-start
  4.9 4.0 %collective-permute-start.1 = (f32[2,8,768]{2,1,0:T(8,128)S(1)}, f32[2,8,768]{2,1,0:T(8,128)S(1)}, u32[]{:S(2)}, u32[]{:S(2)}) collective-permute-start(f32[2,8,768]{2,1,0:T(8,128)S(1)} %get-tuple-element.200), channel_id=1, source_target_pairs={{2,0},{4,2},{6,4},{8,6},{10,8},{12,10},{14,12},{16,14},{18,16},{20... | collective-permute-start | bytes 147464 | tf_op jit(solution)/shard_map/ppermute | solution.py:947
  8.8 2.3 copy.38.states
  12.2 13.9 %front.1 = (f32[2,272,768]{2,1,0:T(8,128)}, f32[2,272,1024]{2,1,0:T(8,128)}, f32[2,256,1024]{2,1,0:T(8,128)}, f32[2,256,1024]{2,1,0:T(8,128)}, f32[2,256,256]{2,...) custom-call(s32[1]{0:T(128)} %bitcast.place, ...), custom_call_target="tpu_custom_call" | custom-call | tf_op jit(solution)/shard_map/front/pallas_call | solution.py:989
  26.1 5.0 %all-to-all-start = ((f32[16,104,128]{2,1,0:T(8,128)}), f32[16,104,128]{2,1,0:T(8,128)}, u32[]{:S(2)}, u32[]{:S(2)}) async-start(f32[16,104,128]{2,1,0:T(8,128)} %get-tuple-element.92), calls=%async_computation | async-start | bytes 1703936 | tf_op jit(solution)/shard_map/all_to_all | solution.py:1081
  31.2 20.3 %all-to-all-done.terms.keeps = f32[16,104,128]{2,1,0:T(8,128)} async-done(((f32[16,104,128]{2,1,0:T(8,128)}), f32[16,104,128]{2,1,0:T(8,128)}, u32[]{:S(2)}, u32[]{:S(2)}) %all-to-all-start) | async-done | bytes 852000 | tf_op jit(solution)/shard_map/all_to_all | solution.py:1081
  51.4 2.5 prefix.2
  53.9 5.1 %all-to-all-start.1 = ((f32[16,96,128]{2,1,0:T(8,128)}), f32[16,96,128]{2,1,0:T(8,128)}, u32[]{:S(2)}, u32[]{:S(2)}) async-start(f32[16,96,128]{2,1,0:T(8,128)} %prefix.2), calls=%async_computation.1 | async-start | bytes 1572864 | tf_op jit(solution)/shard_map/all_to_all | solution.py:1081
  59.2 5.4 %fusion.back = f32[2,256,768]{2,1,0:T(8,128)} fusion(f32[2,256,768]{2,1,0:T(8,128)} %param.33, f32[768,768]{1,0:T(8,128)} %param.32), kind=kOutput, calls=%fused_computation.2 | convolution fusion | flops 1811939328 | bytes 5505024 | tf_op jit(solution)/shard_map/dot_general | solution.py:22
  64.6 5.9 %inside.1 = f32[2,256,768]{2,1,0:T(8,128)} custom-call(s32[1]{0:T(128)} %bitcast.place, s32[2,8]{1,0:T(2,128)S(1)} %copy-done.8, f32[2,256,1024]{2,1,0:T(8,128)} %get-tuple-element.89.act, f32[2,256,24]{2,1,0:T(8,128)S(1)} %get-tuple-element.90.run, f32[2,24,256]{2,1,0:T(8,128)S(1)} %get-tuple-element.91.late_rows), custom_call_target="tpu_custom_call" | custom-call | tf_op jit(solution)/shard_map/inside/pallas_call | solution.py:1089
  70.5 3.5 %fusion.2.gate = f32[2,272,768]{2,1,0:T(8,128)} fusion(f32[2,272,768]{2,1,0:T(8,128)S(1)} %copy-done.14, f32[768,768]{1,0:T(8,128)S(1)} %copy-done), kind=kOutput, calls=%fused_computation.4 | convolution fusion | flops 1925185536 | bytes 5701632 | tf_op jit(solution)/shard_map/dot_general | solution.py:22
  73.9 3.9 %all-to-all-done.1.pay = f32[16,96,128]{2,1,0:T(8,128)} async-done(((f32[16,96,128]{2,1,0:T(8,128)}), f32[16,96,128]{2,1,0:T(8,128)}, u32[]{:S(2)}, u32[]{:S(2)}) %all-to-all-start.1) | async-done | bytes 786464 | tf_op jit(solution)/shard_map/all_to_all | solution.py:1081
  77.9 5.0 %join.1 = (f32[2,256,768]{2,1,0:T(8,128)}, f32[2,256,128]{2,1,0:T(8,128)S(1)}, f32[2,2,64,768]{3,2,1,0:T(8,128)}) custom-call(f32[2,256,768]{2,1,0:T(8,128)} %inside.1, f32[16,96,128]{2,1,0:T(8,128)} %all-to-all-done.1.pay, f32[2,256,1024]{2,1,0:T(8,128)} %get-tuple-element.89.act, f32[2,256,24]{2,1,0:T(8,128)S(1)} %copy-done.2, f32[2,272,768]{2,1,0:T(8,128)} %fusion.2.gate, ...), custom_call_target="tpu_custom_call" | custom-call | tf_op jit(solution)/shard_map/join/pallas_call | solution.py:1103
  82.8 2.3 collective-permute-start.2
  86.3 4.6 %turn.1 = (f32[2,256,768]{2,1,0:T(8,128)}, f32[2,256,768]{2,1,0:T(8,128)}, f32[16,96,128]{2,1,0:T(8,128)}) custom-call(f32[2,256,128]{2,1,0:T(8,128)S(1)} %get-tuple-element.95.sums, f32[2,256,128]{2,1,0:T(8,128)S(1)} %collective-permute-done.2.peer_sums, f32[2,256,768]{2,1,0:T(8,128)} %get-tuple-element.96.mixed_y, f32[2,272,768]{2,1,0:T(8,128)} %fusion.2.gate, ...), custom_call_target="tpu_custom_call" | custom-call | tf_op jit(solution)/shard_map/turn/pallas_call | solution.py:1118
  90.9 4.8 %all-to-all-start.2 = ((f32[16,96,128]{2,1,0:T(8,128)}), f32[16,96,128]{2,1,0:T(8,128)}, u32[]{:S(2)}, u32[]{:S(2)}) async-start(f32[16,96,128]{2,1,0:T(8,128)} %get-tuple-element.101), calls=%async_computation.2 | async-start | bytes 1572864 | tf_op jit(solution)/shard_map/all_to_all | solution.py:1081
  95.7 5.1 %side.1 = (f32[2,272,768]{2,1,0:T(8,128)}, f32[2,8,768]{2,1,0:T(8,128)S(1)}) custom-call(f32[2,256,128]{2,1,0:T(8,128)S(1)} %get-tuple-element.95.sums, f32[2,256,128]{2,1,0:T(8,128)S(1)} %collective-permute-done.2.peer_sums, f32[2,256,768]{2,1,0:T(8,128)} %get-tuple-element.96.mixed_y, f32[2,272,768]{2,1,0:T(8,128)} %fusion.2.gate, ...), custom_call_target="tpu_custom_call" | custom-call | tf_op jit(solution)/shard_map/side/pallas_call | solution.py:1146
  100.8 4.7 %convolution_bitcast_fusion = f32[768,768]{1,0:T(8,128)S(1)} fusion(f32[2,272,768]{2,1,0:T(8,128)S(1)} %copy-done.15, f32[2,272,768]{2,1,0:T(8,128)} %get-tuple-element.100), kind=kOutput, calls=%fused_computation.6 | convolution fusion | flops 1925185536 | bytes 5701632 | tf_op jit(solution)/shard_map/dot_general | solution.py:22
  108.2 2.4 convolution_bitcast_fusion.1
  114.6 2.4 prefix.3
  117.0 5.2 %all-to-all-start.3 = ((f32[16,96,128]{2,1,0:T(8,128)}), f32[16,96,128]{2,1,0:T(8,128)}, u32[]{:S(2)}, u32[]{:S(2)}) async-start(f32[16,96,128]{2,1,0:T(8,128)} %prefix.3), calls=%async_computation.3 | async-start | bytes 1572864 | tf_op jit(solution)/shard_map/all_to_all | solution.py:1081
  124.6 5.0 %fusion.16 = f32[544,768]{1,0:T(8,128)} fusion(f32[544,768]{1,0:T(8,128)} %bitcast.62, f32[768,768]{1,0:T(8,128)S(1)} %copy-done), kind=kOutput, calls=%fused_computation.66 | convolution fusion | flops 1925185536 | bytes 5701632 | tf_op jit(solution)/shard_map/dot_general | solution.py:22
  129.6 13.3 %inside_back.1 = (f32[2,256,768]{2,1,0:T(8,128)}, f32[2,256,256]{2,1,0:T(8,128)}, f32[2,256,24]{2,1,0:T(8,128)S(1)}, f32[2,256,24]{2,1,0:T(8,128)S(1)}) custom-call(s32[1]{0:T(128)} %bitcast.place, s32[2,8]{1,0:T(2,128)S(1)} %copy-done.8, f32[2,256,1024]{2,1,0:T(8,128)} %get-tuple-element.89.act, f32[2,256,768]{2,1,0:T(8,128)} %get-tuple-element.103.grad_y, ...), custom_call_target="tpu_custom_call" | custom-call | tf_op jit(solution)/shard_map/inside_back/pallas_call | solution.py:1164
  143.6 15.7 %end.1 = (f32[2,272,768]{2,1,0:T(8,128)}, f32[2,272,256]{2,1,0:T(8,128)}, f32[2,272,24]{2,1,0:T(8,128)}, f32[2,16,1024]{2,1,0:T(8,128)S(1)}) custom-call(s32[1]{0:T(128)} %bitcast.place, s32[2,8]{1,0:T(2,128)S(1)} %copy-done.8, f32[16,96,128]{2,1,0:T(8,128)} %all-to-all-done.3.pay, f32[2,256,1024]{2,1,0:T(8,128)} %get-tuple-element.89.act, ...), custom_call_target="tpu_custom_call" | custom-call | tf_op jit(solution)/shard_map/end/pallas_call | solution.py:1183
  163.7 2.3 fusion.17
  166.9 3.2 collective-permute-start.7
  170.0 2.4 multiply_reduce_fusion
  172.5 2.3 fusion.5
  179.0 2.1 fusion.7.rest
  181.1 2.5 pack.1
  183.6 2.1 constant_dynamic-slice_fusion.4
  186.9 2.9 collective-permute-done.14
  190.9 2.1 collective-permute-start.15
  193.0 12.9 %collective-permute-done.15 = f32[96,768]{1,0:T(8,128)S(1)} collective-permute-done((f32[96,768]{1,0:T(8,128)S(1)}, f32[96,768]{1,0:T(8,128)S(1)}, u32[]{:S(2)}, u32[]{:S(2)}) %collective-permute-start.15) | collective-permute-done | bytes 294944 | tf_op jit(solution)/shard_map/ppermute | solution.py:809
  206.9 3.2 collective-permute-start.18
  213.7 2.2 collective-permute-start.16
  215.9 4.4 %collective-permute-done.18 = f32[96,768]{1,0:T(8,128)S(1)} collective-permute-done((f32[96,768]{1,0:T(8,128)S(1)}, f32[96,768]{1,0:T(8,128)S(1)}, u32[]{:S(2)}, u32[]{:S(2)}) %collective-permute-start.18) | collective-permute-done | bytes 294944 | tf_op jit(solution)/shard_map/ppermute | solution.py:809
  221.1 1.9 collective-permute-start.20
  223.0 2.3 collective-permute-start.9
  227.7 7.2 %collective-permute-done.20 = f32[192,768]{1,0:T(8,128)} collective-permute-done((f32[192,768]{1,0:T(8,128)}, f32[192,768]{1,0:T(8,128)}, u32[]{:S(2)}, u32[]{:S(2)}) %collective-permute-start.20) | collective-permute-done | bytes 589856 | tf_op jit(solution)/shard_map/ppermute | solution.py:809
  234.9 2.3 broadcast_select_fusion
  237.2 1.9 collective-permute-start.22
  239.3 3.7 %fusion.20 = f32[512,768]{1,0:T(8,128)} fusion(f32[512,768]{1,0:T(8,128)S(1)} %bitcast.65, f32[768,768]{1,0:T(8,128)S(1)} %copy-done.26), kind=kOutput, calls=%fused_computation.70 | convolution fusion | flops 1811939328 | bytes 5505024 | tf_op jit(solution)/shard_map/dot_general | solution.py:22
  242.9 5.7 %collective-permute-start.8 = (f32[512,768]{1,0:T(8,128)}, f32[512,768]{1,0:T(8,128)}, u32[]{:S(2)}, u32[]{:S(2)}) collective-permute-start(f32[512,768]{1,0:T(8,128)} %fusion.20), channel_id=1, source_target_pairs={{0,1},{1,0},{2,3},{3,2},{4,5},{5,4},{6,7},{7,6},{8,9},{9,8},{10,11... | collective-permute-start | bytes 4718600 | tf_op jit(solution)/shard_map/ppermute | solution.py:1295
  251.3 1.8 maximum_select_fusion.2
  253.0 7.0 %collective-permute-done.21 = f32[64,768]{1,0:T(8,128)S(1)} collective-permute-done((f32[64,768]{1,0:T(8,128)S(1)}, f32[64,768]{1,0:T(8,128)S(1)}, u32[]{:S(2)}, u32[]{:S(2)}) %collective-permute-start.21) | collective-permute-done | bytes 196640 | tf_op jit(solution)/shard_map/ppermute | solution.py:809
  260.0 3.2 collective-permute-start.24
  263.2 1.9 maximum_select_fusion.3
  266.6 5.1 %collective-permute-done.24 = f32[64,768]{1,0:T(8,128)S(1)} collective-permute-done((f32[64,768]{1,0:T(8,128)S(1)}, f32[64,768]{1,0:T(8,128)S(1)}, u32[]{:S(2)}, u32[]{:S(2)}) %collective-permute-start.24) | collective-permute-done | bytes 196640 | tf_op jit(solution)/shard_map/ppermute | solution.py:809
  271.7 2.3 collective-permute-start.25
  274.2 2.1 add.158
  276.3 1.6 add.164
  278.0 5.2 %collective-permute-done.25 = f32[128,768]{1,0:T(8,128)S(1)} collective-permute-done((f32[128,768]{1,0:T(8,128)S(1)}, f32[128,768]{1,0:T(8,128)S(1)}, u32[]{:S(2)}, u32[]{:S(2)}) %collective-permute-start.25) | collective-permute-done | bytes 393248 | tf_op jit(solution)/shard_map/ppermute | solution.py:809
  284.7 2.1 collective-permute-start.10
  286.7 5.6 %collective-permute-done.29 = f32[384,768]{1,0:T(8,128)S(1)} collective-permute-done((f32[384,768]{1,0:T(8,128)S(1)}, f32[384,768]{1,0:T(8,128)S(1)}, u32[]{:S(2)}, u32[]{:S(2)}) %collective-permute-start.29) | collective-permute-done | bytes 1179680 | tf_op jit(solution)/shard_map/ppermute | solution.py:809
  292.4 2.8 collective-permute-start.11
  295.2 1.6 maximum_select_fusion
  296.8 4.5 %collective-permute-done.26 = f32[128,768]{1,0:T(8,128)S(1)} collective-permute-done((f32[128,768]{1,0:T(8,128)S(1)}, f32[128,768]{1,0:T(8,128)S(1)}, u32[]{:S(2)}, u32[]{:S(2)}) %collective-permute-start.26) | collective-permute-done | bytes 393248 | tf_op jit(solution)/shard_map/ppermute | solution.py:809
  304.4 2.2 multiply_subtract_fusion
  306.5 11.9 %collective-permute-done.31.came_second = f32[256,768]{1,0:T(8,128)S(1)} collective-permute-done((f32[256,768]{1,0:T(8,128)S(1)}, f32[256,768]{1,0:T(8,128)S(1)}, u32[]{:S(2)}, u32[]{:S(2)}) %collective-permute-start.31) | collective-permute-done | bytes 786464 | tf_op jit(solution)/shard_map/ppermute | solution.py:809
  319.8 4.2 %finish.1 = (f32[768,768]{1,0:T(8,128)}, f32[256,768]{1,0:T(8,128)S(1)}) custom-call(s32[2]{0:T(128)S(1)} %pad_add_fusion.bits, f32[256,768]{1,0:T(8,128)} %copy-done.44, f32[256,768]{1,0:T(8,128)} %copy-done.55, f32[256,768]{1,0:T(8,128)} %copy-done.43, f32[256,768]{1,0:T(8,128)} %copy-done.54), custom_call_target="tpu_custom_call" | custom-call | tf_op jit(solution)/shard_map/finish/pallas_call | solution.py:1310
  324.0 3.8 %collective-permute-start.32 = (f32[256,768]{1,0:T(8,128)S(1)}, f32[256,768]{1,0:T(8,128)}, u32[]{:S(2)}, u32[]{:S(2)}) collective-permute-start(f32[256,768]{1,0:T(8,128)S(1)} %get-tuple-element.150.mine), channel_id=1, source_target_pairs={{0,1},{1,0},{2,3},{3,2},{4,5},{5,4},{6,7},{7,6},{8,9},{9,8},{10,11... | collective-permute-start | bytes 2359304 | tf_op jit(solution)/shard_map/ppermute | solution.py:1326
  327.8 1.6 maximum_select_fusion.1
  332.3 1.9 unpack.1
  (212 shorter events, 45.3 us)
Async XLA Ops:
  0.6 69.8 %copy-start = (f32[768,768]{1,0:T(8,128)S(1)}, f32[768,768]{1,0:T(8,128)}, u32[]{:S(2)}) copy-start(f32[768,768]{1,0:T(8,128)} %param.20) | copy-start | bytes 7077892
  0.7 10.5 %copy-start.58 = (f32[768,2,12]{0,1,2:T(2,128)S(1)}, f32[768,2,12]{0,1,2:T(2,128)}, u32[]{:S(2)}) copy-start(f32[768,2,12]{0,1,2:T(2,128)} %param.23) | copy-start | bytes 221188
  0.7 11.4 %copy-start.8 = (s32[2,8]{1,0:T(2,128)S(1)}, s32[2,8]{1,0:T(2,128)}, u32[]{:S(2)}) copy-start(s32[2,8]{1,0:T(2,128)} %lengths.7) | copy-start | bytes 196
  0.7 11.4 %copy-start.6 = (f32[768]{0:T(1024)S(1)}, f32[768]{0:T(1024)}, u32[]{:S(2)}) copy-start(f32[768]{0:T(1024)} %prenorm.1) | copy-start | bytes 9220
  0.7 11.4 %copy-start.13 = (f32[2,12]{1,0:T(2,128)S(1)}, f32[2,12]{1,0:T(2,128)}, u32[]{:S(2)}) copy-start(f32[2,12]{1,0:T(2,128)} %offsets.1) | copy-start | bytes 292
  0.7 11.4 %copy-start.11 = (f32[2,12]{1,0:T(2,128)S(1)}, f32[2,12]{1,0:T(2,128)}, u32[]{:S(2)}) copy-start(f32[2,12]{1,0:T(2,128)} %decays.3) | copy-start | bytes 292
  0.7 11.4 %copy-start.7 = (f32[7,768]{1,0:T(8,128)S(1)}, f32[7,768]{1,0:T(8,128)}, u32[]{:S(2)}) copy-start(f32[7,768]{1,0:T(8,128)} %filters.1) | copy-start | bytes 64516
  0.7 11.4 %copy-start.10 = (f32[768]{0:T(1024)S(1)}, f32[768]{0:T(1024)}, u32[]{:S(2)}) copy-start(f32[768]{0:T(1024)} %shifts.1) | copy-start | bytes 9220
  0.7 11.4 %copy-start.9 = (f32[7,4,64]{2,1,0:T(4,128)S(1)}, f32[7,4,64]{2,1,0:T(4,128)}, u32[]{:S(2)}) copy-start(f32[7,4,64]{2,1,0:T(4,128)} %kernels.1) | copy-start | bytes 21508
  0.7 11.4 %copy-start.12 = (f32[4,64]{1,0:T(4,128)S(1)}, f32[4,64]{1,0:T(4,128)}, u32[]{:S(2)}) copy-start(f32[4,64]{1,0:T(4,128)} %biases.1) | copy-start | bytes 3076
  1.7 10.3 %collective-permute-start = (f32[2,8,768]{2,1,0:T(8,128)S(1)}, f32[2,8,768]{2,1,0:T(8,128)S(1)}, u32[]{:S(2)}, u32[]{:S(2)}) collective-permute-start(f32[2,8,768]{2,1,0:T(8,128)S(1)} %get-tuple-element.201), channel_id=1, source_target_pairs={{0,2},{2,4},{4,6},{6,8},{8,10},{10,12},{12,14},{14,16},{16,18},{18... | collective-permute-start | bytes 147464 | tf_op jit(solution)/shard_map/ppermute | solution.py:946
  4.9 7.2 %collective-permute-start.1 = (f32[2,8,768]{2,1,0:T(8,128)S(1)}, f32[2,8,768]{2,1,0:T(8,128)S(1)}, u32[]{:S(2)}, u32[]{:S(2)}) collective-permute-start(f32[2,8,768]{2,1,0:T(8,128)S(1)} %get-tuple-element.200), channel_id=1, source_target_pairs={{2,0},{4,2},{6,4},{8,6},{10,8},{12,10},{14,12},{16,14},{18,16},{20... | collective-permute-start | bytes 147464 | tf_op jit(solution)/shard_map/ppermute | solution.py:947
  26.1 25.3 %all-to-all-start = ((f32[16,104,128]{2,1,0:T(8,128)}), f32[16,104,128]{2,1,0:T(8,128)}, u32[]{:S(2)}, u32[]{:S(2)}) async-start(f32[16,104,128]{2,1,0:T(8,128)} %get-tuple-element.92), calls=%async_computation | async-start | bytes 1703936 | tf_op jit(solution)/shard_map/all_to_all | solution.py:1081
  51.4 7.6 %copy-start.60 = (f32[12]{0:T(128)S(1)}, f32[12]{0:T(128)}, u32[]{:S(2)}) copy-start(f32[12]{0:T(128)} %param.30) | copy-start | bytes 148
  53.9 24.0 %all-to-all-start.1 = ((f32[16,96,128]{2,1,0:T(8,128)}), f32[16,96,128]{2,1,0:T(8,128)}, u32[]{:S(2)}, u32[]{:S(2)}) async-start(f32[16,96,128]{2,1,0:T(8,128)} %prefix.2), calls=%async_computation.1 | async-start | bytes 1572864 | tf_op jit(solution)/shard_map/all_to_all | solution.py:1081
  82.8 3.5 %collective-permute-start.2 = (f32[2,256,128]{2,1,0:T(8,128)S(1)}, f32[2,256,128]{2,1,0:T(8,128)S(1)}, u32[]{:S(2)}, u32[]{:S(2)}) collective-permute-start(f32[2,256,128]{2,1,0:T(8,128)S(1)} %get-tuple-element.95.sums), channel_id=1, source_target_pairs={{0,1},{1,0},{2,3},{3,2},{4,5},{5,4},{6,7},{7,6},{8,9},{9,8},{10,11... | collective-permute-start | bytes 786440 | tf_op jit(solution)/shard_map/ppermute | solution.py:1116
  90.9 23.7 %all-to-all-start.2 = ((f32[16,96,128]{2,1,0:T(8,128)}), f32[16,96,128]{2,1,0:T(8,128)}, u32[]{:S(2)}, u32[]{:S(2)}) async-start(f32[16,96,128]{2,1,0:T(8,128)} %get-tuple-element.101), calls=%async_computation.2 | async-start | bytes 1572864 | tf_op jit(solution)/shard_map/all_to_all | solution.py:1081
  117.0 26.6 %all-to-all-start.3 = ((f32[16,96,128]{2,1,0:T(8,128)}), f32[16,96,128]{2,1,0:T(8,128)}, u32[]{:S(2)}, u32[]{:S(2)}) async-start(f32[16,96,128]{2,1,0:T(8,128)} %prefix.3), calls=%async_computation.3 | async-start | bytes 1572864 | tf_op jit(solution)/shard_map/all_to_all | solution.py:1081
  122.2 37.2 %collective-permute-start.4 = (f32[384,768]{1,0:T(8,128)}, f32[384,768]{1,0:T(8,128)}, u32[]{:S(2)}, u32[]{:S(2)}) collective-permute-start(f32[384,768]{1,0:T(8,128)} %constant_dynamic-slice_fusion.8), channel_id=1, source_target_pairs={{0,4},{2,6},{4,0},{6,2},{8,12},{10,14},{12,8},{14,10},{16,20},{18,... | collective-permute-start | bytes 3538952 | tf_op jit(solution)/shard_map/ppermute | solution.py:809
  123.5 35.9 %collective-permute-start.3 = (f32[384,768]{1,0:T(8,128)}, f32[384,768]{1,0:T(8,128)}, u32[]{:S(2)}, u32[]{:S(2)}) collective-permute-start(f32[384,768]{1,0:T(8,128)} %constant_dynamic-slice_fusion.9), channel_id=1, source_target_pairs={{0,2},{2,0},{4,6},{6,4},{8,10},{10,8},{12,14},{14,12},{16,18},{18,... | collective-permute-start | bytes 3538952 | tf_op jit(solution)/shard_map/ppermute | solution.py:809
  129.6 14.0 %copy-start.3 = (f32[2,256,24]{2,1,0:T(8,128)S(1)}, f32[2,256,24]{2,1,0:T(8,128)}, u32[]{:S(2)}) copy-start(f32[2,256,24]{2,1,0:T(8,128)} %get-tuple-element.110.tail) | copy-start | bytes 147460
  143.6 15.8 %copy-start.25 = (f32[768,768]{1,0:T(8,128)S(1)}, f32[768,768]{1,0:T(8,128)}, u32[]{:S(2)}) copy-start(f32[768,768]{1,0:T(8,128)} %copy-done.24) | copy-start | bytes 7077892
  161.1 15.7 %collective-permute-start.6 = (f32[192,768]{1,0:T(8,128)S(1)}, f32[192,768]{1,0:T(8,128)S(1)}, u32[]{:S(2)}, u32[]{:S(2)}) collective-permute-start(f32[192,768]{1,0:T(8,128)S(1)} %constant_dynamic-slice_fusion.6), channel_id=1, source_target_pairs={{0,2},{2,0},{4,6},{6,4},{8,10},{10,8},{12,14},{14,12},{16,18},{18,... | collective-permute-start | bytes 1769480 | tf_op jit(solution)/shard_map/ppermute | solution.py:809
  163.0 13.7 %copy-start.27 = (f32[384,768]{1,0:T(8,128)}, f32[384,768]{1,0:T(8,128)S(1)}, u32[]{:S(2)}) copy-start(f32[384,768]{1,0:T(8,128)S(1)} %dynamic-slice_add_fusion) | copy-start | bytes 3538948
  163.1 13.7 %collective-permute-start.5 = (f32[192,768]{1,0:T(8,128)S(1)}, f32[192,768]{1,0:T(8,128)S(1)}, u32[]{:S(2)}, u32[]{:S(2)}) collective-permute-start(f32[192,768]{1,0:T(8,128)S(1)} %constant_dynamic-slice_fusion.7), channel_id=1, source_target_pairs={{0,4},{2,6},{4,0},{6,2},{8,12},{10,14},{12,8},{14,10},{16,20},{18,... | collective-permute-start | bytes 1769480 | tf_op jit(solution)/shard_map/ppermute | solution.py:809
  166.9 10.7 %collective-permute-start.7 = (f32[544,256]{1,0:T(8,128)S(1)}, f32[544,256]{1,0:T(8,128)S(1)}, u32[]{:S(2)}, u32[]{:S(2)}) collective-permute-start(f32[544,256]{1,0:T(8,128)S(1)} %bitcast.69), channel_id=1, source_target_pairs={{0,1},{1,0},{2,3},{3,2},{4,5},{5,4},{6,7},{7,6},{8,9},{9,8},{10,11... | collective-permute-start | bytes 1671176 | tf_op jit(solution)/shard_map/ppermute | solution.py:1238
  175.9 34.2 %collective-permute-start.12 = (f32[256,768]{1,0:T(8,128)}, f32[256,768]{1,0:T(8,128)}, u32[]{:S(2)}, u32[]{:S(2)}) collective-permute-start(f32[256,768]{1,0:T(8,128)} %constant_dynamic-slice_fusion.5), channel_id=1, source_target_pairs={{0,2},{2,0},{4,6},{6,4},{8,10},{10,8},{12,14},{14,12},{16,18},{18,... | collective-permute-start | bytes 2359304 | tf_op jit(solution)/shard_map/ppermute | solution.py:809
  177.0 12.9 %collective-permute-start.14 = (f32[192,768]{1,0:T(8,128)S(1)}, f32[192,768]{1,0:T(8,128)S(1)}, u32[]{:S(2)}, u32[]{:S(2)}) collective-permute-start(f32[192,768]{1,0:T(8,128)S(1)} %broadcast_select_fusion.2), channel_id=1, source_target_pairs={{0,8},{2,10},{4,12},{6,14},{8,0},{10,2},{12,4},{14,6},{16,24},{18,... | collective-permute-start | bytes 1769480 | tf_op jit(solution)/shard_map/ppermute | solution.py:809
  181.1 8.7 %copy-start.28 = (f32[384,768]{1,0:T(8,128)S(1)}, f32[384,768]{1,0:T(8,128)}, u32[]{:S(2)}) copy-start(f32[384,768]{1,0:T(8,128)} %copy-done.27) | copy-start | bytes 3538948
  181.1 8.7 %copy-start.47 = (f32[192,768]{1,0:T(8,128)S(1)}, f32[192,768]{1,0:T(8,128)}, u32[]{:S(2)}) copy-start(f32[192,768]{1,0:T(8,128)} %copy-done.46) | copy-start | bytes 1769476
  185.7 24.4 %collective-permute-start.13 = (f32[256,768]{1,0:T(8,128)}, f32[256,768]{1,0:T(8,128)}, u32[]{:S(2)}, u32[]{:S(2)}) collective-permute-start(f32[256,768]{1,0:T(8,128)} %constant_dynamic-slice_fusion.4), channel_id=1, source_target_pairs={{0,4},{2,6},{4,0},{6,2},{8,12},{10,14},{12,8},{14,10},{16,20},{18,... | collective-permute-start | bytes 2359304 | tf_op jit(solution)/shard_map/ppermute | solution.py:809
  189.8 20.3 %copy-start.33 = (f32[512,768]{1,0:T(8,128)S(1)}, f32[512,768]{1,0:T(8,128)}, u32[]{:S(2)}) copy-start(f32[512,768]{1,0:T(8,128)} %pack.1) | copy-start | bytes 4718596
  190.9 15.0 %collective-permute-start.15 = (f32[96,768]{1,0:T(8,128)S(1)}, f32[96,768]{1,0:T(8,128)S(1)}, u32[]{:S(2)}, u32[]{:S(2)}) collective-permute-start(f32[96,768]{1,0:T(8,128)S(1)} %constant_dynamic-slice_fusion.3), channel_id=1, source_target_pairs={{0,16},{2,18},{4,20},{6,22},{8,24},{10,26},{12,28},{14,30},{16,0},... | collective-permute-start | bytes 884744 | tf_op jit(solution)/shard_map/ppermute | solution.py:809
  206.9 13.3 %collective-permute-start.18 = (f32[96,768]{1,0:T(8,128)S(1)}, f32[96,768]{1,0:T(8,128)S(1)}, u32[]{:S(2)}, u32[]{:S(2)}) collective-permute-start(f32[96,768]{1,0:T(8,128)S(1)} %dynamic-slice_add_fusion.8), channel_id=1, source_target_pairs={{0,16},{2,18},{4,20},{6,22},{8,24},{10,26},{12,28},{14,30},{16,0},... | collective-permute-start | bytes 884744 | tf_op jit(solution)/shard_map/ppermute | solution.py:809
  211.4 13.9 %collective-permute-start.17 = (f32[128,768]{1,0:T(8,128)S(1)}, f32[128,768]{1,0:T(8,128)S(1)}, u32[]{:S(2)}, u32[]{:S(2)}) collective-permute-start(f32[128,768]{1,0:T(8,128)S(1)} %constant_dynamic-slice_fusion.1), channel_id=1, source_target_pairs={{0,2},{2,0},{4,6},{6,4},{8,10},{10,8},{12,14},{14,12},{16,18},{18,... | collective-permute-start | bytes 1179656 | tf_op jit(solution)/shard_map/ppermute | solution.py:809
  212.9 12.4 %copy-start.38 = (f32[256,768]{1,0:T(8,128)}, f32[256,768]{1,0:T(8,128)S(1)}, u32[]{:S(2)}) copy-start(f32[256,768]{1,0:T(8,128)S(1)} %dynamic-slice_add_fusion.3) | copy-start | bytes 2359300
  212.9 10.1 %copy-start.29 = (f32[544,768]{1,0:T(8,128)S(1)}, f32[544,768]{1,0:T(8,128)}, u32[]{:S(2)}) copy-start(f32[544,768]{1,0:T(8,128)} %get-tuple-element.130) | copy-start | bytes 5013508
  213.7 12.3 %collective-permute-start.16 = (f32[128,768]{1,0:T(8,128)}, f32[128,768]{1,0:T(8,128)}, u32[]{:S(2)}, u32[]{:S(2)}) collective-permute-start(f32[128,768]{1,0:T(8,128)} %constant_dynamic-slice_fusion.2), channel_id=1, source_target_pairs={{0,4},{2,6},{4,0},{6,2},{8,12},{10,14},{12,8},{14,10},{16,20},{18,... | collective-permute-start | bytes 1179656 | tf_op jit(solution)/shard_map/ppermute | solution.py:809
  221.1 13.8 %collective-permute-start.20 = (f32[192,768]{1,0:T(8,128)}, f32[192,768]{1,0:T(8,128)}, u32[]{:S(2)}, u32[]{:S(2)}) collective-permute-start(f32[192,768]{1,0:T(8,128)} %maximum_select_fusion.7), channel_id=1, source_target_pairs={{0,8},{2,10},{4,12},{6,14},{8,0},{10,2},{12,4},{14,6},{16,24},{18,... | collective-permute-start | bytes 1769480 | tf_op jit(solution)/shard_map/ppermute | solution.py:809
  223.0 53.3 %collective-permute-start.9 = (f32[2,272,768]{2,1,0:T(8,128)S(1)}, f32[2,272,768]{2,1,0:T(8,128)}, u32[]{:S(2)}, u32[]{:S(2)}) collective-permute-start(f32[2,272,768]{2,1,0:T(8,128)S(1)} %bitcast.63), channel_id=1, source_target_pairs={{0,1},{1,0},{2,3},{3,2},{4,5},{5,4},{6,7},{7,6},{8,9},{9,8},{10,11... | collective-permute-start | bytes 5013512 | tf_op jit(solution)/shard_map/ppermute | solution.py:1279
  226.0 13.3 %copy-start.35 = (f32[2,256,768]{2,1,0:T(8,128)S(1)}, f32[2,256,768]{2,1,0:T(8,128)}, u32[]{:S(2)}) copy-start(f32[2,256,768]{2,1,0:T(8,128)} %get-tuple-element.98) | copy-start | bytes 4718596
  227.6 11.7 %copy-start.26 = (f32[768,768]{1,0:T(8,128)S(1)}, f32[768,768]{1,0:T(8,128)}, u32[]{:S(2)}) copy-start(f32[768,768]{1,0:T(8,128)} %param.32) | copy-start | bytes 7077892
  227.6 21.0 %collective-permute-start.19 = (f32[128,768]{1,0:T(8,128)S(1)}, f32[128,768]{1,0:T(8,128)S(1)}, u32[]{:S(2)}, u32[]{:S(2)}) collective-permute-start(f32[128,768]{1,0:T(8,128)S(1)} %broadcast_select_fusion.5), channel_id=1, source_target_pairs={{0,8},{2,10},{4,12},{6,14},{8,0},{10,2},{12,4},{14,6},{16,24},{18,... | collective-permute-start | bytes 1179656 | tf_op jit(solution)/shard_map/ppermute | solution.py:809
  237.2 14.0 %collective-permute-start.22 = (f32[192,768]{1,0:T(8,128)}, f32[192,768]{1,0:T(8,128)}, u32[]{:S(2)}, u32[]{:S(2)}) collective-permute-start(f32[192,768]{1,0:T(8,128)} %get-tuple-element.203), channel_id=1, source_target_pairs={{0,4},{2,6},{4,0},{6,2},{8,12},{10,14},{12,8},{14,10},{16,20},{18,... | collective-permute-start | bytes 1769480 | tf_op jit(solution)/shard_map/ppermute | solution.py:809
  239.1 9.5 %copy-start.37 = (f32[256,768]{1,0:T(8,128)S(1)}, f32[256,768]{1,0:T(8,128)}, u32[]{:S(2)}) copy-start(f32[256,768]{1,0:T(8,128)} %copy-done.36) | copy-start | bytes 2359300
  239.1 9.5 %copy-start.39 = (f32[256,768]{1,0:T(8,128)S(1)}, f32[256,768]{1,0:T(8,128)}, u32[]{:S(2)}) copy-start(f32[256,768]{1,0:T(8,128)} %copy-done.38) | copy-start | bytes 2359300
  239.1 9.5 %copy-start.49 = (f32[128,768]{1,0:T(8,128)S(1)}, f32[128,768]{1,0:T(8,128)}, u32[]{:S(2)}) copy-start(f32[128,768]{1,0:T(8,128)} %copy-done.48) | copy-start | bytes 1179652
  239.1 12.1 %collective-permute-start.23 = (f32[192,768]{1,0:T(8,128)}, f32[192,768]{1,0:T(8,128)}, u32[]{:S(2)}, u32[]{:S(2)}) collective-permute-start(f32[192,768]{1,0:T(8,128)} %get-tuple-element.202), channel_id=1, source_target_pairs={{0,2},{2,0},{4,6},{6,4},{8,10},{10,8},{12,14},{14,12},{16,18},{18,... | collective-permute-start | bytes 1769480 | tf_op jit(solution)/shard_map/ppermute | solution.py:809
  242.9 31.3 %collective-permute-start.8 = (f32[512,768]{1,0:T(8,128)}, f32[512,768]{1,0:T(8,128)}, u32[]{:S(2)}, u32[]{:S(2)}) collective-permute-start(f32[512,768]{1,0:T(8,128)} %fusion.20), channel_id=1, source_target_pairs={{0,1},{1,0},{2,3},{3,2},{4,5},{5,4},{6,7},{7,6},{8,9},{9,8},{10,11... | collective-permute-start | bytes 4718600 | tf_op jit(solution)/shard_map/ppermute | solution.py:1295
  249.8 10.2 %collective-permute-start.21 = (f32[64,768]{1,0:T(8,128)S(1)}, f32[64,768]{1,0:T(8,128)S(1)}, u32[]{:S(2)}, u32[]{:S(2)}) collective-permute-start(f32[64,768]{1,0:T(8,128)S(1)} %constant_dynamic-slice_fusion), channel_id=1, source_target_pairs={{0,16},{2,18},{4,20},{6,22},{8,24},{10,26},{12,28},{14,30},{16,0},... | collective-permute-start | bytes 589832 | tf_op jit(solution)/shard_map/ppermute | solution.py:809
  260.0 11.7 %collective-permute-start.24 = (f32[64,768]{1,0:T(8,128)S(1)}, f32[64,768]{1,0:T(8,128)S(1)}, u32[]{:S(2)}, u32[]{:S(2)}) collective-permute-start(f32[64,768]{1,0:T(8,128)S(1)} %dynamic-slice_add_fusion.11), channel_id=1, source_target_pairs={{0,16},{2,18},{4,20},{6,22},{8,24},{10,26},{12,28},{14,30},{16,0},... | collective-permute-start | bytes 589832 | tf_op jit(solution)/shard_map/ppermute | solution.py:809
  265.1 11.2 %copy-start.40 = (f32[384,768]{1,0:T(8,128)}, f32[384,768]{1,0:T(8,128)S(1)}, u32[]{:S(2)}) copy-start(f32[384,768]{1,0:T(8,128)S(1)} %maximum_select_fusion.3) | copy-start | bytes 3538948
  265.1 27.2 %collective-permute-start.29 = (f32[384,768]{1,0:T(8,128)S(1)}, f32[384,768]{1,0:T(8,128)S(1)}, u32[]{:S(2)}, u32[]{:S(2)}) collective-permute-start(f32[384,768]{1,0:T(8,128)S(1)} %maximum_select_fusion.3), channel_id=1, source_target_pairs={{0,4},{2,6},{4,0},{6,2},{8,12},{10,14},{12,8},{14,10},{16,20},{18,... | collective-permute-start | bytes 3538952 | tf_op jit(solution)/shard_map/ppermute | solution.py:809
  265.2 29.9 %collective-permute-start.28 = (f32[384,768]{1,0:T(8,128)S(1)}, f32[384,768]{1,0:T(8,128)S(1)}, u32[]{:S(2)}, u32[]{:S(2)}) collective-permute-start(f32[384,768]{1,0:T(8,128)S(1)} %maximum_select_fusion.2), channel_id=1, source_target_pairs={{0,2},{2,0},{4,6},{6,4},{8,10},{10,8},{12,14},{14,12},{16,18},{18,... | collective-permute-start | bytes 3538952 | tf_op jit(solution)/shard_map/ppermute | solution.py:809
  271.7 11.4 %collective-permute-start.25 = (f32[128,768]{1,0:T(8,128)S(1)}, f32[128,768]{1,0:T(8,128)S(1)}, u32[]{:S(2)}, u32[]{:S(2)}) collective-permute-start(f32[128,768]{1,0:T(8,128)S(1)} %maximum_select_fusion.8), channel_id=1, source_target_pairs={{0,8},{2,10},{4,12},{6,14},{8,0},{10,2},{12,4},{14,6},{16,24},{18,... | collective-permute-start | bytes 1179656 | tf_op jit(solution)/shard_map/ppermute | solution.py:809
  283.2 18.1 %collective-permute-start.26 = (f32[128,768]{1,0:T(8,128)S(1)}, f32[128,768]{1,0:T(8,128)S(1)}, u32[]{:S(2)}, u32[]{:S(2)}) collective-permute-start(f32[128,768]{1,0:T(8,128)S(1)} %get-tuple-element.205), channel_id=1, source_target_pairs={{0,4},{2,6},{4,0},{6,2},{8,12},{10,14},{12,8},{14,10},{16,20},{18,... | collective-permute-start | bytes 1179656 | tf_op jit(solution)/shard_map/ppermute | solution.py:809
  283.3 18.0 %collective-permute-start.27 = (f32[128,768]{1,0:T(8,128)S(1)}, f32[128,768]{1,0:T(8,128)S(1)}, u32[]{:S(2)}, u32[]{:S(2)}) collective-permute-start(f32[128,768]{1,0:T(8,128)S(1)} %get-tuple-element.204), channel_id=1, source_target_pairs={{0,2},{2,0},{4,6},{6,4},{8,10},{10,8},{12,14},{14,12},{16,18},{18,... | collective-permute-start | bytes 1179656 | tf_op jit(solution)/shard_map/ppermute | solution.py:809
  284.7 18.4 %collective-permute-start.10 = (f32[2,8,768]{2,1,0:T(8,128)S(1)}, f32[2,8,768]{2,1,0:T(8,128)S(1)}, u32[]{:S(2)}, u32[]{:S(2)}) collective-permute-start(f32[2,8,768]{2,1,0:T(8,128)S(1)} %get-tuple-element.196), channel_id=1, source_target_pairs={{0,2},{2,4},{4,6},{6,8},{8,10},{10,12},{12,14},{14,16},{16,18},{18... | collective-permute-start | bytes 147464 | tf_op jit(solution)/shard_map/ppermute | solution.py:1281
  292.4 10.7 %collective-permute-start.11 = (f32[2,8,768]{2,1,0:T(8,128)S(1)}, f32[2,8,768]{2,1,0:T(8,128)S(1)}, u32[]{:S(2)}, u32[]{:S(2)}) collective-permute-start(f32[2,8,768]{2,1,0:T(8,128)S(1)} %get-tuple-element.197), channel_id=1, source_target_pairs={{2,0},{4,2},{6,4},{8,6},{10,8},{12,10},{14,12},{16,14},{18,16},{20... | collective-permute-start | bytes 147464 | tf_op jit(solution)/shard_map/ppermute | solution.py:1280
  301.4 17.1 %collective-permute-start.31 = (f32[256,768]{1,0:T(8,128)S(1)}, f32[256,768]{1,0:T(8,128)S(1)}, u32[]{:S(2)}, u32[]{:S(2)}) collective-permute-start(f32[256,768]{1,0:T(8,128)S(1)} %maximum_select_fusion.5.own_second), channel_id=1, source_target_pairs={{0,4},{2,6},{4,0},{6,2},{8,12},{10,14},{12,8},{14,10},{16,20},{18,... | collective-permute-start | bytes 2359304 | tf_op jit(solution)/shard_map/ppermute | solution.py:809
  302.7 16.2 %collective-permute-start.30 = (f32[256,768]{1,0:T(8,128)S(1)}, f32[256,768]{1,0:T(8,128)S(1)}, u32[]{:S(2)}, u32[]{:S(2)}) collective-permute-start(f32[256,768]{1,0:T(8,128)S(1)} %maximum_select_fusion.4.own_first), channel_id=1, source_target_pairs={{0,2},{2,0},{4,6},{6,4},{8,10},{10,8},{12,14},{14,12},{16,18},{18,... | collective-permute-start | bytes 2359304 | tf_op jit(solution)/shard_map/ppermute | solution.py:809
  319.8 8.0 %copy-start.41 = (f32[384,768]{1,0:T(8,128)S(1)}, f32[384,768]{1,0:T(8,128)}, u32[]{:S(2)}) copy-start(f32[384,768]{1,0:T(8,128)} %copy-done.40) | copy-start | bytes 3538948
  319.8 8.0 %copy-start.52 = (f32[384,768]{1,0:T(8,128)S(1)}, f32[384,768]{1,0:T(8,128)}, u32[]{:S(2)}) copy-start(f32[384,768]{1,0:T(8,128)} %copy-done.51) | copy-start | bytes 3538948
  324.0 6.2 %collective-permute-start.32 = (f32[256,768]{1,0:T(8,128)S(1)}, f32[256,768]{1,0:T(8,128)}, u32[]{:S(2)}, u32[]{:S(2)}) collective-permute-start(f32[256,768]{1,0:T(8,128)S(1)} %get-tuple-element.150.mine), channel_id=1, source_target_pairs={{0,1},{1,0},{2,3},{3,2},{4,5},{5,4},{6,7},{7,6},{8,9},{9,8},{10,11... | collective-permute-start | bytes 2359304 | tf_op jit(solution)/shard_map/ppermute | solution.py:1326
  (34 other events, 109.4 us)
